TPU v7x, 256 devices: a whole 4x4x8 slice. The times are simulated.
256 devices in a mesh: ctx: 64 (over x, z, core), tp: 4 (over y).
Axes of the slice: x: 4, y: 4, z: 8, core: 2. Of those that a mesh axis runs over, the one named last changes fastest.
Arguments:
- block_query: bfloat16 [4096, 8192], P('ctx', 'tp'), may hold values from -10 to 10
- block_key: bfloat16 [4096, 1024], P('ctx', 'tp'), may hold values from -10 to 10
- block_value: bfloat16 [4096, 1024], P('ctx', 'tp'), may hold values from -6 to 6
- question_query: bfloat16 [256, 8192], P('ctx', 'tp'), may hold values from -10 to 10
- question_key: bfloat16 [256, 1024], P('ctx', 'tp'), may hold values from -10 to 10
- question_value: bfloat16 [256, 1024], P('ctx', 'tp'), may hold values from -6 to 6
- block_fill: int32 [64], replicated, may hold values from 1 to 64, 2560 in all
Outputs:
- block_output: bfloat16 [4096, 8192], P('ctx', 'tp')
- question_output: bfloat16 [256, 8192], P(('ctx', 'tp'))
Inputs may be any that keep to these rules, and one draw needn't show every extreme that they name: Block d's first block_fill[d] tokens are real, the rest padding.
All inputs are finite; a program needn't handle non-finite values.
Results may differ from a plain program's by a relative error of at most 0.0065.
Values may be sent and summed in bfloat16 or wider, within the bound.
No kernel may reach another device: no remote copies, remote signals or barrier semaphores. Data moves between devices by JAX's collectives and lax.ppermute only.
A program may use at most 256 MiB of HBM per device.

v0:
```python
import jax
import jax.numpy as jnp
from jax import lax
from jax.sharding import PartitionSpec as P

NH = 64
KV_HEADS = 8
HEAD = 128


def spread(array, axis, root):
    mine = lax.axis_index(axis) == root
    return lax.psum(jnp.where(mine, array, jnp.zeros_like(array)), axis)


def masked_parts(scores, allowed):
    masked = jnp.where(allowed, scores, -jnp.inf)
    peak = jnp.max(masked, axis=-1, keepdims=True)
    weights = jnp.exp(masked - peak).astype(jnp.bfloat16)
    totals = jnp.sum(weights.astype(jnp.float32), axis=-1, keepdims=True)
    return (peak, weights, totals)


def transpose_dot(left, right):
    return lax.dot_general(
        left, right, (((1,), (1,)), ((), ())), preferred_element_type=jnp.float32
    )


def per_device(
    block_query, block_key, block_value, question_query, question_key, question_value, block_fill
):
    groups = NH // KV_HEADS
    factor = HEAD ** (-0.5)
    device = lax.axis_index("ctx")
    block_rows = block_query.shape[0]
    own_questions = question_query.shape[0]
    local_heads = block_query.shape[1] // HEAD
    own_fill = lax.dynamic_index_in_dim(block_fill, device, 0, keepdims=False)
    anchor_key, anchor_value = (spread(block_key, "ctx", 0), spread(block_value, "ctx", 0))
    key_rows = jnp.concatenate([anchor_key, block_key], 0)
    value_rows = jnp.concatenate([anchor_value, block_value], 0)
    row_ids = jnp.arange(block_rows, dtype=jnp.int32)[:, None]
    col_ids = jnp.arange(2 * block_rows, dtype=jnp.int32)[None, :]
    own_cols = col_ids - block_rows
    allowed = jnp.where(
        col_ids < block_rows,
        (col_ids < block_fill[0]) & (device > 0),
        (own_cols <= row_ids) & (own_cols < own_fill),
    )
    keep_rows = row_ids < own_fill

    def first_head(head_index, output):
        query_cols = lax.dynamic_slice_in_dim(block_query, head_index * HEAD, HEAD, 1)
        shared = head_index // groups
        head_keys = lax.dynamic_slice_in_dim(key_rows, shared * HEAD, HEAD, 1)
        head_values = lax.dynamic_slice_in_dim(value_rows, shared * HEAD, HEAD, 1)
        scores = transpose_dot(query_cols, head_keys) * factor
        peak, weights, totals = masked_parts(scores, allowed)
        mixed = jnp.dot(weights, head_values, preferred_element_type=jnp.float32) / totals
        mixed = jnp.where(keep_rows, mixed, 0.0).astype(jnp.bfloat16)
        return lax.dynamic_update_slice_in_dim(output, mixed, head_index * HEAD, 1)

    block_output = lax.fori_loop(
        0, local_heads, first_head, jnp.zeros(block_query.shape, jnp.bfloat16)
    )
    whole_query = lax.all_gather(question_query, "ctx", axis=0, tiled=True)
    total_rows = whole_query.shape[0]
    second_keys = jnp.concatenate([block_key, question_key], 0)
    second_values = jnp.concatenate([block_value, question_value], 0)
    query_ids = jnp.arange(total_rows, dtype=jnp.int32)[:, None]
    key_cols = jnp.arange(block_rows + own_questions, dtype=jnp.int32)[None, :]
    allowed_two = jnp.where(
        key_cols < block_rows,
        key_cols < own_fill,
        device * own_questions + key_cols - block_rows <= query_ids,
    )

    def second_head(head_index, carry):
        maxima, totals_all, sums_all = carry
        query_cols = lax.dynamic_slice_in_dim(whole_query, head_index * HEAD, HEAD, 1)
        shared = head_index // groups
        head_keys = lax.dynamic_slice_in_dim(second_keys, shared * HEAD, HEAD, 1)
        head_values = lax.dynamic_slice_in_dim(second_values, shared * HEAD, HEAD, 1)
        scores = transpose_dot(query_cols, head_keys) * factor
        peak, weights, totals = masked_parts(scores, allowed_two)
        sums = jnp.dot(weights, head_values, preferred_element_type=jnp.float32)
        maxima = lax.dynamic_update_slice_in_dim(maxima, peak, head_index, 1)
        totals_all = lax.dynamic_update_slice_in_dim(totals_all, totals, head_index, 1)
        sums_all = lax.dynamic_update_slice_in_dim(sums_all, sums, head_index * HEAD, 1)
        return (maxima, totals_all, sums_all)

    start = (
        jnp.zeros((total_rows, local_heads), jnp.float32),
        jnp.zeros((total_rows, local_heads), jnp.float32),
        jnp.zeros((total_rows, local_heads * HEAD), jnp.float32),
    )
    maxima, totals_all, sums_all = lax.fori_loop(0, local_heads, second_head, start)
    overall = lax.pmax(maxima, "ctx")
    scales = jnp.exp(maxima - overall)
    scaled_sums = (sums_all.reshape(total_rows, local_heads, HEAD) * scales[:, :, None]).reshape(
        total_rows, local_heads * HEAD
    )
    kept_sums, kept_totals = (
        lax.psum_scatter(scaled_sums, "ctx", scatter_dimension=0, tiled=True),
        lax.psum_scatter(totals_all * scales, "ctx", scatter_dimension=0, tiled=True),
    )
    finished = (
        (kept_sums.reshape(own_questions, local_heads, HEAD) / kept_totals[:, :, None])
        .reshape(own_questions, local_heads * HEAD)
        .astype(jnp.bfloat16)
    )
    question_output = lax.all_to_all(finished, "tp", split_axis=0, concat_axis=1, tiled=True)
    return (block_output, question_output)


def solution(mesh):
    placed = (
        P("ctx", "tp"),
        P("ctx", "tp"),
        P("ctx", "tp"),
        P("ctx", "tp"),
        P("ctx", "tp"),
        P("ctx", "tp"),
        P(),
    )
    return jax.shard_map(
        per_device,
        mesh=mesh,
        in_specs=placed,
        out_specs=(P("ctx", "tp"), P(("ctx", "tp"), None)),
        check_vma=False,
    )
```

profile of v0, /device:TPU:32, one launch (start us, length us, event | category | flops | bytes accessed | tf_op | source)
XLA Modules:
  0.0 647.5 jit_solution(5226427981968437722)
XLA Ops:
  7.2 0.7 all-gather.3.cloned.1.call-update
  8.0 0.6 broadcast_select_fusion
  8.7 1.4 fusion.29
  10.1 0.7 iota_compare_fusion.2
  10.8 0.8 pad_maximum_fusion.2
  11.6 77.2 %all-gather.3.cloned.1.call-done = bf16[64,4,2048]{2,1,0:T(4,128)(2,1)} async-done(((bf16[1,4,2048]{2,1,0:T(4,128)(2,1)}), bf16[64,4,2048]{2,1,0:T(4,128)(2,1)}) %all-gather.3.cloned.1.call-update) | async-done | bytes 1048592 | tf_op jit(solution)/shard_map/all_gather | solution.py:67
  88.8 1.3 reshape.67
  90.2 0.2 broadcast_in_dim.132
  90.4 9.8 %while.37 = (s32[]{:T(128)}, f32[256,16]{0,1:T(8,128)S(1)}, f32[256,16]{0,1:T(8,128)S(1)}, f32[256,2048]{1,0:T(8,128)S(1)}, bf16[256,2048]{1,0:T(8,128)(2,1)S(1)...) while((s32[]{:T(128)}, f32[256,16]{0,1:T(8,128)S(1)}, ...), condition=%wide.region_9.10_spmd.clone, body=%wide.region_6.9_spmd.clone.sunk | while | flops 9103890 | bytes 456551 | solution.py:98
  91.7 0.2 fusion.39
  92.9 0.2 fusion.39
  94.7 0.2 fusion.39
  97.2 0.2 fusion.39
  97.8 0.2 fusion.39
  98.4 0.2 fusion.39
  100.2 244.4 %pmax.7 = f32[256,16]{0,1:T(8,128)S(1)} all-reduce(f32[256,16]{0,1:T(8,128)S(1)} %get-tuple-element.382), channel_id=1, replica_groups=mesh['ctx'=64,'tp'=4] {'ctx'}, use_global_device_ids=true, to_apply=%region_10.11 | all-reduce | flops 4096 | bytes 32768 | tf_op jit(solution)/shard_map/pmax | solution.py:99
  344.7 0.6 mul.82
  345.3 2.4 bitcast_multiply_fusion
  347.8 0.6 copy-done.3
  348.4 0.6 dynamic-slice
  349.6 0.7 broadcast_compare_fusion
  350.3 0.6 compare_and_fusion
  351.0 0.8 pad_maximum_fusion
  351.8 0.8 pad_maximum_fusion.1
  352.5 246.4 %all-reduce.1 = f32[256,16]{0,1:T(8,128)S(1)} all-reduce(f32[256,16]{0,1:T(8,128)S(1)} %get-tuple-element.479), channel_id=3, replica_groups=mesh['ctx'=64,'tp'=4] {'ctx'}, use_global_device_ids=true, to_apply=%region_12.13.clone | all-reduce | flops 4096 | bytes 32768
  599.1 0.9 fusion.25
  600.0 0.5 broadcast.121
  600.5 0.7 reduce
  601.2 0.6 reshape.72
  601.8 4.3 all-to-all-start
  606.1 34.1 %while.36 = (s32[]{:T(128)}, bf16[64,2048]{1,0:T(8,128)(2,1)S(1)}, bf16[64,2048]{1,0:T(8,128)(2,1)}, bf16[128,256]{1,0:T(8,128)(2,1)S(1)}, bf16[128,256]{1,0:T(8...) while((s32[]{:T(128)}, bf16[64,2048]{1,0:T(8,128)(2,1)S(1)}, ...), condition=%wide.region_5.6_spmd.clone, body=%wide.region_2.5_spmd.clone.sunk | while | flops 4317138 | bytes 201379 | solution.py:64
  606.2 1.0 fusion.36
  607.3 0.7 compare_bitcast_fusion.2
  608.3 1.0 fusion.36
  609.5 0.7 compare_bitcast_fusion.2
  610.4 1.0 fusion.36
  611.6 0.7 compare_bitcast_fusion.2
  612.5 1.0 fusion.36
  613.7 0.7 compare_bitcast_fusion.2
  614.7 1.0 fusion.36
  615.9 0.7 compare_bitcast_fusion.2
  616.8 1.0 fusion.36
  618.0 0.7 compare_bitcast_fusion.2
  618.9 1.0 fusion.36
  620.1 0.7 compare_bitcast_fusion.2
  621.1 1.0 fusion.36
  622.2 0.7 compare_bitcast_fusion.2
  623.2 1.0 fusion.36
  624.4 0.7 compare_bitcast_fusion.2
  625.3 1.0 fusion.36
  626.5 0.7 compare_bitcast_fusion.2
  627.5 1.0 fusion.36
  628.6 0.7 compare_bitcast_fusion.2
  629.6 1.0 fusion.36
  630.8 0.7 compare_bitcast_fusion.2
  631.7 1.0 fusion.36
  632.9 0.7 compare_bitcast_fusion.2
  633.9 1.0 fusion.36
  635.1 0.7 compare_bitcast_fusion.2
  636.0 1.0 fusion.36
  637.2 0.7 compare_bitcast_fusion.2
  638.2 1.0 fusion.36
  639.3 0.7 compare_bitcast_fusion.2
  640.3 0.7 reshape.73
  (131 shorter events, 14.6 us)
Async XLA Ops:
  7.2 81.7 %all-gather.3.cloned.1.call-start = ((), (), s32[]{:S(2)}) async-start(), calls=%async_computation.1 | async-start | bytes 1064960 | tf_op jit(solution)/shard_map/all_gather | solution.py:67
  7.9 343.1 %all-reduce.8.cloned.1.call-start = ((), (), s32[]{:S(2)}) async-start(), calls=%async_computation.3 | async-start | bytes 131072 | tf_op jit(solution)/shard_map/psum | solution.py:13
  8.6 590.5 %all-reduce.6.cloned.1.call-start = ((), (), s32[]{:S(2)}) async-start(), calls=%async_computation.2 | async-start | bytes 4194304
  347.7 0.7 copy-start.3
  347.7 3.3 copy-start
  347.7 4.0 copy-start.1
  601.8 38.5 %all-to-all-start = ((bf16[4,2,1024]{2,1,0:T(2,128)(2,1)}), bf16[4,2,1024]{2,1,0:T(2,128)(2,1)S(1)}, u32[]{:S(2)}, u32[]{:S(2)}) async-start(bf16[4,2,1024]{2,1,0:T(2,128)(2,1)} %reshape.72), calls=%async_computation | async-start | bytes 32768 | tf_op jit(solution)/shard_map/all_to_all | solution.py:113
  640.3 0.7 copy-start.2
Sparse Core Ops, SparseCore 0:
  10.8 78.0 all-gather.2
  93.0 165.2 all-reduce.7
  347.9 186.0 all-reduce.5
where the time goes:
time: 655 us; the launch traced here: 647 us
  blocking collectives  491 us (75%)
  waiting for transfers between devices  78 us (12%)
  matrix products  25.9 us (4%)
  other arithmetic  23.7 us (4%)
  between operations  14.5 us (2%)
  local copies, waits for them, and re-layouts  8.36 us (1%)
    unnamed x1, blocking collectives  246 us
    pmax x1, blocking collectives, per_device(): overall = lax.pmax(maxima, 'ctx')  244 us
    all_gather x1, waiting for transfers between devices, per_device(): whole_query = lax.all_gather(question_query, 'ctx', axis=0, tiled=True)  77.2 us
    dot_general x32, matrix products, transpose_dot(): lax.dot_general(left, right, (((1,), (1,)), ((), ())), preferred_element_...  19.2 us
  transfers between devices with their start and end apart: 4, of which 1 were waited for; matrix products, arithmetic and copies ran while one was open for 8% of the time, Pallas kernels for 0%

commit v1 on v0

v1 whole, which is shorter than its diff:
```python
import functools

import jax
import jax.numpy as jnp
from jax import lax
from jax.experimental import pallas as pl
from jax.experimental.pallas import tpu as pltpu
from jax.sharding import Mesh, PartitionSpec as P

NH = 64
KV_HEADS = 8
HEAD = 128
GROUPS = NH // KV_HEADS
BLOCK = 64
QTOK = 4
NX, NZ, NC, NT = 4, 8, 2, 4
HEADS = NH // NT
KVS = KV_HEADS // NT
UNIT = 144
SCALE = HEAD**-0.5
NEG = float("-inf")
Z_OFFSETS = (0, -1, -2, -3, -4, 1, 2, 3)
X_SHIFTS = (0, 1, 3, 2)

VMEM = pl.BlockSpec(memory_space=pltpu.VMEM)
SMEM = pl.BlockSpec(memory_space=pltpu.SMEM)
PARAMS = pltpu.CompilerParams(vmem_limit_bytes=32 * 1024 * 1024)


def transpose_dot(left, right):
    return lax.dot_general(
        left, right, (((1,), (1,)), ((), ())), preferred_element_type=jnp.float32
    )


def prepare_kernel(query_ref, key_ref, value_ref, ask_key_ref, ask_value_ref, unit_ref, rows_ref):
    unit_ref[0:BLOCK, :] = key_ref[...]
    unit_ref[BLOCK : 2 * BLOCK, :] = value_ref[...]
    gap = jnp.zeros((8 - QTOK, KVS * HEAD), jnp.float32)
    tail = jnp.concatenate(
        [ask_key_ref[...].astype(jnp.float32), gap, ask_value_ref[...].astype(jnp.float32), gap], 0
    )
    unit_ref[2 * BLOCK : UNIT, :] = tail.astype(jnp.bfloat16)
    query = query_ref[...].astype(jnp.float32)
    for row in range(QTOK):
        heads = [query[row : row + 1, h * HEAD : (h + 1) * HEAD] for h in range(HEADS)]
        rows_ref[row] = jnp.concatenate(heads, 0).astype(jnp.bfloat16)


def question_kernel(
    place_ref, fill_ref, q0_ref, q1_ref, q2_ref, q3_ref, near_ref, far_ref, out_ref
):
    x, z, core = place_ref[0], place_ref[1], place_ref[2]
    units = [
        x * (NZ * NC) + lax.rem(z + offset + NZ, NZ) * NC + c
        for c in (core, 1 - core)
        for offset in Z_OFFSETS
    ]
    owners = [lax.rem(x - shift + NX, NX) for shift in X_SHIFTS]
    count = len(units)

    lane = lax.broadcasted_iota(jnp.int32, (1, count * BLOCK), 1)
    fills = jnp.zeros_like(lane)
    for n, unit in enumerate(units):
        fills = jnp.where(lane // BLOCK == n, fill_ref[unit], fills)
    bias = jnp.where(lane % BLOCK < fills, 0.0, NEG)

    lane = lax.broadcasted_iota(jnp.int32, (1, count * 8), 1)
    key_ids = jnp.zeros_like(lane)
    for n, unit in enumerate(units):
        key_ids = jnp.where(lane // 8 == n, unit * QTOK, key_ids)
    key_ids = jnp.where(lane % 8 < QTOK, key_ids + lane % 8, 1 << 20)
    rows = NX * QTOK * GROUPS
    row = lax.broadcasted_iota(jnp.int32, (rows, 1), 0)
    row_ids = (row // GROUPS) % QTOK
    for n, owner in enumerate(owners):
        first = (owner * (NZ * NC) + z * NC + core) * QTOK
        row_ids = jnp.where(row // (QTOK * GROUPS) == n, first + row_ids, row_ids)
    seen = key_ids <= row_ids

    queries = jnp.concatenate([r[...] for r in (q0_ref, q1_ref, q2_ref, q3_ref)], 0)
    queries = queries.astype(jnp.float32)
    outs, peaks, sums = [], [], []
    for kv in range(KVS):
        cols = slice(kv * HEAD, (kv + 1) * HEAD)
        q = queries[:, kv * GROUPS : (kv + 1) * GROUPS, :].reshape(rows, HEAD).astype(jnp.bfloat16)
        keys = [r[:, 0:BLOCK, cols].reshape(NZ * BLOCK, HEAD) for r in (near_ref, far_ref)]
        values = [r[:, BLOCK : 2 * BLOCK, cols].reshape(NZ * BLOCK, HEAD) for r in (near_ref, far_ref)]
        tails = [r[:, 2 * BLOCK : UNIT, cols].astype(jnp.float32) for r in (near_ref, far_ref)]
        tail_keys = jnp.concatenate([t[:, 0:8].reshape(NZ * 8, HEAD) for t in tails], 0)
        tail_values = jnp.concatenate([t[:, 8:16].reshape(NZ * 8, HEAD) for t in tails], 0)
        keys = jnp.concatenate(keys, 0)
        values = jnp.concatenate(values, 0)
        scores = transpose_dot(q, keys) * SCALE + bias
        tail = transpose_dot(q, tail_keys.astype(jnp.bfloat16)) * SCALE
        tail = jnp.where(seen, tail, NEG)
        peak = jnp.maximum(
            jnp.max(scores, axis=1, keepdims=True), jnp.max(tail, axis=1, keepdims=True)
        )
        peak = peak.astype(jnp.bfloat16).astype(jnp.float32)
        weights = jnp.exp(scores - peak).astype(jnp.bfloat16)
        tail_weights = jnp.exp(tail - peak).astype(jnp.bfloat16)
        total = jnp.sum(weights.astype(jnp.float32), axis=1, keepdims=True) + jnp.sum(
            tail_weights.astype(jnp.float32), axis=1, keepdims=True
        )
        mixed = jnp.dot(weights, values, preferred_element_type=jnp.float32) + jnp.dot(
            tail_weights, tail_values.astype(jnp.bfloat16), preferred_element_type=jnp.float32
        )
        shape = (NX * QTOK, GROUPS, HEAD)
        outs.append(mixed.reshape(shape))
        peaks.append(jnp.broadcast_to(peak, (rows, HEAD)).reshape(shape))
        sums.append(jnp.broadcast_to(total, (rows, HEAD)).reshape(shape))
    out = jnp.concatenate(outs, 1).astype(jnp.bfloat16)
    peak = jnp.concatenate(peaks, 1)
    total = jnp.concatenate(sums, 1)
    high = total.astype(jnp.bfloat16).astype(jnp.float32)
    lane = lax.broadcasted_iota(jnp.int32, peak.shape, 2)
    stats = jnp.where(lane == 0, peak, jnp.where(lane == 1, high, jnp.where(lane == 2, total - high, 0.0)))
    stats = stats.astype(jnp.bfloat16)
    for n, owner in enumerate(owners):
        target = pl.ds(owner * QTOK, QTOK)
        out_ref[target, 0:HEADS, :] = out[n * QTOK : (n + 1) * QTOK]
        out_ref[target, HEADS : 2 * HEADS, :] = stats[n * QTOK : (n + 1) * QTOK]


def merge_kernel(parts_ref, out_ref):
    sums = parts_ref[:, 0:HEADS, :].astype(jnp.float32)
    stats = parts_ref[:, HEADS : 2 * HEADS, :].astype(jnp.float32)
    peaks = stats[:, :, 0:1]
    totals = stats[:, :, 1:2] + stats[:, :, 2:3]
    parts = [slice(x * NT, (x + 1) * NT) for x in range(NX)]
    top = functools.reduce(jnp.maximum, [peaks[p] for p in parts])
    scales = [jnp.exp(peaks[p] - top) for p in parts]
    num = sum(sums[p] * s for p, s in zip(parts, scales))
    den = sum(totals[p] * s for p, s in zip(parts, scales))
    result = num / den
    for t in range(NT):
        for h in range(HEADS):
            at = (t * HEADS + h) * HEAD
            out_ref[:, at : at + HEAD] = result[t, h : h + 1, :].astype(jnp.bfloat16)


def block_kernel(
    place_ref, fill_ref, query_ref, unit_ref, a0_ref, a1_ref, a2_ref, a3_ref, out_ref, anchor_ref
):
    x, z, core = place_ref[0], place_ref[1], place_ref[2]
    device = x * (NZ * NC) + z * NC + core
    for n, ref in enumerate((a0_ref, a1_ref, a2_ref, a3_ref)):

        @pl.when(x == n)
        def _():
            anchor_ref[...] = ref[...]

    row = lax.broadcasted_iota(jnp.int32, (BLOCK, 2 * BLOCK), 0)
    col = lax.broadcasted_iota(jnp.int32, (BLOCK, 2 * BLOCK), 1)
    own = col - BLOCK
    own_fill = fill_ref[device]
    anchor_fill = jnp.where(device > 0, fill_ref[0], 0)
    limit = jnp.where(col < BLOCK, anchor_fill, own_fill + BLOCK)
    allowed = (col < limit) & (own <= row)
    keep = lax.broadcasted_iota(jnp.int32, (BLOCK, 1), 0) < own_fill
    for kv in range(KVS):
        cols = slice(kv * HEAD, (kv + 1) * HEAD)
        keys = jnp.concatenate([anchor_ref[0:BLOCK, cols], unit_ref[0:BLOCK, cols]], 0)
        values = jnp.concatenate(
            [anchor_ref[BLOCK : 2 * BLOCK, cols], unit_ref[BLOCK : 2 * BLOCK, cols]], 0
        )
        heads = range(kv * GROUPS, (kv + 1) * GROUPS)
        q = jnp.concatenate([query_ref[:, h * HEAD : (h + 1) * HEAD] for h in heads], 0)
        scores = transpose_dot(q, keys) * SCALE
        scores = scores.reshape(GROUPS, BLOCK, 2 * BLOCK)
        scores = jnp.where(allowed[None], scores, NEG)
        peak = jnp.max(scores, axis=2, keepdims=True)
        weights = jnp.exp(scores - peak).astype(jnp.bfloat16)
        total = jnp.sum(weights.astype(jnp.float32), axis=2, keepdims=True)
        mixed = jnp.dot(
            weights.reshape(GROUPS * BLOCK, 2 * BLOCK), values, preferred_element_type=jnp.float32
        )
        mixed = mixed.reshape(GROUPS, BLOCK, HEAD) / total
        mixed = jnp.where(keep[None], mixed, 0.0).astype(jnp.bfloat16)
        for n, h in enumerate(heads):
            out_ref[:, h * HEAD : (h + 1) * HEAD] = mixed[n]


def shifted(array, axis, size, shift):
    return lax.ppermute(array, axis, [(i, (i + shift) % size) for i in range(size)])


def per_device(
    block_query, block_key, block_value, question_query, question_key, question_value, block_fill
):
    bf16 = jnp.bfloat16
    x, z, core = lax.axis_index("x"), lax.axis_index("z"), lax.axis_index("core")
    place = jnp.stack([x, z, core]).astype(jnp.int32)

    unit, asked = pl.pallas_call(
        prepare_kernel,
        out_shape=(
            jax.ShapeDtypeStruct((UNIT, KVS * HEAD), bf16),
            jax.ShapeDtypeStruct((QTOK, HEADS, HEAD), bf16),
        ),
        in_specs=[VMEM] * 5,
        out_specs=(VMEM, VMEM),
        compiler_params=PARAMS,
        name="prepare",
    )(question_query, block_key, block_value, question_key, question_value)

    up = down = unit
    ups, downs = [], []
    for step in range(1, NZ // 2 + 1):
        up = shifted(up, "z", NZ, 1)
        ups.append(up)
        if step < NZ // 2:
            down = shifted(down, "z", NZ, NZ - 1)
            downs.append(down)
    others = [shifted(asked, "x", NX, s) for s in X_SHIFTS[1:]]
    near = jnp.stack([unit] + ups + downs)
    far = lax.ppermute(near, "core", [(0, 1), (1, 0)])

    offset = lax.rem(NZ - z, NZ)
    index = jnp.where(z <= NZ // 2, z, NZ // 2 + offset)
    first = lax.dynamic_index_in_dim(
        jnp.where(core == 0, near[:, : 2 * BLOCK], far[:, : 2 * BLOCK]), index, 0, keepdims=False
    )
    anchor1 = lax.ppermute(first, "x", [(0, 1)])
    anchor3 = lax.ppermute(first, "x", [(0, 3)])
    anchor2 = lax.ppermute(anchor1, "x", [(1, 2)])

    parts = pl.pallas_call(
        question_kernel,
        out_shape=jax.ShapeDtypeStruct((NX * NT, 2 * HEADS, HEAD), bf16),
        in_specs=[SMEM, SMEM] + [VMEM] * 6,
        out_specs=VMEM,
        compiler_params=PARAMS,
        name="question",
    )(place, block_fill, asked, *others, near, far)

    parts = lax.all_to_all(parts, ("x", "tp"), 0, 0, tiled=True)

    block_output = pl.pallas_call(
        block_kernel,
        out_shape=jax.ShapeDtypeStruct(block_query.shape, bf16),
        in_specs=[SMEM, SMEM] + [VMEM] * 6,
        out_specs=VMEM,
        scratch_shapes=[pltpu.VMEM((2 * BLOCK, KVS * HEAD), bf16)],
        compiler_params=PARAMS,
        name="block",
    )(place, block_fill, block_query, unit, first, anchor1, anchor2, anchor3)

    question_output = pl.pallas_call(
        merge_kernel,
        out_shape=jax.ShapeDtypeStruct((1, NH * HEAD), bf16),
        in_specs=[VMEM],
        out_specs=VMEM,
        compiler_params=PARAMS,
        name="merge",
    )(parts)
    return block_output, question_output


def solution(mesh):
    fine = Mesh(mesh.devices.reshape(NX, NZ, NC, NT), ("x", "z", "core", "tp"))
    ctx = ("x", "z", "core")
    placed = P(ctx, "tp")
    return jax.shard_map(
        per_device,
        mesh=fine,
        in_specs=(placed,) * 6 + (P(),),
        out_specs=(placed, P(("x", "z", "core", "tp"), None)),
        check_vma=False,
    )
```

time: 655 us -> 56.2 us (0.09)
  the two profiles are of different devices: /device:TPU:32 before, /device:TPU:6 now
where the time goes in v1:
time: 56.2 us; the launch traced here: 55.8 us
  starting transfers between devices  26.4 us (47%)
  waiting for transfers between devices  19.8 us (35%)
  Pallas kernels  5.03 us (9%)
  local copies, waits for them, and re-layouts  3.72 us (7%)
  between operations  0.79 us (1%)
    ppermute x10, starting transfers between devices, shifted(): lax.ppermute(array, axis, [(i, (i + shift) % size) for i in range(size)])  16.1 us
    ppermute x10, waiting for transfers between devices, shifted(): lax.ppermute(array, axis, [(i, (i + shift) % size) for i in range(size)])  15.2 us
    all_to_all x1, starting transfers between devices, per_device(): parts = lax.all_to_all(parts, ('x', 'tp'), 0, 0, tiled=True)  7.56 us
    all_to_all x1, waiting for transfers between devices, per_device(): parts = lax.all_to_all(parts, ('x', 'tp'), 0, 0, tiled=True)  3.9 us
    unnamed x21, local copies, waits for them, and re-layouts  3.64 us
    pallas_call x1, Pallas kernels, per_device(): pl.pallas_call(question_kernel, out_shape=jax.ShapeDtypeStruct((NX * NT,...  2.18 us
    pallas_call x1, Pallas kernels, per_device(): pl.pallas_call(block_kernel, out_shape=jax.ShapeDtypeStruct(block_query.s...  1.97 us
    ppermute x1, starting transfers between devices, per_device(): anchor3 = lax.ppermute(first, 'x', [(0, 3)])  1.28 us
  transfers between devices with their start and end apart: 15, of which 8 were waited for; matrix products, arithmetic and copies ran while one was open for 0% of the time, Pallas kernels for 5%

profile of v1, /device:TPU:6, one launch (start us, length us, event | category | flops | bytes accessed | tf_op | source)
XLA Modules:
  0.0 55.8 jit_solution(5268122862020510256)
XLA Ops:
  0.6 0.0 copy-start.1
  0.6 0.7 %copy-done.1 = bf16[64,256]{1,0:T(8,128)(2,1)S(1)} copy-done((bf16[64,256]{1,0:T(8,128)(2,1)S(1)}, bf16[64,256]{1,0:T(8,128)(2,1)}, u32[]{:S(2)}) %copy-start.1) | copy-done | bytes 32792
  1.4 0.0 copy-start.2
  1.4 0.8 %copy-done.2 = bf16[64,256]{1,0:T(8,128)(2,1)S(1)} copy-done((bf16[64,256]{1,0:T(8,128)(2,1)S(1)}, bf16[64,256]{1,0:T(8,128)(2,1)}, u32[]{:S(2)}) %copy-start.2) | copy-done | bytes 32792
  2.1 0.0 copy-start.3
  2.2 0.7 %copy-done.3 = bf16[4,2048]{1,0:T(4,128)(2,1)S(1)} copy-done((bf16[4,2048]{1,0:T(4,128)(2,1)S(1)}, bf16[4,2048]{1,0:T(4,128)(2,1)}, u32[]{:S(2)}) %copy-start.3) | copy-done | bytes 16408
  2.9 0.0 copy-start.4
  2.9 0.7 %copy-done.4 = bf16[4,256]{1,0:T(4,128)(2,1)S(1)} copy-done((bf16[4,256]{1,0:T(4,128)(2,1)S(1)}, bf16[4,256]{1,0:T(4,128)(2,1)}, u32[]{:S(2)}) %copy-start.4) | copy-done | bytes 2072
  3.5 0.0 copy-start.5
  3.6 0.7 %copy-done.5 = bf16[4,256]{1,0:T(4,128)(2,1)S(1)} copy-done((bf16[4,256]{1,0:T(4,128)(2,1)S(1)}, bf16[4,256]{1,0:T(4,128)(2,1)}, u32[]{:S(2)}) %copy-start.5) | copy-done | bytes 2072
  4.3 2.0 %collective-permute-start = (bf16[144,256]{1,0:T(8,128)(2,1)S(1)}, bf16[144,256]{1,0:T(8,128)(2,1)S(1)}, u32[]{:S(2)}, u32[]{:S(2)}) collective-permute-start(bf16[144,256]{1,0:T(8,128)(2,1)S(1)} %get-tuple-element.4.unit_ref), channel_id=1, source_target_pairs={{0,8},{8,16},{16,24},{24,32},{32,40},{40,48},{48,56},{56,0},{1,9},... | collective-permute-start | bytes 221192 | tf_op jit(solution)/shard_map/ppermute | solution.py:186
  6.3 4.0 %collective-permute-start.4 = (bf16[144,256]{1,0:T(8,128)(2,1)S(1)}, bf16[144,256]{1,0:T(8,128)(2,1)S(1)}, u32[]{:S(2)}, u32[]{:S(2)}) collective-permute-start(bf16[144,256]{1,0:T(8,128)(2,1)S(1)} %get-tuple-element.4.unit_ref), channel_id=1, source_target_pairs={{0,56},{8,0},{16,8},{24,16},{32,24},{40,32},{48,40},{56,48},{1,57}... | collective-permute-start | bytes 221192 | tf_op jit(solution)/shard_map/ppermute | solution.py:186
  10.3 2.2 %collective-permute-done = bf16[144,256]{1,0:T(8,128)(2,1)S(1)} collective-permute-done((bf16[144,256]{1,0:T(8,128)(2,1)S(1)}, bf16[144,256]{1,0:T(8,128)(2,1)S(1)}, u32[]{:S(2)}, u32[]{:S(2)}) %collective-permute-start) | collective-permute-done | bytes 73760 | tf_op jit(solution)/shard_map/ppermute | solution.py:186
  12.5 0.0 collective-permute-start.1
  12.5 0.0 collective-permute-done.4
  12.6 3.3 %collective-permute-start.5 = (bf16[144,256]{1,0:T(8,128)(2,1)S(1)}, bf16[144,256]{1,0:T(8,128)(2,1)S(1)}, u32[]{:S(2)}, u32[]{:S(2)}) collective-permute-start(bf16[144,256]{1,0:T(8,128)(2,1)S(1)} %collective-permute-done.4), channel_id=1, source_target_pairs={{0,56},{8,0},{16,8},{24,16},{32,24},{40,32},{48,40},{56,48},{1,57}... | collective-permute-start | bytes 221192 | tf_op jit(solution)/shard_map/ppermute | solution.py:186
  15.9 2.2 %collective-permute-done.1 = bf16[144,256]{1,0:T(8,128)(2,1)S(1)} collective-permute-done((bf16[144,256]{1,0:T(8,128)(2,1)S(1)}, bf16[144,256]{1,0:T(8,128)(2,1)S(1)}, u32[]{:S(2)}, u32[]{:S(2)}) %collective-permute-start.1) | collective-permute-done | bytes 73760 | tf_op jit(solution)/shard_map/ppermute | solution.py:186
  18.1 0.0 collective-permute-start.2
  18.1 0.0 collective-permute-done.5
  18.1 3.3 %collective-permute-start.6 = (bf16[144,256]{1,0:T(8,128)(2,1)S(1)}, bf16[144,256]{1,0:T(8,128)(2,1)S(1)}, u32[]{:S(2)}, u32[]{:S(2)}) collective-permute-start(bf16[144,256]{1,0:T(8,128)(2,1)S(1)} %collective-permute-done.5), channel_id=1, source_target_pairs={{0,56},{8,0},{16,8},{24,16},{32,24},{40,32},{48,40},{56,48},{1,57}... | collective-permute-start | bytes 221192 | tf_op jit(solution)/shard_map/ppermute | solution.py:186
  21.4 2.2 %collective-permute-done.2 = bf16[144,256]{1,0:T(8,128)(2,1)S(1)} collective-permute-done((bf16[144,256]{1,0:T(8,128)(2,1)S(1)}, bf16[144,256]{1,0:T(8,128)(2,1)S(1)}, u32[]{:S(2)}, u32[]{:S(2)}) %collective-permute-start.2) | collective-permute-done | bytes 73760 | tf_op jit(solution)/shard_map/ppermute | solution.py:186
  23.7 0.0 collective-permute-start.3
  23.7 5.6 %collective-permute-done.3 = bf16[144,256]{1,0:T(8,128)(2,1)S(1)} collective-permute-done((bf16[144,256]{1,0:T(8,128)(2,1)S(1)}, bf16[144,256]{1,0:T(8,128)(2,1)S(1)}, u32[]{:S(2)}, u32[]{:S(2)}) %collective-permute-start.3) | collective-permute-done | bytes 73760 | tf_op jit(solution)/shard_map/ppermute | solution.py:186
  29.3 0.0 collective-permute-done.6
  29.3 0.1 collective-permute-start.7
  29.4 0.6 collective-permute-start.11
  29.9 1.5 %collective-permute-start.12 = (bf16[4,16,128]{2,1,0:T(8,128)(2,1)S(1)}, bf16[4,16,128]{2,1,0:T(8,128)(2,1)S(1)}, u32[]{:S(2)}, u32[]{:S(2)}) collective-permute-start(bf16[4,16,128]{2,1,0:T(8,128)(2,1)S(1)} %get-tuple-element.5.q0_ref), channel_id=1, source_target_pairs={{0,192},{64,0},{128,64},{192,128},{1,193},{65,1},{129,65},{193,129... | collective-permute-start | bytes 49160 | tf_op jit(solution)/shard_map/ppermute | solution.py:186
  31.5 1.4 %collective-permute-start.13 = (bf16[4,16,128]{2,1,0:T(8,128)(2,1)S(1)}, bf16[4,16,128]{2,1,0:T(8,128)(2,1)S(1)}, u32[]{:S(2)}, u32[]{:S(2)}) collective-permute-start(bf16[4,16,128]{2,1,0:T(8,128)(2,1)S(1)} %get-tuple-element.5.q0_ref), channel_id=1, source_target_pairs={{0,128},{64,192},{128,0},{192,64},{1,129},{65,193},{129,1},{193,65... | collective-permute-start | bytes 49160 | tf_op jit(solution)/shard_map/ppermute | solution.py:186
  32.9 0.0 collective-permute-done.7.far_ref
  33.0 0.7 %collective-permute-start.8 = (bf16[128,256]{1,0:T(8,128)(2,1)S(1)}, bf16[128,256]{1,0:T(8,128)(2,1)S(1)}, u32[]{:S(2)}, u32[]{:S(2)}) collective-permute-start(bf16[128,256]{1,0:T(8,128)(2,1)S(1)} %fusion.a0_ref), channel_id=1, source_target_pairs={{0,64},{1,65},{2,66},{3,67},{4,68},{5,69},{6,70},{7,71},{8,72},{9,... | collective-permute-start | bytes 196616 | tf_op jit(solution)/shard_map/ppermute | solution.py:225
  33.7 0.0 copy-start.6
  33.7 0.1 pad_add_fusion.place_ref
  33.8 0.0 collective-permute-done.11.q1_ref
  33.8 1.1 %collective-permute-done.12.q2_ref = bf16[4,16,128]{2,1,0:T(8,128)(2,1)S(1)} collective-permute-done((bf16[4,16,128]{2,1,0:T(8,128)(2,1)S(1)}, bf16[4,16,128]{2,1,0:T(8,128)(2,1)S(1)}, u32[]{:S(2)}, u32[]{:S(2)}) %collective-permute-start.12) | collective-permute-done | bytes 16416 | tf_op jit(solution)/shard_map/ppermute | solution.py:186
  34.9 1.8 %collective-permute-done.13.q3_ref = bf16[4,16,128]{2,1,0:T(8,128)(2,1)S(1)} collective-permute-done((bf16[4,16,128]{2,1,0:T(8,128)(2,1)S(1)}, bf16[4,16,128]{2,1,0:T(8,128)(2,1)S(1)}, u32[]{:S(2)}, u32[]{:S(2)}) %collective-permute-start.13) | collective-permute-done | bytes 16416 | tf_op jit(solution)/shard_map/ppermute | solution.py:186
  36.7 0.0 copy-done.6
  36.7 2.2 %question.1 = bf16[16,32,128]{2,1,0:T(8,128)(2,1)} custom-call(s32[3]{0:T(128)S(1)} %pad_add_fusion.place_ref, s32[64]{0:T(128)S(1)} %copy-done.6, bf16[4,16,128]{2,1,0:T(8,128)(2,1)S(1)} %get-tuple-element.5.q0_ref, bf16[4,16,128]{2,1,0:T(8,128)(2,1)S(1)} %collective-permute-done.11.q1_ref, bf16[4,16,128]{2,1,0:T(8,128)(2,1)S(1)} %collective-permute-done.12.q2_ref, ...), custom_call_target="tpu_custom_call" | custom-call | tf_op jit(solution)/shard_map/question/pallas_call | solution.py:229
  38.9 0.0 copy-start
  38.9 7.6 %all-to-all-start = ((bf16[16,32,128]{2,1,0:T(8,128)(2,1)}), bf16[16,32,128]{2,1,0:T(8,128)(2,1)S(1)}, u32[]{:S(2)}, u32[]{:S(2)}) async-start(bf16[16,32,128]{2,1,0:T(8,128)(2,1)} %question.1), calls=%async_computation | async-start | bytes 262144 | tf_op jit(solution)/shard_map/all_to_all | solution.py:238
  46.5 1.3 %collective-permute-start.10 = (bf16[128,256]{1,0:T(8,128)(2,1)S(1)}, bf16[128,256]{1,0:T(8,128)(2,1)S(1)}, u32[]{:S(2)}, u32[]{:S(2)}) collective-permute-start(bf16[128,256]{1,0:T(8,128)(2,1)S(1)} %fusion.a0_ref), channel_id=1, source_target_pairs={{0,192},{1,193},{2,194},{3,195},{4,196},{5,197},{6,198},{7,199},{8... | collective-permute-start | bytes 196616 | tf_op jit(solution)/shard_map/ppermute | solution.py:226
  47.8 0.0 collective-permute-done.8.a1_ref
  47.8 0.7 %collective-permute-start.9 = (bf16[128,256]{1,0:T(8,128)(2,1)S(1)}, bf16[128,256]{1,0:T(8,128)(2,1)S(1)}, u32[]{:S(2)}, u32[]{:S(2)}) collective-permute-start(bf16[128,256]{1,0:T(8,128)(2,1)S(1)} %collective-permute-done.8.a1_ref), channel_id=1, source_target_pairs={{64,128},{65,129},{66,130},{67,131},{68,132},{69,133},{70,134},{71... | collective-permute-start | bytes 196616 | tf_op jit(solution)/shard_map/ppermute | solution.py:227
  48.4 3.9 %all-to-all-done.parts_ref = bf16[16,32,128]{2,1,0:T(8,128)(2,1)S(1)} async-done(((bf16[16,32,128]{2,1,0:T(8,128)(2,1)}), bf16[16,32,128]{2,1,0:T(8,128)(2,1)S(1)}, u32[]{:S(2)}, u32[]{:S(2)}) %all-to-all-start) | async-done | bytes 131104 | tf_op jit(solution)/shard_map/all_to_all | solution.py:238
  52.3 0.9 %merge.1 = bf16[1,8192]{1,0:T(2,128)(2,1)} custom-call(bf16[16,32,128]{2,1,0:T(8,128)(2,1)S(1)} %all-to-all-done.parts_ref), custom_call_target="tpu_custom_call" | custom-call | tf_op jit(solution)/shard_map/merge/pallas_call | solution.py:250
  53.2 0.6 %collective-permute-done.10.a3_ref = bf16[128,256]{1,0:T(8,128)(2,1)S(1)} collective-permute-done((bf16[128,256]{1,0:T(8,128)(2,1)S(1)}, bf16[128,256]{1,0:T(8,128)(2,1)S(1)}, u32[]{:S(2)}, u32[]{:S(2)}) %collective-permute-start.10) | collective-permute-done | bytes 65568 | tf_op jit(solution)/shard_map/ppermute | solution.py:226
  53.8 0.0 collective-permute-done.9.a2_ref
  53.8 0.0 copy-done
  53.8 2.0 %block.1 = bf16[64,2048]{1,0:T(8,128)(2,1)} custom-call(s32[3]{0:T(128)S(1)} %pad_add_fusion.place_ref, s32[64]{0:T(128)S(1)} %copy-done.6, bf16[64,2048]{1,0:T(8,128)(2,1)S(1)} %copy-done, bf16[144,256]{1,0:T(8,128)(2,1)S(1)} %get-tuple-element.4.unit_ref, bf16[128,256]{1,0:T(8,128)(2,1)S(1)} %fusion.a0_ref, ...), custom_call_target="tpu_custom_call" | custom-call | tf_op jit(solution)/shard_map/block/pallas_call | solution.py:240
  (12 shorter events, 0.2 us)
Async XLA Ops:
  0.6 0.8 %copy-start.1 = (bf16[64,256]{1,0:T(8,128)(2,1)S(1)}, bf16[64,256]{1,0:T(8,128)(2,1)}, u32[]{:S(2)}) copy-start(bf16[64,256]{1,0:T(8,128)(2,1)} %key_ref.1) | copy-start | bytes 98308
  1.4 0.8 %copy-start.2 = (bf16[64,256]{1,0:T(8,128)(2,1)S(1)}, bf16[64,256]{1,0:T(8,128)(2,1)}, u32[]{:S(2)}) copy-start(bf16[64,256]{1,0:T(8,128)(2,1)} %value_ref.1) | copy-start | bytes 98308
  2.1 0.7 %copy-start.3 = (bf16[4,2048]{1,0:T(4,128)(2,1)S(1)}, bf16[4,2048]{1,0:T(4,128)(2,1)}, u32[]{:S(2)}) copy-start(bf16[4,2048]{1,0:T(4,128)(2,1)} %query_ref.2) | copy-start | bytes 49156
  2.9 0.7 %copy-start.4 = (bf16[4,256]{1,0:T(4,128)(2,1)S(1)}, bf16[4,256]{1,0:T(4,128)(2,1)}, u32[]{:S(2)}) copy-start(bf16[4,256]{1,0:T(4,128)(2,1)} %ask_key_ref.1) | copy-start | bytes 6148
  3.5 0.7 %copy-start.5 = (bf16[4,256]{1,0:T(4,128)(2,1)S(1)}, bf16[4,256]{1,0:T(4,128)(2,1)}, u32[]{:S(2)}) copy-start(bf16[4,256]{1,0:T(4,128)(2,1)} %ask_value_ref.1) | copy-start | bytes 6148
  4.3 8.3 %collective-permute-start = (bf16[144,256]{1,0:T(8,128)(2,1)S(1)}, bf16[144,256]{1,0:T(8,128)(2,1)S(1)}, u32[]{:S(2)}, u32[]{:S(2)}) collective-permute-start(bf16[144,256]{1,0:T(8,128)(2,1)S(1)} %get-tuple-element.4.unit_ref), channel_id=1, source_target_pairs={{0,8},{8,16},{16,24},{24,32},{32,40},{40,48},{48,56},{56,0},{1,9},... | collective-permute-start | bytes 221192 | tf_op jit(solution)/shard_map/ppermute | solution.py:186
  6.3 6.3 %collective-permute-start.4 = (bf16[144,256]{1,0:T(8,128)(2,1)S(1)}, bf16[144,256]{1,0:T(8,128)(2,1)S(1)}, u32[]{:S(2)}, u32[]{:S(2)}) collective-permute-start(bf16[144,256]{1,0:T(8,128)(2,1)S(1)} %get-tuple-element.4.unit_ref), channel_id=1, source_target_pairs={{0,56},{8,0},{16,8},{24,16},{32,24},{40,32},{48,40},{56,48},{1,57}... | collective-permute-start | bytes 221192 | tf_op jit(solution)/shard_map/ppermute | solution.py:186
  12.5 5.6 %collective-permute-start.1 = (bf16[144,256]{1,0:T(8,128)(2,1)S(1)}, bf16[144,256]{1,0:T(8,128)(2,1)S(1)}, u32[]{:S(2)}, u32[]{:S(2)}) collective-permute-start(bf16[144,256]{1,0:T(8,128)(2,1)S(1)} %collective-permute-done), channel_id=1, source_target_pairs={{0,8},{8,16},{16,24},{24,32},{32,40},{40,48},{48,56},{56,0},{1,9},... | collective-permute-start | bytes 221192 | tf_op jit(solution)/shard_map/ppermute | solution.py:186
  12.6 5.6 %collective-permute-start.5 = (bf16[144,256]{1,0:T(8,128)(2,1)S(1)}, bf16[144,256]{1,0:T(8,128)(2,1)S(1)}, u32[]{:S(2)}, u32[]{:S(2)}) collective-permute-start(bf16[144,256]{1,0:T(8,128)(2,1)S(1)} %collective-permute-done.4), channel_id=1, source_target_pairs={{0,56},{8,0},{16,8},{24,16},{32,24},{40,32},{48,40},{56,48},{1,57}... | collective-permute-start | bytes 221192 | tf_op jit(solution)/shard_map/ppermute | solution.py:186
  18.1 5.6 %collective-permute-start.2 = (bf16[144,256]{1,0:T(8,128)(2,1)S(1)}, bf16[144,256]{1,0:T(8,128)(2,1)S(1)}, u32[]{:S(2)}, u32[]{:S(2)}) collective-permute-start(bf16[144,256]{1,0:T(8,128)(2,1)S(1)} %collective-permute-done.1), channel_id=1, source_target_pairs={{0,8},{8,16},{16,24},{24,32},{32,40},{40,48},{48,56},{56,0},{1,9},... | collective-permute-start | bytes 221192 | tf_op jit(solution)/shard_map/ppermute | solution.py:186
  18.1 11.1 %collective-permute-start.6 = (bf16[144,256]{1,0:T(8,128)(2,1)S(1)}, bf16[144,256]{1,0:T(8,128)(2,1)S(1)}, u32[]{:S(2)}, u32[]{:S(2)}) collective-permute-start(bf16[144,256]{1,0:T(8,128)(2,1)S(1)} %collective-permute-done.5), channel_id=1, source_target_pairs={{0,56},{8,0},{16,8},{24,16},{32,24},{40,32},{48,40},{56,48},{1,57}... | collective-permute-start | bytes 221192 | tf_op jit(solution)/shard_map/ppermute | solution.py:186
  23.7 5.6 %collective-permute-start.3 = (bf16[144,256]{1,0:T(8,128)(2,1)S(1)}, bf16[144,256]{1,0:T(8,128)(2,1)S(1)}, u32[]{:S(2)}, u32[]{:S(2)}) collective-permute-start(bf16[144,256]{1,0:T(8,128)(2,1)S(1)} %collective-permute-done.2), channel_id=1, source_target_pairs={{0,8},{8,16},{16,24},{24,32},{32,40},{40,48},{48,56},{56,0},{1,9},... | collective-permute-start | bytes 221192 | tf_op jit(solution)/shard_map/ppermute | solution.py:186
  29.3 3.7 %collective-permute-start.7 = (bf16[8,144,256]{2,1,0:T(8,128)(2,1)S(1)}, bf16[8,144,256]{2,1,0:T(8,128)(2,1)S(1)}, u32[]{:S(2)}, u32[]{:S(2)}) collective-permute-start(bf16[8,144,256]{2,1,0:T(8,128)(2,1)S(1)} %bitcast_dynamic-update-slice_fusion.near_ref), channel_id=1, source_target_pairs={{0,4},{4,0},{1,5},{5,1},{2,6},{6,2},{3,7},{7,3},{8,12},{12,8},{9,1... | collective-permute-start | bytes 1769480 | tf_op jit(solution)/shard_map/ppermute | solution.py:218
  29.4 4.4 %collective-permute-start.11 = (bf16[4,16,128]{2,1,0:T(8,128)(2,1)S(1)}, bf16[4,16,128]{2,1,0:T(8,128)(2,1)S(1)}, u32[]{:S(2)}, u32[]{:S(2)}) collective-permute-start(bf16[4,16,128]{2,1,0:T(8,128)(2,1)S(1)} %get-tuple-element.5.q0_ref), channel_id=1, source_target_pairs={{0,64},{64,128},{128,192},{192,0},{1,65},{65,129},{129,193},{193,1... | collective-permute-start | bytes 49160 | tf_op jit(solution)/shard_map/ppermute | solution.py:186
  29.9 4.9 %collective-permute-start.12 = (bf16[4,16,128]{2,1,0:T(8,128)(2,1)S(1)}, bf16[4,16,128]{2,1,0:T(8,128)(2,1)S(1)}, u32[]{:S(2)}, u32[]{:S(2)}) collective-permute-start(bf16[4,16,128]{2,1,0:T(8,128)(2,1)S(1)} %get-tuple-element.5.q0_ref), channel_id=1, source_target_pairs={{0,192},{64,0},{128,64},{192,128},{1,193},{65,1},{129,65},{193,129... | collective-permute-start | bytes 49160 | tf_op jit(solution)/shard_map/ppermute | solution.py:186
  31.5 5.2 %collective-permute-start.13 = (bf16[4,16,128]{2,1,0:T(8,128)(2,1)S(1)}, bf16[4,16,128]{2,1,0:T(8,128)(2,1)S(1)}, u32[]{:S(2)}, u32[]{:S(2)}) collective-permute-start(bf16[4,16,128]{2,1,0:T(8,128)(2,1)S(1)} %get-tuple-element.5.q0_ref), channel_id=1, source_target_pairs={{0,128},{64,192},{128,0},{192,64},{1,129},{65,193},{129,1},{193,65... | collective-permute-start | bytes 49160 | tf_op jit(solution)/shard_map/ppermute | solution.py:186
  33.0 14.8 %collective-permute-start.8 = (bf16[128,256]{1,0:T(8,128)(2,1)S(1)}, bf16[128,256]{1,0:T(8,128)(2,1)S(1)}, u32[]{:S(2)}, u32[]{:S(2)}) collective-permute-start(bf16[128,256]{1,0:T(8,128)(2,1)S(1)} %fusion.a0_ref), channel_id=1, source_target_pairs={{0,64},{1,65},{2,66},{3,67},{4,68},{5,69},{6,70},{7,71},{8,72},{9,... | collective-permute-start | bytes 196616 | tf_op jit(solution)/shard_map/ppermute | solution.py:225
  33.7 3.0 %copy-start.6 = (s32[64]{0:T(128)S(1)}, s32[64]{0:T(128)}, u32[]{:S(2)}) copy-start(s32[64]{0:T(128)} %fill_ref.3) | copy-start | bytes 772
  38.9 14.9 %copy-start = (bf16[64,2048]{1,0:T(8,128)(2,1)S(1)}, bf16[64,2048]{1,0:T(8,128)(2,1)}, u32[]{:S(2)}) copy-start(bf16[64,2048]{1,0:T(8,128)(2,1)} %query_ref.3) | copy-start | bytes 786436
  38.9 13.4 %all-to-all-start = ((bf16[16,32,128]{2,1,0:T(8,128)(2,1)}), bf16[16,32,128]{2,1,0:T(8,128)(2,1)S(1)}, u32[]{:S(2)}, u32[]{:S(2)}) async-start(bf16[16,32,128]{2,1,0:T(8,128)(2,1)} %question.1), calls=%async_computation | async-start | bytes 262144 | tf_op jit(solution)/shard_map/all_to_all | solution.py:238
  46.5 7.4 %collective-permute-start.10 = (bf16[128,256]{1,0:T(8,128)(2,1)S(1)}, bf16[128,256]{1,0:T(8,128)(2,1)S(1)}, u32[]{:S(2)}, u32[]{:S(2)}) collective-permute-start(bf16[128,256]{1,0:T(8,128)(2,1)S(1)} %fusion.a0_ref), channel_id=1, source_target_pairs={{0,192},{1,193},{2,194},{3,195},{4,196},{5,197},{6,198},{7,199},{8... | collective-permute-start | bytes 196616 | tf_op jit(solution)/shard_map/ppermute | solution.py:226
  47.8 6.1 %collective-permute-start.9 = (bf16[128,256]{1,0:T(8,128)(2,1)S(1)}, bf16[128,256]{1,0:T(8,128)(2,1)S(1)}, u32[]{:S(2)}, u32[]{:S(2)}) collective-permute-start(bf16[128,256]{1,0:T(8,128)(2,1)S(1)} %collective-permute-done.8.a1_ref), channel_id=1, source_target_pairs={{64,128},{65,129},{66,130},{67,131},{68,132},{69,133},{70,134},{71... | collective-permute-start | bytes 196616 | tf_op jit(solution)/shard_map/ppermute | solution.py:227

commit v2 on v1

v2 whole, which is shorter than its diff:
```python
import functools

import jax
import jax.numpy as jnp
from jax import lax
from jax.experimental import pallas as pl
from jax.experimental.pallas import tpu as pltpu
from jax.sharding import Mesh, PartitionSpec as P

NH = 64
KV_HEADS = 8
HEAD = 128
GROUPS = NH // KV_HEADS
BLOCK = 64
QTOK = 4
NX, NZ, NC, NT = 4, 8, 2, 4
HEADS = NH // NT
KVS = KV_HEADS // NT
UNIT = 144
SCALE = HEAD**-0.5
NEG = float("-inf")
ARRIVALS = ((0, 1), (1, 1), (0, 2), (1, 2), (0, 3), (1, 3), (0, 4))
X_FLIPS = (0, 1, 3, 2)
ROWS = NX * QTOK * GROUPS
SWAP = [(0, 1), (1, 0)]

VMEM = pl.BlockSpec(memory_space=pltpu.VMEM)
SMEM = pl.BlockSpec(memory_space=pltpu.SMEM)
PARAMS = pltpu.CompilerParams(vmem_limit_bytes=32 * 1024 * 1024)


def transpose_dot(left, right):
    return lax.dot_general(
        left, right, (((1,), (1,)), ((), ())), preferred_element_type=jnp.float32
    )


def arrived(place_ref, gatherer):
    x, z = place_ref[0], place_ref[1]
    blocks = []
    for crossed, steps in ARRIVALS:
        core = 1 - gatherer if crossed else gatherer
        at = lax.rem(z + NZ + jnp.where(gatherer == 0, -steps, steps), NZ)
        blocks.append(x * (NZ * NC) + at * NC + core)
    return blocks


def question_part(place_ref, fill_ref, asked_ref, others_ref, held, blocks):
    x, z, core = place_ref[0], place_ref[1], place_ref[2]
    count = len(blocks)
    context = count * BLOCK
    lane = lax.broadcasted_iota(jnp.int32, (1, context + count * 8), 1)
    is_tail = lane >= context
    tail_lane = lane - context
    owner = jnp.where(is_tail, tail_lane // 8, lane // BLOCK)
    offset = jnp.where(is_tail, tail_lane % 8, lane % BLOCK)
    fills = jnp.zeros_like(lane)
    first_ids = jnp.zeros_like(lane)
    for n, block in enumerate(blocks):
        fills = jnp.where(owner == n, fill_ref[block], fills)
        first_ids = jnp.where(owner == n, block * QTOK, first_ids)
    fills = jnp.where(is_tail, QTOK, fills)
    seen_from = jnp.where(is_tail, first_ids + offset, 0)
    seen_from = jnp.where(offset < fills, seen_from, 1 << 20)

    row = lax.broadcasted_iota(jnp.int32, (ROWS, 1), 0)
    row_ids = (row // GROUPS) % QTOK
    for n, flip in enumerate(X_FLIPS):
        first = ((x ^ flip) * (NZ * NC) + z * NC + core) * QTOK
        row_ids = jnp.where(row // (QTOK * GROUPS) == n, first + row_ids, row_ids)
    seen = seen_from <= row_ids

    queries = jnp.concatenate([asked_ref[...], others_ref[...].reshape(-1, HEADS, HEAD)], 0)
    queries = queries.astype(jnp.float32)
    tails = [ref[..., 2 * BLOCK : UNIT, :].astype(jnp.float32) for ref in held]
    tails = jnp.concatenate([t.reshape(-1, 16, KVS * HEAD) for t in tails], 0)
    tail_keys = tails[:, 0:8].reshape(count * 8, KVS * HEAD).astype(jnp.bfloat16)
    tail_values = tails[:, 8:16].reshape(count * 8, KVS * HEAD).astype(jnp.bfloat16)
    found = []
    for kv in range(KVS):
        cols = slice(kv * HEAD, (kv + 1) * HEAD)
        q = queries[:, kv * GROUPS : (kv + 1) * GROUPS, :].reshape(ROWS, HEAD).astype(jnp.bfloat16)
        keys = [ref[..., 0:BLOCK, cols].reshape(-1, HEAD) for ref in held]
        values = [ref[..., BLOCK : 2 * BLOCK, cols].reshape(-1, HEAD) for ref in held]
        keys = jnp.concatenate(keys + [tail_keys[:, cols]], 0)
        values = jnp.concatenate(values + [tail_values[:, cols]], 0)
        scores = jnp.where(seen, transpose_dot(q, keys) * SCALE, NEG)
        found.append((scores, jnp.max(scores, axis=1, keepdims=True), values))
    return found


def weigh(scores, peak, values):
    weights = jnp.exp(scores - peak).astype(jnp.bfloat16)
    total = jnp.sum(weights.astype(jnp.float32), axis=1, keepdims=True)
    return total, jnp.dot(weights, values, preferred_element_type=jnp.float32)


def rounded(array):
    return array.astype(jnp.bfloat16).astype(jnp.float32)


def near_kernel(
    place_ref, fill_ref, asked_ref, others_ref, unit_ref, swapped_ref, near_ref,
    peak_ref, total_ref, mixed_ref
):
    x, z, core = place_ref[0], place_ref[1], place_ref[2]
    own = x * (NZ * NC) + z * NC
    blocks = [own + core, own + 1 - core] + arrived(place_ref, core)
    held = (unit_ref, swapped_ref, near_ref)
    found = question_part(place_ref, fill_ref, asked_ref, others_ref, held, blocks)
    for kv, (scores, peak, values) in enumerate(found):
        peak = rounded(peak)
        total, mixed = weigh(scores, peak, values)
        peak_ref[kv] = jnp.broadcast_to(peak, (ROWS, HEAD))
        total_ref[kv] = jnp.broadcast_to(total, (ROWS, HEAD))
        mixed_ref[kv] = mixed


def far_kernel(
    place_ref, fill_ref, asked_ref, others_ref, far_ref, peak_ref, total_ref, mixed_ref, out_ref
):
    x, core = place_ref[0], place_ref[2]
    blocks = arrived(place_ref, 1 - core)
    found = question_part(place_ref, fill_ref, asked_ref, others_ref, (far_ref,), blocks)
    shape = (NX * QTOK, GROUPS, HEAD)
    outs, peaks, sums = [], [], []
    for kv, (scores, peak, values) in enumerate(found):
        old = peak_ref[kv]
        peak = rounded(jnp.maximum(peak, old[:, 0:1]))
        total, mixed = weigh(scores, peak, values)
        scale = jnp.exp(old - peak)
        outs.append((mixed + mixed_ref[kv] * scale).reshape(shape))
        peaks.append(jnp.broadcast_to(peak, (ROWS, HEAD)).reshape(shape))
        sums.append((total + total_ref[kv] * scale).reshape(shape))
    out = jnp.concatenate(outs, 1).astype(jnp.bfloat16)
    peak = jnp.concatenate(peaks, 1)
    total = jnp.concatenate(sums, 1)
    high = rounded(total)
    lane = lax.broadcasted_iota(jnp.int32, peak.shape, 2)
    stats = jnp.where(lane == 0, peak, jnp.where(lane == 1, high, jnp.where(lane == 2, total - high, 0.0)))
    stats = stats.astype(jnp.bfloat16)
    for n, flip in enumerate(X_FLIPS):
        target = pl.ds((x ^ flip) * QTOK, QTOK)
        out_ref[target, 0:HEADS, :] = out[n * QTOK : (n + 1) * QTOK]
        out_ref[target, HEADS : 2 * HEADS, :] = stats[n * QTOK : (n + 1) * QTOK]


def merge_kernel(parts_ref, out_ref):
    sums = parts_ref[:, 0:HEADS, :].astype(jnp.float32)
    stats = parts_ref[:, HEADS : 2 * HEADS, :].astype(jnp.float32)
    peaks = stats[:, :, 0:1]
    totals = stats[:, :, 1:2] + stats[:, :, 2:3]
    parts = [slice(x * NT, (x + 1) * NT) for x in range(NX)]
    top = functools.reduce(jnp.maximum, [peaks[p] for p in parts])
    scales = [jnp.exp(peaks[p] - top) for p in parts]
    num = sum(sums[p] * s for p, s in zip(parts, scales))
    den = sum(totals[p] * s for p, s in zip(parts, scales))
    result = num / den
    for t in range(NT):
        for h in range(HEADS):
            at = (t * HEADS + h) * HEAD
            out_ref[:, at : at + HEAD] = result[t, h : h + 1, :].astype(jnp.bfloat16)


def block_kernel(
    place_ref, fill_ref, query_ref, unit_ref, anchor_ref, out_ref
):
    x, z, core = place_ref[0], place_ref[1], place_ref[2]
    device = x * (NZ * NC) + z * NC + core
    row = lax.broadcasted_iota(jnp.int32, (BLOCK, 2 * BLOCK), 0)
    col = lax.broadcasted_iota(jnp.int32, (BLOCK, 2 * BLOCK), 1)
    own = col - BLOCK
    own_fill = fill_ref[device]
    anchor_fill = jnp.where(device > 0, fill_ref[0], 0)
    limit = jnp.where(col < BLOCK, anchor_fill, own_fill + BLOCK)
    allowed = (col < limit) & (own <= row)
    keep = lax.broadcasted_iota(jnp.int32, (BLOCK, 1), 0) < own_fill
    for kv in range(KVS):
        cols = slice(kv * HEAD, (kv + 1) * HEAD)
        keys = jnp.concatenate([anchor_ref[0:BLOCK, cols], unit_ref[0:BLOCK, cols]], 0)
        values = jnp.concatenate(
            [anchor_ref[BLOCK : 2 * BLOCK, cols], unit_ref[BLOCK : 2 * BLOCK, cols]], 0
        )
        heads = range(kv * GROUPS, (kv + 1) * GROUPS)
        q = jnp.concatenate([query_ref[:, h * HEAD : (h + 1) * HEAD] for h in heads], 0)
        scores = transpose_dot(q, keys) * SCALE
        scores = scores.reshape(GROUPS, BLOCK, 2 * BLOCK)
        scores = jnp.where(allowed[None], scores, NEG)
        peak = jnp.max(scores, axis=2, keepdims=True)
        weights = jnp.exp(scores - peak).astype(jnp.bfloat16)
        total = jnp.sum(weights.astype(jnp.float32), axis=2, keepdims=True)
        mixed = jnp.dot(
            weights.reshape(GROUPS * BLOCK, 2 * BLOCK), values, preferred_element_type=jnp.float32
        )
        mixed = mixed.reshape(GROUPS, BLOCK, HEAD) / total
        mixed = jnp.where(keep[None], mixed, 0.0).astype(jnp.bfloat16)
        for n, h in enumerate(heads):
            out_ref[:, h * HEAD : (h + 1) * HEAD] = mixed[n]


def flipped(array, flip):
    return lax.ppermute(array, "x", [(i, i ^ flip) for i in range(NX)])


def moved(array, steps):
    up = [(i * NC, (i + steps) % NZ * NC) for i in range(NZ)]
    down = [(i * NC + 1, (i - steps) % NZ * NC + 1) for i in range(NZ)]
    return lax.ppermute(array, ("z", "core"), up + down)


def per_device(
    block_query, block_key, block_value, question_query, question_key, question_value, block_fill
):
    bf16, f32 = jnp.bfloat16, jnp.float32
    x, z, core = lax.axis_index("x"), lax.axis_index("z"), lax.axis_index("core")
    place = jnp.stack([x, z, core]).astype(jnp.int32)

    gap = jnp.zeros((8 - QTOK, KVS * HEAD), bf16)
    unit = jnp.concatenate([block_key, block_value, question_key, gap, question_value, gap], 0)
    swapped = lax.ppermute(unit, "core", SWAP)
    pair = jnp.stack([unit, swapped])
    step1 = moved(pair, 1)
    step2 = moved(pair, 2)
    asked = question_query.reshape(QTOK, HEADS, HEAD)
    others = [flipped(asked, f) for f in X_FLIPS[1:]]
    step2, *others = lax.optimization_barrier((step2, *others))
    others = jnp.stack(others)
    step3 = moved(step2, 1)
    step4 = moved(step2[0], 2)
    near = jnp.concatenate([step1, step2, step3, step4[None]])
    far = lax.ppermute(near, "core", SWAP)

    rising = lax.dynamic_index_in_dim(
        jnp.where(core == 0, near, far), jnp.clip(2 * z - 2, 0, 6), 0, keepdims=False
    )
    falling = lax.dynamic_index_in_dim(
        jnp.where(core == 0, far, near), jnp.clip(2 * (NZ - z) - 1, 0, 6), 0, keepdims=False
    )
    here = jnp.where(core == 0, unit, swapped)
    first = jnp.where(z == 0, here, jnp.where(z <= NZ // 2, rising, falling))[: 2 * BLOCK]
    sent = lax.ppermute(first, ("x", "core"), [(0, NC), (1, 2 * NC + 1)])
    late = lax.ppermute(first, ("x", "core"), [(1, 3 * NC + 1)])

    question = functools.partial(pl.pallas_call, compiler_params=PARAMS)
    state = jax.ShapeDtypeStruct((KVS, ROWS, HEAD), f32)
    carry = question(
        near_kernel,
        out_shape=(state,) * 3,
        in_specs=[SMEM, SMEM] + [VMEM] * 5,
        out_specs=(VMEM,) * 3,
        cost_estimate=pl.CostEstimate(flops=10**8, bytes_accessed=10**6, transcendentals=10**5),
        name="question_near",
    )(place, block_fill, asked, others, unit, swapped, near)
    parts = question(
        far_kernel,
        out_shape=jax.ShapeDtypeStruct((NX * NT, 2 * HEADS, HEAD), bf16),
        in_specs=[SMEM, SMEM] + [VMEM] * 6,
        out_specs=VMEM,
        cost_estimate=pl.CostEstimate(flops=10**8, bytes_accessed=10**6, transcendentals=10**5),
        name="question_far",
    )(place, block_fill, asked, others, far, *carry)

    parts, sent, late = lax.optimization_barrier((parts, sent, late))
    got = jnp.where(x == NX - 1, late, sent)
    passed = lax.ppermute(got, ("x", "core"), [(2, 3), (5, 4), (7, 6)])
    receiver = jnp.where(x == 1, 0, 1)
    anchor = jnp.where(x == 0, first, jnp.where(core == receiver, got, passed))
    parts = lax.all_to_all(parts, ("x", "tp"), 0, 0, tiled=True)

    block_output = pl.pallas_call(
        block_kernel,
        out_shape=jax.ShapeDtypeStruct(block_query.shape, bf16),
        in_specs=[SMEM, SMEM] + [VMEM] * 3,
        out_specs=VMEM,
        compiler_params=PARAMS,
        name="block",
    )(place, block_fill, block_query, unit, anchor)

    question_output = pl.pallas_call(
        merge_kernel,
        out_shape=jax.ShapeDtypeStruct((1, NH * HEAD), bf16),
        in_specs=[VMEM],
        out_specs=VMEM,
        compiler_params=PARAMS,
        name="merge",
    )(parts)
    return block_output, question_output


def solution(mesh):
    fine = Mesh(mesh.devices.reshape(NX, NZ, NC, NT), ("x", "z", "core", "tp"))
    ctx = ("x", "z", "core")
    placed = P(ctx, "tp")
    return jax.shard_map(
        per_device,
        mesh=fine,
        in_specs=(placed,) * 6 + (P(),),
        out_specs=(placed, P(("x", "z", "core", "tp"), None)),
        check_vma=False,
    )
```

time: 56.2 us -> 52 us (0.925)
  the two profiles are of different devices: /device:TPU:6 before, /device:TPU:1 now
where the time goes in v2:
time: 52 us; the launch traced here: 51.5 us
  starting transfers between devices  26.4 us (51%)
  waiting for transfers between devices  14.8 us (28%)
  Pallas kernels  5.74 us (11%)
  local copies, waits for them, and re-layouts  3.56 us (7%)
  between operations  0.78 us (2%)
    ppermute x4, starting transfers between devices, moved(): return lax.ppermute(array, ('z', 'core'), up + down)  6.45 us
    all_to_all x1, starting transfers between devices, per_device(): parts = lax.all_to_all(parts, ('x', 'tp'), 0, 0, tiled=True)  5.47 us
    all_to_all x1, waiting for transfers between devices, per_device(): parts = lax.all_to_all(parts, ('x', 'tp'), 0, 0, tiled=True)  5.06 us
    ppermute x4, waiting for transfers between devices, moved(): return lax.ppermute(array, ('z', 'core'), up + down)  4.67 us
    ppermute x3, starting transfers between devices, flipped(): return lax.ppermute(array, 'x', [(i, i ^ flip) for i in range(NX)])  3.75 us
    ppermute x1, starting transfers between devices, per_device(): swapped = lax.ppermute(unit, 'core', SWAP)  3.24 us
    ppermute x1, starting transfers between devices, per_device(): sent = lax.ppermute(first, ('x', 'core'), [(0, NC), (1, 2 * NC + 1)])  2.87 us
    ppermute x3, waiting for transfers between devices, flipped(): return lax.ppermute(array, 'x', [(i, i ^ flip) for i in range(NX)])  2.73 us
  transfers between devices with their start and end apart: 13, of which 6 were waited for; matrix products, arithmetic and copies ran while one was open for 0% of the time, Pallas kernels for 9%

profile of v2, /device:TPU:1, one launch (start us, length us, event | category | flops | bytes accessed | tf_op | source)
XLA Modules:
  0.0 51.5 jit_solution(511178665702229957)
XLA Ops:
  0.6 0.0 copy-start.3
  0.7 0.7 %copy-done.3 = bf16[4,256]{1,0:T(4,128)(2,1)S(1)} copy-done((bf16[4,256]{1,0:T(4,128)(2,1)S(1)}, bf16[4,256]{1,0:T(4,128)(2,1)}, u32[]{:S(2)}) %copy-start.3) | copy-done | bytes 2072
  1.3 2.2 %concatenate.6.unit_ref = bf16[144,256]{1,0:T(8,128)(2,1)S(1)} concatenate(bf16[64,256]{1,0:T(8,128)(2,1)} %param.8, bf16[64,256]{1,0:T(8,128)(2,1)} %param.9, bf16[4,256]{1,0:T(4,128)(2,1)S(1)} %copy-done.3, bf16[4,256]{1,0:T(4,128)(2,1)S(1)} %broadcast_in_dim.6, bf16[4,256]{1,0:T(4,128)(2,1)} %param.12, bf16[4,256]{1,0:T(4,128)(2,1)S(1)} %broadcast_in_dim.6), dimensions={0} | concatenate | bytes 147456 | tf_op jit(solution)/shard_map/concatenate | solution.py:219
  3.6 3.2 %collective-permute-start = (bf16[144,256]{1,0:T(8,128)(2,1)S(1)}, bf16[144,256]{1,0:T(8,128)(2,1)S(1)}, u32[]{:S(2)}, u32[]{:S(2)}) collective-permute-start(bf16[144,256]{1,0:T(8,128)(2,1)S(1)} %concatenate.6.unit_ref), channel_id=1, source_target_pairs={{0,4},{4,0},{1,5},{5,1},{2,6},{6,2},{3,7},{7,3},{8,12},{12,8},{9,1... | collective-permute-start | bytes 221192 | tf_op jit(solution)/shard_map/ppermute | solution.py:220
  6.8 0.9 %collective-permute-done.swapped_ref = bf16[144,256]{1,0:T(8,128)(2,1)S(1)} collective-permute-done((bf16[144,256]{1,0:T(8,128)(2,1)S(1)}, bf16[144,256]{1,0:T(8,128)(2,1)S(1)}, u32[]{:S(2)}, u32[]{:S(2)}) %collective-permute-start) | collective-permute-done | bytes 73760 | tf_op jit(solution)/shard_map/ppermute | solution.py:220
  7.7 0.0 copy-start.2
  7.7 4.4 %collective-permute-start.2 = (bf16[2,144,256]{2,1,0:T(8,128)(2,1)S(1)}, bf16[2,144,256]{2,1,0:T(8,128)(2,1)S(1)}, u32[]{:S(2)}, u32[]{:S(2)}) collective-permute-start(bf16[2,144,256]{2,1,0:T(8,128)(2,1)S(1)} %pad_maximum_fusion.1), channel_id=1, source_target_pairs={{0,16},{8,24},{16,32},{24,40},{32,48},{40,56},{48,0},{56,8},{4,52}... | collective-permute-start | bytes 442376 | tf_op jit(solution)/shard_map/ppermute | solution.py:208
  12.1 0.0 copy-done.2
  12.1 1.3 %collective-permute-start.3 = (bf16[4,16,128]{2,1,0:T(8,128)(2,1)S(1)}, bf16[4,16,128]{2,1,0:T(8,128)(2,1)S(1)}, u32[]{:S(2)}, u32[]{:S(2)}) collective-permute-start(bf16[4,16,128]{2,1,0:T(8,128)(2,1)S(1)} %bitcast.19), channel_id=1, source_target_pairs={{0,64},{64,0},{128,192},{192,128},{1,65},{65,1},{129,193},{193,129... | collective-permute-start | bytes 49160 | tf_op jit(solution)/shard_map/ppermute | solution.py:202
  13.4 1.8 %collective-permute-start.4 = (bf16[4,16,128]{2,1,0:T(8,128)(2,1)S(1)}, bf16[4,16,128]{2,1,0:T(8,128)(2,1)S(1)}, u32[]{:S(2)}, u32[]{:S(2)}) collective-permute-start(bf16[4,16,128]{2,1,0:T(8,128)(2,1)S(1)} %bitcast.20), channel_id=1, source_target_pairs={{0,192},{64,128},{128,64},{192,0},{1,193},{65,129},{129,65},{193,1... | collective-permute-start | bytes 49160 | tf_op jit(solution)/shard_map/ppermute | solution.py:202
  15.2 0.6 %collective-permute-start.5 = (bf16[4,16,128]{2,1,0:T(8,128)(2,1)S(1)}, bf16[4,16,128]{2,1,0:T(8,128)(2,1)S(1)}, u32[]{:S(2)}, u32[]{:S(2)}) collective-permute-start(bf16[4,16,128]{2,1,0:T(8,128)(2,1)S(1)} %bitcast.21), channel_id=1, source_target_pairs={{0,128},{64,192},{128,0},{192,64},{1,129},{65,193},{129,1},{193,65... | collective-permute-start | bytes 49160 | tf_op jit(solution)/shard_map/ppermute | solution.py:202
  15.8 0.7 %collective-permute-start.1 = (bf16[2,144,256]{2,1,0:T(8,128)(2,1)S(1)}, bf16[2,144,256]{2,1,0:T(8,128)(2,1)S(1)}, u32[]{:S(2)}, u32[]{:S(2)}) collective-permute-start(bf16[2,144,256]{2,1,0:T(8,128)(2,1)S(1)} %pad_maximum_fusion.1), channel_id=1, source_target_pairs={{0,8},{8,16},{16,24},{24,32},{32,40},{40,48},{48,56},{56,0},{4,60}... | collective-permute-start | bytes 442376 | tf_op jit(solution)/shard_map/ppermute | solution.py:208
  16.6 0.0 collective-permute-done.3
  16.6 0.6 %collective-permute-done.4 = bf16[4,16,128]{2,1,0:T(8,128)(2,1)S(1)} collective-permute-done((bf16[4,16,128]{2,1,0:T(8,128)(2,1)S(1)}, bf16[4,16,128]{2,1,0:T(8,128)(2,1)S(1)}, u32[]{:S(2)}, u32[]{:S(2)}) %collective-permute-start.4) | collective-permute-done | bytes 16416 | tf_op jit(solution)/shard_map/ppermute | solution.py:202
  17.2 2.1 %collective-permute-done.5 = bf16[4,16,128]{2,1,0:T(8,128)(2,1)S(1)} collective-permute-done((bf16[4,16,128]{2,1,0:T(8,128)(2,1)S(1)}, bf16[4,16,128]{2,1,0:T(8,128)(2,1)S(1)}, u32[]{:S(2)}, u32[]{:S(2)}) %collective-permute-start.5) | collective-permute-done | bytes 16416 | tf_op jit(solution)/shard_map/ppermute | solution.py:202
  19.3 0.0 collective-permute-done.2
  19.3 0.7 %collective-permute-start.6 = (bf16[2,144,256]{2,1,0:T(8,128)(2,1)S(1)}, bf16[2,144,256]{2,1,0:T(8,128)(2,1)S(1)}, u32[]{:S(2)}, u32[]{:S(2)}) collective-permute-start(bf16[2,144,256]{2,1,0:T(8,128)(2,1)S(1)} %collective-permute-done.2), channel_id=1, source_target_pairs={{0,8},{8,16},{16,24},{24,32},{32,40},{40,48},{48,56},{56,0},{4,60}... | collective-permute-start | bytes 442376 | tf_op jit(solution)/shard_map/ppermute | solution.py:208
  20.0 0.6 %collective-permute-start.7 = (bf16[144,256]{1,0:T(8,128)(2,1)S(1)}, bf16[144,256]{1,0:T(8,128)(2,1)S(1)}, u32[]{:S(2)}, u32[]{:S(2)}) collective-permute-start(bf16[144,256]{1,0:T(8,128)(2,1)S(1)} %slice_bitcast_fusion), channel_id=1, source_target_pairs={{0,16},{8,24},{16,32},{24,40},{32,48},{40,56},{48,0},{56,8},{4,52}... | collective-permute-start | bytes 221192 | tf_op jit(solution)/shard_map/ppermute | solution.py:208
  20.7 0.0 collective-permute-done.1
  20.7 4.7 %collective-permute-done.7 = bf16[144,256]{1,0:T(8,128)(2,1)S(1)} collective-permute-done((bf16[144,256]{1,0:T(8,128)(2,1)S(1)}, bf16[144,256]{1,0:T(8,128)(2,1)S(1)}, u32[]{:S(2)}, u32[]{:S(2)}) %collective-permute-start.7) | collective-permute-done | bytes 73760 | tf_op jit(solution)/shard_map/ppermute | solution.py:208
  25.3 0.0 collective-permute-done.6
  25.3 0.1 pad_maximum_fusion.near_ref
  25.4 2.7 %collective-permute-start.8 = (bf16[7,144,256]{2,1,0:T(8,128)(2,1)S(1)}, bf16[7,144,256]{2,1,0:T(8,128)(2,1)S(1)}, u32[]{:S(2)}, u32[]{:S(2)}) collective-permute-start(bf16[7,144,256]{2,1,0:T(8,128)(2,1)S(1)} %pad_maximum_fusion.near_ref), channel_id=1, source_target_pairs={{0,4},{4,0},{1,5},{5,1},{2,6},{6,2},{3,7},{7,3},{8,12},{12,8},{9,1... | collective-permute-start | bytes 1548296 | tf_op jit(solution)/shard_map/ppermute | solution.py:231
  28.1 0.1 pad_add_fusion.place_ref
  28.1 1.4 %collective-permute-done.8.far_ref = bf16[7,144,256]{2,1,0:T(8,128)(2,1)S(1)} collective-permute-done((bf16[7,144,256]{2,1,0:T(8,128)(2,1)S(1)}, bf16[7,144,256]{2,1,0:T(8,128)(2,1)S(1)}, u32[]{:S(2)}, u32[]{:S(2)}) %collective-permute-start.8) | collective-permute-done | bytes 516128 | tf_op jit(solution)/shard_map/ppermute | solution.py:231
  29.6 2.9 %collective-permute-start.9 = (bf16[128,256]{1,0:T(8,128)(2,1)S(1)}, bf16[128,256]{1,0:T(8,128)(2,1)S(1)}, u32[]{:S(2)}, u32[]{:S(2)}) collective-permute-start(bf16[128,256]{1,0:T(8,128)(2,1)S(1)} %slice_select_fusion), channel_id=1, source_target_pairs={{0,64},{4,132},{1,65},{5,133},{2,66},{6,134},{3,67},{7,135},{8,72}... | collective-permute-start | bytes 196616 | tf_op jit(solution)/shard_map/ppermute | solution.py:241
  32.5 1.3 %collective-permute-start.10 = (bf16[128,256]{1,0:T(8,128)(2,1)S(1)}, bf16[128,256]{1,0:T(8,128)(2,1)S(1)}, u32[]{:S(2)}, u32[]{:S(2)}) collective-permute-start(bf16[128,256]{1,0:T(8,128)(2,1)S(1)} %slice_select_fusion), channel_id=1, source_target_pairs={{4,196},{5,197},{6,198},{7,199},{12,204},{13,205},{14,206},{15,207... | collective-permute-start | bytes 196616 | tf_op jit(solution)/shard_map/ppermute | solution.py:242
  33.8 0.0 copy-start.1
  33.9 0.6 %copy-done.1 = s32[64]{0:T(128)S(1)} copy-done((s32[64]{0:T(128)S(1)}, s32[64]{0:T(128)}, u32[]{:S(2)}) %copy-start.1) | copy-done | bytes 280
  34.5 1.1 %question_near.1 = (f32[2,128,128]{2,1,0:T(8,128)S(1)}, f32[2,128,128]{2,1,0:T(8,128)S(1)}, f32[2,128,128]{2,1,0:T(8,128)S(1)}) custom-call(s32[3]{0:T(128)S(1)} %pad_add_fusion.place_ref, s32[64]{0:T(128)S(1)} %copy-done.1, bf16[4,16,128]{2,1,0:T(8,128)(2,1)S(1)} %bitcast.22, bf16[3,4,16,128]{3,2,1,0:T(8,128)(2,1)S(1)} %pad_maximum_fusion.2.others_ref, ...), custom_call_target="tpu_custom_call" | custom-call | flops 100000000 | bytes 1000000 | tf_op jit(solution)/shard_map/question_near/pallas_call | solution.py:246
  35.6 1.8 %question_far.1 = bf16[16,32,128]{2,1,0:T(8,128)(2,1)} custom-call(s32[3]{0:T(128)S(1)} %pad_add_fusion.place_ref, s32[64]{0:T(128)S(1)} %copy-done.1, bf16[4,16,128]{2,1,0:T(8,128)(2,1)S(1)} %bitcast.23, bf16[3,4,16,128]{3,2,1,0:T(8,128)(2,1)S(1)} %pad_maximum_fusion.2.others_ref, bf16[7,144,256]{2,1,0:T(8,128)(2,1)S(1)} %collective-permute-done.8.far_ref, ...), custom_call_target="tpu_custom_call" | custom-call | flops 100000000 | bytes 1000000 | tf_op jit(solution)/shard_map/question_far/pallas_call | solution.py:254
  37.4 0.0 collective-permute-done.9
  37.4 0.0 collective-permute-done.10
  37.5 0.7 %collective-permute-start.11 = (bf16[128,256]{1,0:T(8,128)(2,1)S(1)}, bf16[128,256]{1,0:T(8,128)(2,1)S(1)}, u32[]{:S(2)}, u32[]{:S(2)}) collective-permute-start(bf16[128,256]{1,0:T(8,128)(2,1)S(1)} %broadcast_select_fusion), channel_id=1, source_target_pairs={{64,68},{132,128},{196,192},{65,69},{133,129},{197,193},{66,70},{1... | collective-permute-start | bytes 196616 | tf_op jit(solution)/shard_map/ppermute | solution.py:265
  38.1 0.0 copy-start
  38.1 5.5 %all-to-all-start = ((bf16[16,32,128]{2,1,0:T(8,128)(2,1)}), bf16[16,32,128]{2,1,0:T(8,128)(2,1)S(1)}, u32[]{:S(2)}, u32[]{:S(2)}) async-start(bf16[16,32,128]{2,1,0:T(8,128)(2,1)} %question_far.1), calls=%async_computation | async-start | bytes 262144 | tf_op jit(solution)/shard_map/all_to_all | solution.py:268
  43.6 0.0 collective-permute-done.11
  43.7 0.0 copy-done
  43.7 1.9 %block.1 = bf16[64,2048]{1,0:T(8,128)(2,1)} custom-call(s32[3]{0:T(128)S(1)} %pad_add_fusion.place_ref, s32[64]{0:T(128)S(1)} %copy-done.1, bf16[64,2048]{1,0:T(8,128)(2,1)S(1)} %copy-done, bf16[144,256]{1,0:T(8,128)(2,1)S(1)} %concatenate.6.unit_ref, bf16[128,256]{1,0:T(8,128)(2,1)S(1)} %select_select_fusion.anchor_ref), custom_call_target="tpu_custom_call" | custom-call | tf_op jit(solution)/shard_map/block/pallas_call | solution.py:270
  45.6 5.1 %all-to-all-done.parts_ref = bf16[16,32,128]{2,1,0:T(8,128)(2,1)S(1)} async-done(((bf16[16,32,128]{2,1,0:T(8,128)(2,1)}), bf16[16,32,128]{2,1,0:T(8,128)(2,1)S(1)}, u32[]{:S(2)}, u32[]{:S(2)}) %all-to-all-start) | async-done | bytes 131104 | tf_op jit(solution)/shard_map/all_to_all | solution.py:268
  50.7 0.9 %merge.1 = bf16[1,8192]{1,0:T(2,128)(2,1)} custom-call(bf16[16,32,128]{2,1,0:T(8,128)(2,1)S(1)} %all-to-all-done.parts_ref), custom_call_target="tpu_custom_call" | custom-call | tf_op jit(solution)/shard_map/merge/pallas_call | solution.py:279
  (9 shorter events, 0.1 us)
Async XLA Ops:
  0.6 0.7 %copy-start.3 = (bf16[4,256]{1,0:T(4,128)(2,1)S(1)}, bf16[4,256]{1,0:T(4,128)(2,1)}, u32[]{:S(2)}) copy-start(bf16[4,256]{1,0:T(4,128)(2,1)} %param.11) | copy-start | bytes 6148
  3.6 4.2 %collective-permute-start = (bf16[144,256]{1,0:T(8,128)(2,1)S(1)}, bf16[144,256]{1,0:T(8,128)(2,1)S(1)}, u32[]{:S(2)}, u32[]{:S(2)}) collective-permute-start(bf16[144,256]{1,0:T(8,128)(2,1)S(1)} %concatenate.6.unit_ref), channel_id=1, source_target_pairs={{0,4},{4,0},{1,5},{5,1},{2,6},{6,2},{3,7},{7,3},{8,12},{12,8},{9,1... | collective-permute-start | bytes 221192 | tf_op jit(solution)/shard_map/ppermute | solution.py:220
  7.7 4.4 %copy-start.2 = (bf16[4,2048]{1,0:T(4,128)(2,1)S(1)}, bf16[4,2048]{1,0:T(4,128)(2,1)}, u32[]{:S(2)}) copy-start(bf16[4,2048]{1,0:T(4,128)(2,1)} %param.10) | copy-start | bytes 49156
  7.7 11.6 %collective-permute-start.2 = (bf16[2,144,256]{2,1,0:T(8,128)(2,1)S(1)}, bf16[2,144,256]{2,1,0:T(8,128)(2,1)S(1)}, u32[]{:S(2)}, u32[]{:S(2)}) collective-permute-start(bf16[2,144,256]{2,1,0:T(8,128)(2,1)S(1)} %pad_maximum_fusion.1), channel_id=1, source_target_pairs={{0,16},{8,24},{16,32},{24,40},{32,48},{40,56},{48,0},{56,8},{4,52}... | collective-permute-start | bytes 442376 | tf_op jit(solution)/shard_map/ppermute | solution.py:208
  12.1 4.5 %collective-permute-start.3 = (bf16[4,16,128]{2,1,0:T(8,128)(2,1)S(1)}, bf16[4,16,128]{2,1,0:T(8,128)(2,1)S(1)}, u32[]{:S(2)}, u32[]{:S(2)}) collective-permute-start(bf16[4,16,128]{2,1,0:T(8,128)(2,1)S(1)} %bitcast.19), channel_id=1, source_target_pairs={{0,64},{64,0},{128,192},{192,128},{1,65},{65,1},{129,193},{193,129... | collective-permute-start | bytes 49160 | tf_op jit(solution)/shard_map/ppermute | solution.py:202
  13.4 3.8 %collective-permute-start.4 = (bf16[4,16,128]{2,1,0:T(8,128)(2,1)S(1)}, bf16[4,16,128]{2,1,0:T(8,128)(2,1)S(1)}, u32[]{:S(2)}, u32[]{:S(2)}) collective-permute-start(bf16[4,16,128]{2,1,0:T(8,128)(2,1)S(1)} %bitcast.20), channel_id=1, source_target_pairs={{0,192},{64,128},{128,64},{192,0},{1,193},{65,129},{129,65},{193,1... | collective-permute-start | bytes 49160 | tf_op jit(solution)/shard_map/ppermute | solution.py:202
  15.2 4.1 %collective-permute-start.5 = (bf16[4,16,128]{2,1,0:T(8,128)(2,1)S(1)}, bf16[4,16,128]{2,1,0:T(8,128)(2,1)S(1)}, u32[]{:S(2)}, u32[]{:S(2)}) collective-permute-start(bf16[4,16,128]{2,1,0:T(8,128)(2,1)S(1)} %bitcast.21), channel_id=1, source_target_pairs={{0,128},{64,192},{128,0},{192,64},{1,129},{65,193},{129,1},{193,65... | collective-permute-start | bytes 49160 | tf_op jit(solution)/shard_map/ppermute | solution.py:202
  15.8 4.8 %collective-permute-start.1 = (bf16[2,144,256]{2,1,0:T(8,128)(2,1)S(1)}, bf16[2,144,256]{2,1,0:T(8,128)(2,1)S(1)}, u32[]{:S(2)}, u32[]{:S(2)}) collective-permute-start(bf16[2,144,256]{2,1,0:T(8,128)(2,1)S(1)} %pad_maximum_fusion.1), channel_id=1, source_target_pairs={{0,8},{8,16},{16,24},{24,32},{32,40},{40,48},{48,56},{56,0},{4,60}... | collective-permute-start | bytes 442376 | tf_op jit(solution)/shard_map/ppermute | solution.py:208
  19.3 6.0 %collective-permute-start.6 = (bf16[2,144,256]{2,1,0:T(8,128)(2,1)S(1)}, bf16[2,144,256]{2,1,0:T(8,128)(2,1)S(1)}, u32[]{:S(2)}, u32[]{:S(2)}) collective-permute-start(bf16[2,144,256]{2,1,0:T(8,128)(2,1)S(1)} %collective-permute-done.2), channel_id=1, source_target_pairs={{0,8},{8,16},{16,24},{24,32},{32,40},{40,48},{48,56},{56,0},{4,60}... | collective-permute-start | bytes 442376 | tf_op jit(solution)/shard_map/ppermute | solution.py:208
  20.0 5.3 %collective-permute-start.7 = (bf16[144,256]{1,0:T(8,128)(2,1)S(1)}, bf16[144,256]{1,0:T(8,128)(2,1)S(1)}, u32[]{:S(2)}, u32[]{:S(2)}) collective-permute-start(bf16[144,256]{1,0:T(8,128)(2,1)S(1)} %slice_bitcast_fusion), channel_id=1, source_target_pairs={{0,16},{8,24},{16,32},{24,40},{32,48},{40,56},{48,0},{56,8},{4,52}... | collective-permute-start | bytes 221192 | tf_op jit(solution)/shard_map/ppermute | solution.py:208
  25.4 4.2 %collective-permute-start.8 = (bf16[7,144,256]{2,1,0:T(8,128)(2,1)S(1)}, bf16[7,144,256]{2,1,0:T(8,128)(2,1)S(1)}, u32[]{:S(2)}, u32[]{:S(2)}) collective-permute-start(bf16[7,144,256]{2,1,0:T(8,128)(2,1)S(1)} %pad_maximum_fusion.near_ref), channel_id=1, source_target_pairs={{0,4},{4,0},{1,5},{5,1},{2,6},{6,2},{3,7},{7,3},{8,12},{12,8},{9,1... | collective-permute-start | bytes 1548296 | tf_op jit(solution)/shard_map/ppermute | solution.py:231
  29.6 7.8 %collective-permute-start.9 = (bf16[128,256]{1,0:T(8,128)(2,1)S(1)}, bf16[128,256]{1,0:T(8,128)(2,1)S(1)}, u32[]{:S(2)}, u32[]{:S(2)}) collective-permute-start(bf16[128,256]{1,0:T(8,128)(2,1)S(1)} %slice_select_fusion), channel_id=1, source_target_pairs={{0,64},{4,132},{1,65},{5,133},{2,66},{6,134},{3,67},{7,135},{8,72}... | collective-permute-start | bytes 196616 | tf_op jit(solution)/shard_map/ppermute | solution.py:241
  32.5 4.9 %collective-permute-start.10 = (bf16[128,256]{1,0:T(8,128)(2,1)S(1)}, bf16[128,256]{1,0:T(8,128)(2,1)S(1)}, u32[]{:S(2)}, u32[]{:S(2)}) collective-permute-start(bf16[128,256]{1,0:T(8,128)(2,1)S(1)} %slice_select_fusion), channel_id=1, source_target_pairs={{4,196},{5,197},{6,198},{7,199},{12,204},{13,205},{14,206},{15,207... | collective-permute-start | bytes 196616 | tf_op jit(solution)/shard_map/ppermute | solution.py:242
  33.8 0.7 %copy-start.1 = (s32[64]{0:T(128)S(1)}, s32[64]{0:T(128)}, u32[]{:S(2)}) copy-start(s32[64]{0:T(128)} %fill_ref.5) | copy-start | bytes 772
  37.5 6.2 %collective-permute-start.11 = (bf16[128,256]{1,0:T(8,128)(2,1)S(1)}, bf16[128,256]{1,0:T(8,128)(2,1)S(1)}, u32[]{:S(2)}, u32[]{:S(2)}) collective-permute-start(bf16[128,256]{1,0:T(8,128)(2,1)S(1)} %broadcast_select_fusion), channel_id=1, source_target_pairs={{64,68},{132,128},{196,192},{65,69},{133,129},{197,193},{66,70},{1... | collective-permute-start | bytes 196616 | tf_op jit(solution)/shard_map/ppermute | solution.py:265
  38.1 5.5 %copy-start = (bf16[64,2048]{1,0:T(8,128)(2,1)S(1)}, bf16[64,2048]{1,0:T(8,128)(2,1)}, u32[]{:S(2)}) copy-start(bf16[64,2048]{1,0:T(8,128)(2,1)} %query_ref.1) | copy-start | bytes 786436
  38.1 12.5 %all-to-all-start = ((bf16[16,32,128]{2,1,0:T(8,128)(2,1)}), bf16[16,32,128]{2,1,0:T(8,128)(2,1)S(1)}, u32[]{:S(2)}, u32[]{:S(2)}) async-start(bf16[16,32,128]{2,1,0:T(8,128)(2,1)} %question_far.1), calls=%async_computation | async-start | bytes 262144 | tf_op jit(solution)/shard_map/all_to_all | solution.py:268

commit v3 on v2

--- a/solution.py
+++ b/solution.py
@@ -20,9 +20,10 @@
 SCALE = HEAD**-0.5
 NEG = float("-inf")
 ARRIVALS = ((0, 1), (1, 1), (0, 2), (1, 2), (0, 3), (1, 3), (0, 4))
-X_FLIPS = (0, 1, 3, 2)
+X_FLIPS = (0, 2, 1, 3)
 ROWS = NX * QTOK * GROUPS
 SWAP = [(0, 1), (1, 0)]
+GATHERED = len(ARRIVALS) * UNIT
 
 VMEM = pl.BlockSpec(memory_space=pltpu.VMEM)
 SMEM = pl.BlockSpec(memory_space=pltpu.SMEM)
@@ -72,16 +73,15 @@
 
     queries = jnp.concatenate([asked_ref[...], others_ref[...].reshape(-1, HEADS, HEAD)], 0)
     queries = queries.astype(jnp.float32)
-    tails = [ref[..., 2 * BLOCK : UNIT, :].astype(jnp.float32) for ref in held]
-    tails = jnp.concatenate([t.reshape(-1, 16, KVS * HEAD) for t in tails], 0)
-    tail_keys = tails[:, 0:8].reshape(count * 8, KVS * HEAD).astype(jnp.bfloat16)
-    tail_values = tails[:, 8:16].reshape(count * 8, KVS * HEAD).astype(jnp.bfloat16)
+    tails = [ref[at + 2 * BLOCK : at + UNIT, :].astype(jnp.float32) for ref, at in held]
+    tail_keys = jnp.concatenate([t[0:8] for t in tails], 0).astype(jnp.bfloat16)
+    tail_values = jnp.concatenate([t[8:16] for t in tails], 0).astype(jnp.bfloat16)
     found = []
     for kv in range(KVS):
         cols = slice(kv * HEAD, (kv + 1) * HEAD)
         q = queries[:, kv * GROUPS : (kv + 1) * GROUPS, :].reshape(ROWS, HEAD).astype(jnp.bfloat16)
-        keys = [ref[..., 0:BLOCK, cols].reshape(-1, HEAD) for ref in held]
-        values = [ref[..., BLOCK : 2 * BLOCK, cols].reshape(-1, HEAD) for ref in held]
+        keys = [ref[at : at + BLOCK, cols] for ref, at in held]
+        values = [ref[at + BLOCK : at + 2 * BLOCK, cols] for ref, at in held]
         keys = jnp.concatenate(keys + [tail_keys[:, cols]], 0)
         values = jnp.concatenate(values + [tail_values[:, cols]], 0)
         scores = jnp.where(seen, transpose_dot(q, keys) * SCALE, NEG)
@@ -106,7 +106,8 @@
     x, z, core = place_ref[0], place_ref[1], place_ref[2]
     own = x * (NZ * NC) + z * NC
     blocks = [own + core, own + 1 - core] + arrived(place_ref, core)
-    held = (unit_ref, swapped_ref, near_ref)
+    held = [(unit_ref, 0), (swapped_ref, 0)]
+    held += [(near_ref, at) for at in range(0, GATHERED, UNIT)]
     found = question_part(place_ref, fill_ref, asked_ref, others_ref, held, blocks)
     for kv, (scores, peak, values) in enumerate(found):
         peak = rounded(peak)
@@ -121,7 +122,8 @@
 ):
     x, core = place_ref[0], place_ref[2]
     blocks = arrived(place_ref, 1 - core)
-    found = question_part(place_ref, fill_ref, asked_ref, others_ref, (far_ref,), blocks)
+    held = [(far_ref, at) for at in range(0, GATHERED, UNIT)]
+    found = question_part(place_ref, fill_ref, asked_ref, others_ref, held, blocks)
     shape = (NX * QTOK, GROUPS, HEAD)
     outs, peaks, sums = [], [], []
     for kv, (scores, peak, values) in enumerate(found):
@@ -163,10 +165,11 @@
 
 
 def block_kernel(
-    place_ref, fill_ref, query_ref, unit_ref, anchor_ref, out_ref
+    place_ref, fill_ref, query_ref, unit_ref, near_ref, far_ref, out_ref
 ):
     x, z, core = place_ref[0], place_ref[1], place_ref[2]
     device = x * (NZ * NC) + z * NC + core
+    received = (z < NZ // 2) == (core == 0)
     row = lax.broadcasted_iota(jnp.int32, (BLOCK, 2 * BLOCK), 0)
     col = lax.broadcasted_iota(jnp.int32, (BLOCK, 2 * BLOCK), 1)
     own = col - BLOCK
@@ -177,10 +180,10 @@
     keep = lax.broadcasted_iota(jnp.int32, (BLOCK, 1), 0) < own_fill
     for kv in range(KVS):
         cols = slice(kv * HEAD, (kv + 1) * HEAD)
-        keys = jnp.concatenate([anchor_ref[0:BLOCK, cols], unit_ref[0:BLOCK, cols]], 0)
-        values = jnp.concatenate(
-            [anchor_ref[BLOCK : 2 * BLOCK, cols], unit_ref[BLOCK : 2 * BLOCK, cols]], 0
-        )
+        anchor_rows = slice(GATHERED, GATHERED + 2 * BLOCK)
+        anchor = jnp.where(received, near_ref[anchor_rows, cols], far_ref[anchor_rows, cols])
+        keys = jnp.concatenate([anchor[0:BLOCK], unit_ref[0:BLOCK, cols]], 0)
+        values = jnp.concatenate([anchor[BLOCK : 2 * BLOCK], unit_ref[BLOCK : 2 * BLOCK, cols]], 0)
         heads = range(kv * GROUPS, (kv + 1) * GROUPS)
         q = jnp.concatenate([query_ref[:, h * HEAD : (h + 1) * HEAD] for h in heads], 0)
         scores = transpose_dot(q, keys) * SCALE
@@ -215,31 +218,41 @@
     x, z, core = lax.axis_index("x"), lax.axis_index("z"), lax.axis_index("core")
     place = jnp.stack([x, z, core]).astype(jnp.int32)
 
-    gap = jnp.zeros((8 - QTOK, KVS * HEAD), bf16)
-    unit = jnp.concatenate([block_key, block_value, question_key, gap, question_value, gap], 0)
+    placed = (
+        (block_key, 0),
+        (block_value, BLOCK),
+        (question_key, 2 * BLOCK),
+        (question_value, 2 * BLOCK + 8),
+    )
+    unit = sum(jnp.pad(v, ((at, UNIT - at - v.shape[0]), (0, 0))) for v, at in placed)
     swapped = lax.ppermute(unit, "core", SWAP)
     pair = jnp.stack([unit, swapped])
+    pair, question_query = lax.optimization_barrier((pair, question_query))
+    asked = question_query.reshape(QTOK, HEADS, HEAD)
     step1 = moved(pair, 1)
     step2 = moved(pair, 2)
-    asked = question_query.reshape(QTOK, HEADS, HEAD)
-    others = [flipped(asked, f) for f in X_FLIPS[1:]]
-    step2, *others = lax.optimization_barrier((step2, *others))
-    others = jnp.stack(others)
+    first = jnp.where(core == 0, unit, swapped)[: 2 * BLOCK]
+    third = lax.ppermute(first, ("x", "z", "core"), [(0, 3 * NC), (1, 5 * NC + 1)])
+    fourth = lax.ppermute(first, ("x", "z", "core"), [(1, 4 * NC + 1)])
+
+    step1, step2, third, fourth = lax.optimization_barrier((step1, step2, third, fourth))
+    carried = jnp.where((z == 1) | (z == NZ - 1), jnp.where(core == 0, step1[0], step1[1]), unit)
+    carried = jnp.where((z == 2) | (z == NZ - 2), jnp.where(core == 0, step2[0], step2[1]), carried)
+    carried = carried[: 2 * BLOCK]
+    carried = jnp.where((z == 3) | (z == 5), third, jnp.where(z == 4, fourth, carried))
+    sent = jnp.concatenate([carried[:, :HEAD], carried[:, HEAD:], asked.reshape(-1, HEAD)], 0)
     step3 = moved(step2, 1)
     step4 = moved(step2[0], 2)
-    near = jnp.concatenate([step1, step2, step3, step4[None]])
+    came = [flipped(sent, f) for f in X_FLIPS[1:]]
+    step3, step4, *came = lax.optimization_barrier((step3, step4, *came))
+    near = jnp.concatenate([step1, step2, step3, step4[None]]).reshape(GATHERED, KVS * HEAD)
+    others = jnp.stack([c[4 * BLOCK :] for c in came]).reshape(-1, HEADS, HEAD)
+    anchor = sent
+    for flip, c in zip(X_FLIPS[1:], came):
+        anchor = jnp.where(x == flip, c, anchor)
+    anchor = jnp.concatenate([anchor[: 2 * BLOCK], anchor[2 * BLOCK : 4 * BLOCK]], 1)
+    near = jnp.concatenate([near, anchor], 0)
     far = lax.ppermute(near, "core", SWAP)
-
-    rising = lax.dynamic_index_in_dim(
-        jnp.where(core == 0, near, far), jnp.clip(2 * z - 2, 0, 6), 0, keepdims=False
-    )
-    falling = lax.dynamic_index_in_dim(
-        jnp.where(core == 0, far, near), jnp.clip(2 * (NZ - z) - 1, 0, 6), 0, keepdims=False
-    )
-    here = jnp.where(core == 0, unit, swapped)
-    first = jnp.where(z == 0, here, jnp.where(z <= NZ // 2, rising, falling))[: 2 * BLOCK]
-    sent = lax.ppermute(first, ("x", "core"), [(0, NC), (1, 2 * NC + 1)])
-    late = lax.ppermute(first, ("x", "core"), [(1, 3 * NC + 1)])
 
     question = functools.partial(pl.pallas_call, compiler_params=PARAMS)
     state = jax.ShapeDtypeStruct((KVS, ROWS, HEAD), f32)
@@ -260,21 +273,16 @@
         name="question_far",
     )(place, block_fill, asked, others, far, *carry)
 
-    parts, sent, late = lax.optimization_barrier((parts, sent, late))
-    got = jnp.where(x == NX - 1, late, sent)
-    passed = lax.ppermute(got, ("x", "core"), [(2, 3), (5, 4), (7, 6)])
-    receiver = jnp.where(x == 1, 0, 1)
-    anchor = jnp.where(x == 0, first, jnp.where(core == receiver, got, passed))
     parts = lax.all_to_all(parts, ("x", "tp"), 0, 0, tiled=True)
 
     block_output = pl.pallas_call(
         block_kernel,
         out_shape=jax.ShapeDtypeStruct(block_query.shape, bf16),
-        in_specs=[SMEM, SMEM] + [VMEM] * 3,
+        in_specs=[SMEM, SMEM] + [VMEM] * 4,
         out_specs=VMEM,
         compiler_params=PARAMS,
         name="block",
-    )(place, block_fill, block_query, unit, anchor)
+    )(place, block_fill, block_query, unit, near, far)
 
     question_output = pl.pallas_call(
         merge_kernel,

time: 52 us -> 46.3 us (0.89)
  the two profiles are of different devices: /device:TPU:1 before, /device:TPU:32 now
where the time goes in v3:
time: 46.3 us; the launch traced here: 46 us
  starting transfers between devices  25.6 us (55%)
  waiting for transfers between devices  12.3 us (27%)
  Pallas kernels  5.73 us (12%)
  other arithmetic  1.15 us (2%)
  between operations  0.87 us (2%)
    ppermute x4, starting transfers between devices, moved(): return lax.ppermute(array, ('z', 'core'), up + down)  12.2 us
    all_to_all x1, starting transfers between devices, per_device(): parts = lax.all_to_all(parts, ('x', 'tp'), 0, 0, tiled=True)  7.64 us
    all_to_all x1, waiting for transfers between devices, per_device(): parts = lax.all_to_all(parts, ('x', 'tp'), 0, 0, tiled=True)  5.87 us
    ppermute x4, waiting for transfers between devices, moved(): return lax.ppermute(array, ('z', 'core'), up + down)  4.79 us
    ppermute x3, starting transfers between devices, flipped(): return lax.ppermute(array, 'x', [(i, i ^ flip) for i in range(NX)])  4.25 us
    pallas_call x1, Pallas kernels, per_device(): pl.pallas_call(block_kernel, out_shape=jax.ShapeDtypeStruct(block_query.s...  1.96 us
    pallas_call x1, Pallas kernels, per_device(): question(far_kernel, out_shape=jax.ShapeDtypeStruct((NX * NT, 2 * HEADS,...  1.78 us
    ppermute x1, waiting for transfers between devices, per_device(): swapped = lax.ppermute(unit, 'core', SWAP)  1.24 us
  transfers between devices with their start and end apart: 12, of which 5 were waited for; matrix products, arithmetic and copies ran while one was open for 0% of the time, Pallas kernels for 7%

profile of v3, /device:TPU:32, one launch (start us, length us, event | category | flops | bytes accessed | tf_op | source)
XLA Modules:
  0.0 46.0 jit_solution(9412472507773316344)
XLA Ops:
  0.6 0.0 copy-start.2
  0.6 0.8 %fusion.3 = (bf16[1,144,256]{2,1,0:T(8,128)(2,1)S(1)}, bf16[144,256]{1,0:T(8,128)(2,1)S(1)}) fusion(bf16[4,256]{1,0:T(4,128)(2,1)} %param.12, bf16[4,256]{1,0:T(4,128)(2,1)} %param.11, bf16[64,256]{1,0:T(8,128)(2,1)} %param.9, bf16[64,256]{1,0:T(8,128)(2,1)} %param.8), kind=kLoop, calls=%fused_computation.21 | loop fusion | flops 294912 | bytes 217088 | tf_op jit(solution)/shard_map/stack | solution.py:229
  1.5 0.1 collective-permute-start
  1.6 1.2 %collective-permute-done.swapped_ref = bf16[144,256]{1,0:T(8,128)(2,1)S(1)} collective-permute-done((bf16[144,256]{1,0:T(8,128)(2,1)S(1)}, bf16[144,256]{1,0:T(8,128)(2,1)S(1)}, u32[]{:S(2)}, u32[]{:S(2)}) %collective-permute-start) | collective-permute-done | bytes 73760 | tf_op jit(solution)/shard_map/ppermute | solution.py:228
  2.8 2.0 %collective-permute-start.1 = (bf16[2,144,256]{2,1,0:T(8,128)(2,1)S(1)}, bf16[2,144,256]{2,1,0:T(8,128)(2,1)S(1)}, u32[]{:S(2)}, u32[]{:S(2)}) collective-permute-start(bf16[2,144,256]{2,1,0:T(8,128)(2,1)S(1)} %pad_maximum_fusion.1), channel_id=1, source_target_pairs={{0,8},{8,16},{16,24},{24,32},{32,40},{40,48},{48,56},{56,0},{4,60}... | collective-permute-start | bytes 442376 | tf_op jit(solution)/shard_map/ppermute | solution.py:211
  4.8 4.5 %collective-permute-start.2 = (bf16[2,144,256]{2,1,0:T(8,128)(2,1)S(1)}, bf16[2,144,256]{2,1,0:T(8,128)(2,1)S(1)}, u32[]{:S(2)}, u32[]{:S(2)}) collective-permute-start(bf16[2,144,256]{2,1,0:T(8,128)(2,1)S(1)} %pad_maximum_fusion.1), channel_id=1, source_target_pairs={{0,16},{8,24},{16,32},{24,40},{32,48},{40,56},{48,0},{56,8},{4,52}... | collective-permute-start | bytes 442376 | tf_op jit(solution)/shard_map/ppermute | solution.py:211
  9.3 0.7 %collective-permute-start.3 = (bf16[128,256]{1,0:T(8,128)(2,1)S(1)}, bf16[128,256]{1,0:T(8,128)(2,1)S(1)}, u32[]{:S(2)}, u32[]{:S(2)}) collective-permute-start(bf16[128,256]{1,0:T(8,128)(2,1)S(1)} %slice_select_fusion.2), channel_id=1, source_target_pairs={{0,24},{4,44},{1,25},{5,45},{2,26},{6,46},{3,27},{7,47}} | collective-permute-start | bytes 196616 | tf_op jit(solution)/shard_map/ppermute | solution.py:235
  10.0 0.7 %collective-permute-start.4 = (bf16[128,256]{1,0:T(8,128)(2,1)S(1)}, bf16[128,256]{1,0:T(8,128)(2,1)S(1)}, u32[]{:S(2)}, u32[]{:S(2)}) collective-permute-start(bf16[128,256]{1,0:T(8,128)(2,1)S(1)} %slice_select_fusion.2), channel_id=1, source_target_pairs={{4,36},{5,37},{6,38},{7,39}} | collective-permute-start | bytes 196616 | tf_op jit(solution)/shard_map/ppermute | solution.py:236
  10.7 0.0 copy-done.2
  10.7 0.0 collective-permute-done.3
  10.7 0.0 collective-permute-done.4
  10.8 0.0 collective-permute-done.1
  10.8 2.8 %collective-permute-done.2 = bf16[2,144,256]{2,1,0:T(8,128)(2,1)S(1)} collective-permute-done((bf16[2,144,256]{2,1,0:T(8,128)(2,1)S(1)}, bf16[2,144,256]{2,1,0:T(8,128)(2,1)S(1)}, u32[]{:S(2)}, u32[]{:S(2)}) %collective-permute-start.2) | collective-permute-done | bytes 147488 | tf_op jit(solution)/shard_map/ppermute | solution.py:211
  13.6 1.1 %collective-permute-start.5 = (bf16[2,144,256]{2,1,0:T(8,128)(2,1)S(1)}, bf16[2,144,256]{2,1,0:T(8,128)(2,1)S(1)}, u32[]{:S(2)}, u32[]{:S(2)}) collective-permute-start(bf16[2,144,256]{2,1,0:T(8,128)(2,1)S(1)} %collective-permute-done.2), channel_id=1, source_target_pairs={{0,8},{8,16},{16,24},{24,32},{32,40},{40,48},{48,56},{56,0},{4,60}... | collective-permute-start | bytes 442376 | tf_op jit(solution)/shard_map/ppermute | solution.py:211
  14.8 3.1 %collective-permute-start.7 = (bf16[320,128]{1,0:T(8,128)(2,1)S(1)}, bf16[320,128]{1,0:T(8,128)(2,1)S(1)}, u32[]{:S(2)}, u32[]{:S(2)}) collective-permute-start(bf16[320,128]{1,0:T(8,128)(2,1)S(1)} %pad_maximum_fusion.2), channel_id=1, source_target_pairs={{0,128},{64,192},{128,0},{192,64},{1,129},{65,193},{129,1},{193,65... | collective-permute-start | bytes 245768 | tf_op jit(solution)/shard_map/ppermute | solution.py:205
  17.9 0.6 %collective-permute-start.8 = (bf16[320,128]{1,0:T(8,128)(2,1)S(1)}, bf16[320,128]{1,0:T(8,128)(2,1)S(1)}, u32[]{:S(2)}, u32[]{:S(2)}) collective-permute-start(bf16[320,128]{1,0:T(8,128)(2,1)S(1)} %pad_maximum_fusion.2), channel_id=1, source_target_pairs={{0,64},{64,0},{128,192},{192,128},{1,65},{65,1},{129,193},{193,129... | collective-permute-start | bytes 245768 | tf_op jit(solution)/shard_map/ppermute | solution.py:205
  18.5 0.6 %collective-permute-start.9 = (bf16[320,128]{1,0:T(8,128)(2,1)S(1)}, bf16[320,128]{1,0:T(8,128)(2,1)S(1)}, u32[]{:S(2)}, u32[]{:S(2)}) collective-permute-start(bf16[320,128]{1,0:T(8,128)(2,1)S(1)} %pad_maximum_fusion.2), channel_id=1, source_target_pairs={{0,192},{64,128},{128,64},{192,0},{1,193},{65,129},{129,65},{193,1... | collective-permute-start | bytes 245768 | tf_op jit(solution)/shard_map/ppermute | solution.py:205
  19.0 4.6 %collective-permute-start.6 = (bf16[144,256]{1,0:T(8,128)(2,1)S(1)}, bf16[144,256]{1,0:T(8,128)(2,1)S(1)}, u32[]{:S(2)}, u32[]{:S(2)}) collective-permute-start(bf16[144,256]{1,0:T(8,128)(2,1)S(1)} %get-tuple-element.31), channel_id=1, source_target_pairs={{0,16},{8,24},{16,32},{24,40},{32,48},{40,56},{48,0},{56,8},{4,52}... | collective-permute-start | bytes 221192 | tf_op jit(solution)/shard_map/ppermute | solution.py:211
  23.6 2.0 %collective-permute-done.6 = bf16[144,256]{1,0:T(8,128)(2,1)S(1)} collective-permute-done((bf16[144,256]{1,0:T(8,128)(2,1)S(1)}, bf16[144,256]{1,0:T(8,128)(2,1)S(1)}, u32[]{:S(2)}, u32[]{:S(2)}) %collective-permute-start.6) | collective-permute-done | bytes 73760 | tf_op jit(solution)/shard_map/ppermute | solution.py:211
  25.6 0.0 collective-permute-done.7
  25.6 0.0 collective-permute-done.8
  25.6 0.0 collective-permute-done.9
  25.6 0.0 collective-permute-done.5
  25.7 0.1 pad_maximum_fusion
  25.8 0.0 copy-start.1
  25.8 0.1 collective-permute-start.10
  25.9 0.1 pad_add_fusion.1.place_ref
  26.0 0.4 copy-done.1
  26.4 1.1 %question_near.1 = (f32[2,128,128]{2,1,0:T(8,128)S(1)}, f32[2,128,128]{2,1,0:T(8,128)S(1)}, f32[2,128,128]{2,1,0:T(8,128)S(1)}) custom-call(s32[3]{0:T(128)S(1)} %pad_add_fusion.1.place_ref, s32[64]{0:T(128)S(1)} %copy-done.1, bf16[4,16,128]{2,1,0:T(8,128)(2,1)S(1)} %bitcast.28, bf16[12,16,128]{2,1,0:T(8,128)(2,1)S(1)} %bitcast.26, ...), custom_call_target="tpu_custom_call" | custom-call | flops 100000000 | bytes 1000000 | tf_op jit(solution)/shard_map/question_near/pallas_call | solution.py:259
  27.6 0.3 collective-permute-done.10.far_ref
  27.9 0.0 copy-start
  27.9 1.8 %question_far.1 = bf16[16,32,128]{2,1,0:T(8,128)(2,1)} custom-call(s32[3]{0:T(128)S(1)} %pad_add_fusion.1.place_ref, s32[64]{0:T(128)S(1)} %copy-done.1, bf16[4,16,128]{2,1,0:T(8,128)(2,1)S(1)} %bitcast.29, bf16[12,16,128]{2,1,0:T(8,128)(2,1)S(1)} %bitcast.27, bf16[1136,256]{1,0:T(8,128)(2,1)S(1)} %collective-permute-done.10.far_ref, ...), custom_call_target="tpu_custom_call" | custom-call | flops 100000000 | bytes 1000000 | tf_op jit(solution)/shard_map/question_far/pallas_call | solution.py:267
  29.7 7.6 %all-to-all-start = ((bf16[16,32,128]{2,1,0:T(8,128)(2,1)}), bf16[16,32,128]{2,1,0:T(8,128)(2,1)S(1)}, u32[]{:S(2)}, u32[]{:S(2)}) async-start(bf16[16,32,128]{2,1,0:T(8,128)(2,1)} %question_far.1), calls=%async_computation | async-start | bytes 262144 | tf_op jit(solution)/shard_map/all_to_all | solution.py:276
  37.3 0.0 copy-done
  37.3 2.0 %block.1 = bf16[64,2048]{1,0:T(8,128)(2,1)} custom-call(s32[3]{0:T(128)S(1)} %pad_add_fusion.1.place_ref, s32[64]{0:T(128)S(1)} %copy-done.1, bf16[64,2048]{1,0:T(8,128)(2,1)S(1)} %copy-done, bf16[144,256]{1,0:T(8,128)(2,1)S(1)} %get-tuple-element.35.unit_ref, bf16[1136,256]{1,0:T(8,128)(2,1)S(1)} %maximum_maximum_fusion.near_ref, ...), custom_call_target="tpu_custom_call" | custom-call | tf_op jit(solution)/shard_map/block/pallas_call | solution.py:278
  39.3 5.9 %all-to-all-done.parts_ref = bf16[16,32,128]{2,1,0:T(8,128)(2,1)S(1)} async-done(((bf16[16,32,128]{2,1,0:T(8,128)(2,1)}), bf16[16,32,128]{2,1,0:T(8,128)(2,1)S(1)}, u32[]{:S(2)}, u32[]{:S(2)}) %all-to-all-start) | async-done | bytes 131104 | tf_op jit(solution)/shard_map/all_to_all | solution.py:276
  45.2 0.9 %merge.1 = bf16[1,8192]{1,0:T(2,128)(2,1)} custom-call(bf16[16,32,128]{2,1,0:T(8,128)(2,1)S(1)} %all-to-all-done.parts_ref), custom_call_target="tpu_custom_call" | custom-call | tf_op jit(solution)/shard_map/merge/pallas_call | solution.py:287
  (15 shorter events, 0.2 us)
Async XLA Ops:
  0.6 10.1 %copy-start.2 = (bf16[4,2048]{1,0:T(4,128)(2,1)S(1)}, bf16[4,2048]{1,0:T(4,128)(2,1)}, u32[]{:S(2)}) copy-start(bf16[4,2048]{1,0:T(4,128)(2,1)} %param.10) | copy-start | bytes 49156
  1.5 1.4 %collective-permute-start = (bf16[144,256]{1,0:T(8,128)(2,1)S(1)}, bf16[144,256]{1,0:T(8,128)(2,1)S(1)}, u32[]{:S(2)}, u32[]{:S(2)}) collective-permute-start(bf16[144,256]{1,0:T(8,128)(2,1)S(1)} %get-tuple-element.35.unit_ref), channel_id=1, source_target_pairs={{0,4},{4,0},{1,5},{5,1},{2,6},{6,2},{3,7},{7,3},{8,12},{12,8},{9,1... | collective-permute-start | bytes 221192 | tf_op jit(solution)/shard_map/ppermute | solution.py:228
  2.8 7.9 %collective-permute-start.1 = (bf16[2,144,256]{2,1,0:T(8,128)(2,1)S(1)}, bf16[2,144,256]{2,1,0:T(8,128)(2,1)S(1)}, u32[]{:S(2)}, u32[]{:S(2)}) collective-permute-start(bf16[2,144,256]{2,1,0:T(8,128)(2,1)S(1)} %pad_maximum_fusion.1), channel_id=1, source_target_pairs={{0,8},{8,16},{16,24},{24,32},{32,40},{40,48},{48,56},{56,0},{4,60}... | collective-permute-start | bytes 442376 | tf_op jit(solution)/shard_map/ppermute | solution.py:211
  4.8 8.7 %collective-permute-start.2 = (bf16[2,144,256]{2,1,0:T(8,128)(2,1)S(1)}, bf16[2,144,256]{2,1,0:T(8,128)(2,1)S(1)}, u32[]{:S(2)}, u32[]{:S(2)}) collective-permute-start(bf16[2,144,256]{2,1,0:T(8,128)(2,1)S(1)} %pad_maximum_fusion.1), channel_id=1, source_target_pairs={{0,16},{8,24},{16,32},{24,40},{32,48},{40,56},{48,0},{56,8},{4,52}... | collective-permute-start | bytes 442376 | tf_op jit(solution)/shard_map/ppermute | solution.py:211
  9.3 1.4 %collective-permute-start.3 = (bf16[128,256]{1,0:T(8,128)(2,1)S(1)}, bf16[128,256]{1,0:T(8,128)(2,1)S(1)}, u32[]{:S(2)}, u32[]{:S(2)}) collective-permute-start(bf16[128,256]{1,0:T(8,128)(2,1)S(1)} %slice_select_fusion.2), channel_id=1, source_target_pairs={{0,24},{4,44},{1,25},{5,45},{2,26},{6,46},{3,27},{7,47}} | collective-permute-start | bytes 196616 | tf_op jit(solution)/shard_map/ppermute | solution.py:235
  10.0 0.7 %collective-permute-start.4 = (bf16[128,256]{1,0:T(8,128)(2,1)S(1)}, bf16[128,256]{1,0:T(8,128)(2,1)S(1)}, u32[]{:S(2)}, u32[]{:S(2)}) collective-permute-start(bf16[128,256]{1,0:T(8,128)(2,1)S(1)} %slice_select_fusion.2), channel_id=1, source_target_pairs={{4,36},{5,37},{6,38},{7,39}} | collective-permute-start | bytes 196616 | tf_op jit(solution)/shard_map/ppermute | solution.py:236
  13.6 12.0 %collective-permute-start.5 = (bf16[2,144,256]{2,1,0:T(8,128)(2,1)S(1)}, bf16[2,144,256]{2,1,0:T(8,128)(2,1)S(1)}, u32[]{:S(2)}, u32[]{:S(2)}) collective-permute-start(bf16[2,144,256]{2,1,0:T(8,128)(2,1)S(1)} %collective-permute-done.2), channel_id=1, source_target_pairs={{0,8},{8,16},{16,24},{24,32},{32,40},{40,48},{48,56},{56,0},{4,60}... | collective-permute-start | bytes 442376 | tf_op jit(solution)/shard_map/ppermute | solution.py:211
  14.8 10.8 %collective-permute-start.7 = (bf16[320,128]{1,0:T(8,128)(2,1)S(1)}, bf16[320,128]{1,0:T(8,128)(2,1)S(1)}, u32[]{:S(2)}, u32[]{:S(2)}) collective-permute-start(bf16[320,128]{1,0:T(8,128)(2,1)S(1)} %pad_maximum_fusion.2), channel_id=1, source_target_pairs={{0,128},{64,192},{128,0},{192,64},{1,129},{65,193},{129,1},{193,65... | collective-permute-start | bytes 245768 | tf_op jit(solution)/shard_map/ppermute | solution.py:205
  17.9 7.7 %collective-permute-start.8 = (bf16[320,128]{1,0:T(8,128)(2,1)S(1)}, bf16[320,128]{1,0:T(8,128)(2,1)S(1)}, u32[]{:S(2)}, u32[]{:S(2)}) collective-permute-start(bf16[320,128]{1,0:T(8,128)(2,1)S(1)} %pad_maximum_fusion.2), channel_id=1, source_target_pairs={{0,64},{64,0},{128,192},{192,128},{1,65},{65,1},{129,193},{193,129... | collective-permute-start | bytes 245768 | tf_op jit(solution)/shard_map/ppermute | solution.py:205
  18.5 7.1 %collective-permute-start.9 = (bf16[320,128]{1,0:T(8,128)(2,1)S(1)}, bf16[320,128]{1,0:T(8,128)(2,1)S(1)}, u32[]{:S(2)}, u32[]{:S(2)}) collective-permute-start(bf16[320,128]{1,0:T(8,128)(2,1)S(1)} %pad_maximum_fusion.2), channel_id=1, source_target_pairs={{0,192},{64,128},{128,64},{192,0},{1,193},{65,129},{129,65},{193,1... | collective-permute-start | bytes 245768 | tf_op jit(solution)/shard_map/ppermute | solution.py:205
  19.0 6.6 %collective-permute-start.6 = (bf16[144,256]{1,0:T(8,128)(2,1)S(1)}, bf16[144,256]{1,0:T(8,128)(2,1)S(1)}, u32[]{:S(2)}, u32[]{:S(2)}) collective-permute-start(bf16[144,256]{1,0:T(8,128)(2,1)S(1)} %get-tuple-element.31), channel_id=1, source_target_pairs={{0,16},{8,24},{16,32},{24,40},{32,48},{40,56},{48,0},{56,8},{4,52}... | collective-permute-start | bytes 221192 | tf_op jit(solution)/shard_map/ppermute | solution.py:211
  25.8 0.7 %copy-start.1 = (s32[64]{0:T(128)S(1)}, s32[64]{0:T(128)}, u32[]{:S(2)}) copy-start(s32[64]{0:T(128)} %fill_ref.5) | copy-start | bytes 772
  25.8 2.1 %collective-permute-start.10 = (bf16[1136,256]{1,0:T(8,128)(2,1)S(1)}, bf16[1136,256]{1,0:T(8,128)(2,1)S(1)}, u32[]{:S(2)}, u32[]{:S(2)}) collective-permute-start(bf16[1136,256]{1,0:T(8,128)(2,1)S(1)} %maximum_maximum_fusion.near_ref), channel_id=1, source_target_pairs={{0,4},{4,0},{1,5},{5,1},{2,6},{6,2},{3,7},{7,3},{8,12},{12,8},{9,1... | collective-permute-start | bytes 1744904 | tf_op jit(solution)/shard_map/ppermute | solution.py:255
  27.9 9.4 %copy-start = (bf16[64,2048]{1,0:T(8,128)(2,1)S(1)}, bf16[64,2048]{1,0:T(8,128)(2,1)}, u32[]{:S(2)}) copy-start(bf16[64,2048]{1,0:T(8,128)(2,1)} %query_ref.1) | copy-start | bytes 786436
  29.7 15.5 %all-to-all-start = ((bf16[16,32,128]{2,1,0:T(8,128)(2,1)}), bf16[16,32,128]{2,1,0:T(8,128)(2,1)S(1)}, u32[]{:S(2)}, u32[]{:S(2)}) async-start(bf16[16,32,128]{2,1,0:T(8,128)(2,1)} %question_far.1), calls=%async_computation | async-start | bytes 262144 | tf_op jit(solution)/shard_map/all_to_all | solution.py:276

commit v4 on v3

--- a/solution.py
+++ b/solution.py
@@ -230,22 +230,23 @@
     pair, question_query = lax.optimization_barrier((pair, question_query))
     asked = question_query.reshape(QTOK, HEADS, HEAD)
     step1 = moved(pair, 1)
-    step2 = moved(pair, 2)
+    step2 = moved(unit, 2)
     first = jnp.where(core == 0, unit, swapped)[: 2 * BLOCK]
     third = lax.ppermute(first, ("x", "z", "core"), [(0, 3 * NC), (1, 5 * NC + 1)])
-    fourth = lax.ppermute(first, ("x", "z", "core"), [(1, 4 * NC + 1)])
-
-    step1, step2, third, fourth = lax.optimization_barrier((step1, step2, third, fourth))
+    fourth = lax.ppermute(first, ("x", "z", "core"), [(1, 4 * NC + 1), (0, 6 * NC + 1)])
+
+    step1, step2 = lax.optimization_barrier((step1, step2))
     carried = jnp.where((z == 1) | (z == NZ - 1), jnp.where(core == 0, step1[0], step1[1]), unit)
-    carried = jnp.where((z == 2) | (z == NZ - 2), jnp.where(core == 0, step2[0], step2[1]), carried)
+    carried = jnp.where(z == 2, step2, carried)
     carried = carried[: 2 * BLOCK]
-    carried = jnp.where((z == 3) | (z == 5), third, jnp.where(z == 4, fourth, carried))
+    carried = jnp.where((z == 3) | (z == 5), third, jnp.where((z == 4) | (z == 6), fourth, carried))
     sent = jnp.concatenate([carried[:, :HEAD], carried[:, HEAD:], asked.reshape(-1, HEAD)], 0)
-    step3 = moved(step2, 1)
-    step4 = moved(step2[0], 2)
+    onward = jnp.stack([step1[1], step2])
+    step3 = moved(onward, 1)
+    step4 = moved(onward, 2)
     came = [flipped(sent, f) for f in X_FLIPS[1:]]
     step3, step4, *came = lax.optimization_barrier((step3, step4, *came))
-    near = jnp.concatenate([step1, step2, step3, step4[None]]).reshape(GATHERED, KVS * HEAD)
+    near = jnp.concatenate([step1, step2[None], step3, step4]).reshape(GATHERED, KVS * HEAD)
     others = jnp.stack([c[4 * BLOCK :] for c in came]).reshape(-1, HEADS, HEAD)
     anchor = sent
     for flip, c in zip(X_FLIPS[1:], came):

time: 46.3 us -> 43.8 us (0.946)
  starting transfers between devices: 25.6 us -> 22.7 us
    ppermute x3, waiting for transfers between devices: 0.01 us -> 5.1 us  [flipped(): return lax.ppermute(array, 'x', [(i, i ^ flip) for i in range(NX)])]
    ppermute x4, waiting for transfers between devices: 4.79 us -> 1.42 us  [moved(): return lax.ppermute(array, ('z', 'core'), up + down)]
    all_to_all x1, starting transfers between devices: 7.64 us -> 4.81 us  [per_device(): parts = lax.all_to_all(parts, ('x', 'tp'), 0, 0, tiled=True)]
    ppermute x1, waiting for transfers between devices: 1.24 us -> 0.01 us  [per_device(): swapped = lax.ppermute(unit, 'core', SWAP)]
  transfers between devices with their start and end apart: 12 -> 12, of which waited for: 5 -> 7; matrix products, arithmetic and copies ran while one was open for 0% -> 0% of each run, Pallas kernels for 7% -> 7%
where the time goes in v4:
time: 43.8 us; the launch traced here: 43.6 us
  starting transfers between devices  22.7 us (52%)
  waiting for transfers between devices  12.7 us (29%)
  Pallas kernels  5.73 us (13%)
  other arithmetic  1.16 us (3%)
  between operations  0.81 us (2%)
    ppermute x4, starting transfers between devices, moved(): return lax.ppermute(array, ('z', 'core'), up + down)  12.1 us
    all_to_all x1, waiting for transfers between devices, per_device(): parts = lax.all_to_all(parts, ('x', 'tp'), 0, 0, tiled=True)  5.87 us
    ppermute x3, waiting for transfers between devices, flipped(): return lax.ppermute(array, 'x', [(i, i ^ flip) for i in range(NX)])  5.1 us
    all_to_all x1, starting transfers between devices, per_device(): parts = lax.all_to_all(parts, ('x', 'tp'), 0, 0, tiled=True)  4.81 us
    ppermute x3, starting transfers between devices, flipped(): return lax.ppermute(array, 'x', [(i, i ^ flip) for i in range(NX)])  4.25 us
    pallas_call x1, Pallas kernels, per_device(): pl.pallas_call(block_kernel, out_shape=jax.ShapeDtypeStruct(block_query.s...  1.96 us
    pallas_call x1, Pallas kernels, per_device(): question(far_kernel, out_shape=jax.ShapeDtypeStruct((NX * NT, 2 * HEADS,...  1.78 us
    ppermute x4, waiting for transfers between devices, moved(): return lax.ppermute(array, ('z', 'core'), up + down)  1.42 us
  transfers between devices with their start and end apart: 12, of which 7 were waited for; matrix products, arithmetic and copies ran while one was open for 0% of the time, Pallas kernels for 7%

profile of v4, /device:TPU:32, one launch (start us, length us, event | category | flops | bytes accessed | tf_op | source)
XLA Modules:
  0.0 43.6 jit_solution(17463118453877329124)
XLA Ops:
  0.6 0.0 copy-start.2
  0.6 0.8 %fusion.2 = (bf16[1,144,256]{2,1,0:T(8,128)(2,1)S(1)}, bf16[144,256]{1,0:T(8,128)(2,1)S(1)}) fusion(bf16[4,256]{1,0:T(4,128)(2,1)} %param.12, bf16[4,256]{1,0:T(4,128)(2,1)} %param.11, bf16[64,256]{1,0:T(8,128)(2,1)} %param.9, bf16[64,256]{1,0:T(8,128)(2,1)} %param.8), kind=kLoop, calls=%fused_computation.19 | loop fusion | flops 294912 | bytes 217088 | tf_op jit(solution)/shard_map/stack | solution.py:229
  1.5 0.1 collective-permute-start
  1.6 3.3 %collective-permute-start.2 = (bf16[144,256]{1,0:T(8,128)(2,1)S(1)}, bf16[144,256]{1,0:T(8,128)(2,1)S(1)}, u32[]{:S(2)}, u32[]{:S(2)}) collective-permute-start(bf16[144,256]{1,0:T(8,128)(2,1)S(1)} %get-tuple-element.31.unit_ref), channel_id=1, source_target_pairs={{0,16},{8,24},{16,32},{24,40},{32,48},{40,56},{48,0},{56,8},{4,52}... | collective-permute-start | bytes 221192 | tf_op jit(solution)/shard_map/ppermute | solution.py:211
  4.9 0.0 collective-permute-done.swapped_ref
  4.9 3.2 %collective-permute-start.1 = (bf16[2,144,256]{2,1,0:T(8,128)(2,1)S(1)}, bf16[2,144,256]{2,1,0:T(8,128)(2,1)S(1)}, u32[]{:S(2)}, u32[]{:S(2)}) collective-permute-start(bf16[2,144,256]{2,1,0:T(8,128)(2,1)S(1)} %pad_maximum_fusion.1), channel_id=1, source_target_pairs={{0,8},{8,16},{16,24},{24,32},{32,40},{40,48},{48,56},{56,0},{4,60}... | collective-permute-start | bytes 442376 | tf_op jit(solution)/shard_map/ppermute | solution.py:211
  8.2 0.7 %collective-permute-start.5 = (bf16[128,256]{1,0:T(8,128)(2,1)S(1)}, bf16[128,256]{1,0:T(8,128)(2,1)S(1)}, u32[]{:S(2)}, u32[]{:S(2)}) collective-permute-start(bf16[128,256]{1,0:T(8,128)(2,1)S(1)} %slice_select_fusion.2), channel_id=1, source_target_pairs={{0,24},{4,44},{1,25},{5,45},{2,26},{6,46},{3,27},{7,47}} | collective-permute-start | bytes 196616 | tf_op jit(solution)/shard_map/ppermute | solution.py:235
  8.8 0.7 %collective-permute-start.6 = (bf16[128,256]{1,0:T(8,128)(2,1)S(1)}, bf16[128,256]{1,0:T(8,128)(2,1)S(1)}, u32[]{:S(2)}, u32[]{:S(2)}) collective-permute-start(bf16[128,256]{1,0:T(8,128)(2,1)S(1)} %slice_select_fusion.2), channel_id=1, source_target_pairs={{4,36},{0,52},{5,37},{1,53},{6,38},{2,54},{7,39},{3,55}} | collective-permute-start | bytes 196616 | tf_op jit(solution)/shard_map/ppermute | solution.py:236
  9.5 0.0 copy-done.2
  9.5 0.7 %collective-permute-done.2 = bf16[144,256]{1,0:T(8,128)(2,1)S(1)} collective-permute-done((bf16[144,256]{1,0:T(8,128)(2,1)S(1)}, bf16[144,256]{1,0:T(8,128)(2,1)S(1)}, u32[]{:S(2)}, u32[]{:S(2)}) %collective-permute-start.2) | collective-permute-done | bytes 73760 | tf_op jit(solution)/shard_map/ppermute | solution.py:211
  10.3 0.7 %collective-permute-done.1 = bf16[2,144,256]{2,1,0:T(8,128)(2,1)S(1)} collective-permute-done((bf16[2,144,256]{2,1,0:T(8,128)(2,1)S(1)}, bf16[2,144,256]{2,1,0:T(8,128)(2,1)S(1)}, u32[]{:S(2)}, u32[]{:S(2)}) %collective-permute-start.1) | collective-permute-done | bytes 147488 | tf_op jit(solution)/shard_map/ppermute | solution.py:211
  11.0 2.4 %collective-permute-start.3 = (bf16[2,144,256]{2,1,0:T(8,128)(2,1)S(1)}, bf16[2,144,256]{2,1,0:T(8,128)(2,1)S(1)}, u32[]{:S(2)}, u32[]{:S(2)}) collective-permute-start(bf16[2,144,256]{2,1,0:T(8,128)(2,1)S(1)} %pad_maximum_fusion.2), channel_id=1, source_target_pairs={{0,8},{8,16},{16,24},{24,32},{32,40},{40,48},{48,56},{56,0},{4,60}... | collective-permute-start | bytes 442376 | tf_op jit(solution)/shard_map/ppermute | solution.py:211
  13.4 3.1 %collective-permute-start.4 = (bf16[2,144,256]{2,1,0:T(8,128)(2,1)S(1)}, bf16[2,144,256]{2,1,0:T(8,128)(2,1)S(1)}, u32[]{:S(2)}, u32[]{:S(2)}) collective-permute-start(bf16[2,144,256]{2,1,0:T(8,128)(2,1)S(1)} %pad_maximum_fusion.2), channel_id=1, source_target_pairs={{0,16},{8,24},{16,32},{24,40},{32,48},{40,56},{48,0},{56,8},{4,52}... | collective-permute-start | bytes 442376 | tf_op jit(solution)/shard_map/ppermute | solution.py:211
  16.6 0.0 collective-permute-done.5
  16.6 0.0 collective-permute-done.6
  16.6 3.1 %collective-permute-start.7 = (bf16[320,128]{1,0:T(8,128)(2,1)S(1)}, bf16[320,128]{1,0:T(8,128)(2,1)S(1)}, u32[]{:S(2)}, u32[]{:S(2)}) collective-permute-start(bf16[320,128]{1,0:T(8,128)(2,1)S(1)} %pad_maximum_fusion.3), channel_id=1, source_target_pairs={{0,128},{64,192},{128,0},{192,64},{1,129},{65,193},{129,1},{193,65... | collective-permute-start | bytes 245768 | tf_op jit(solution)/shard_map/ppermute | solution.py:205
  19.7 0.6 %collective-permute-start.8 = (bf16[320,128]{1,0:T(8,128)(2,1)S(1)}, bf16[320,128]{1,0:T(8,128)(2,1)S(1)}, u32[]{:S(2)}, u32[]{:S(2)}) collective-permute-start(bf16[320,128]{1,0:T(8,128)(2,1)S(1)} %pad_maximum_fusion.3), channel_id=1, source_target_pairs={{0,64},{64,0},{128,192},{192,128},{1,65},{65,1},{129,193},{193,129... | collective-permute-start | bytes 245768 | tf_op jit(solution)/shard_map/ppermute | solution.py:205
  20.3 0.6 %collective-permute-start.9 = (bf16[320,128]{1,0:T(8,128)(2,1)S(1)}, bf16[320,128]{1,0:T(8,128)(2,1)S(1)}, u32[]{:S(2)}, u32[]{:S(2)}) collective-permute-start(bf16[320,128]{1,0:T(8,128)(2,1)S(1)} %pad_maximum_fusion.3), channel_id=1, source_target_pairs={{0,192},{64,128},{128,64},{192,0},{1,193},{65,129},{129,65},{193,1... | collective-permute-start | bytes 245768 | tf_op jit(solution)/shard_map/ppermute | solution.py:205
  20.9 1.9 %collective-permute-done.7 = bf16[320,128]{1,0:T(8,128)(2,1)S(1)} collective-permute-done((bf16[320,128]{1,0:T(8,128)(2,1)S(1)}, bf16[320,128]{1,0:T(8,128)(2,1)S(1)}, u32[]{:S(2)}, u32[]{:S(2)}) %collective-permute-start.7) | collective-permute-done | bytes 81952 | tf_op jit(solution)/shard_map/ppermute | solution.py:205
  22.8 1.4 %collective-permute-done.8 = bf16[320,128]{1,0:T(8,128)(2,1)S(1)} collective-permute-done((bf16[320,128]{1,0:T(8,128)(2,1)S(1)}, bf16[320,128]{1,0:T(8,128)(2,1)S(1)}, u32[]{:S(2)}, u32[]{:S(2)}) %collective-permute-start.8) | collective-permute-done | bytes 81952 | tf_op jit(solution)/shard_map/ppermute | solution.py:205
  24.2 1.8 %collective-permute-done.9 = bf16[320,128]{1,0:T(8,128)(2,1)S(1)} collective-permute-done((bf16[320,128]{1,0:T(8,128)(2,1)S(1)}, bf16[320,128]{1,0:T(8,128)(2,1)S(1)}, u32[]{:S(2)}, u32[]{:S(2)}) %collective-permute-start.9) | collective-permute-done | bytes 81952 | tf_op jit(solution)/shard_map/ppermute | solution.py:205
  26.0 0.0 collective-permute-done.3
  26.0 0.0 collective-permute-done.4
  26.0 0.1 pad_maximum_fusion
  26.1 0.0 copy-start.1
  26.2 0.1 collective-permute-start.10
  26.3 0.1 pad_add_fusion.1.place_ref
  26.4 0.4 copy-done.1
  26.8 1.1 %question_near.1 = (f32[2,128,128]{2,1,0:T(8,128)S(1)}, f32[2,128,128]{2,1,0:T(8,128)S(1)}, f32[2,128,128]{2,1,0:T(8,128)S(1)}) custom-call(s32[3]{0:T(128)S(1)} %pad_add_fusion.1.place_ref, s32[64]{0:T(128)S(1)} %copy-done.1, bf16[4,16,128]{2,1,0:T(8,128)(2,1)S(1)} %bitcast.24, bf16[12,16,128]{2,1,0:T(8,128)(2,1)S(1)} %bitcast.22, ...), custom_call_target="tpu_custom_call" | custom-call | flops 100000000 | bytes 1000000 | tf_op jit(solution)/shard_map/question_near/pallas_call | solution.py:260
  27.9 0.3 collective-permute-done.10.far_ref
  28.3 0.0 copy-start
  28.3 1.8 %question_far.1 = bf16[16,32,128]{2,1,0:T(8,128)(2,1)} custom-call(s32[3]{0:T(128)S(1)} %pad_add_fusion.1.place_ref, s32[64]{0:T(128)S(1)} %copy-done.1, bf16[4,16,128]{2,1,0:T(8,128)(2,1)S(1)} %bitcast.25, bf16[12,16,128]{2,1,0:T(8,128)(2,1)S(1)} %bitcast.23, bf16[1136,256]{1,0:T(8,128)(2,1)S(1)} %collective-permute-done.10.far_ref, ...), custom_call_target="tpu_custom_call" | custom-call | flops 100000000 | bytes 1000000 | tf_op jit(solution)/shard_map/question_far/pallas_call | solution.py:268
  30.0 4.8 %all-to-all-start = ((bf16[16,32,128]{2,1,0:T(8,128)(2,1)}), bf16[16,32,128]{2,1,0:T(8,128)(2,1)S(1)}, u32[]{:S(2)}, u32[]{:S(2)}) async-start(bf16[16,32,128]{2,1,0:T(8,128)(2,1)} %question_far.1), calls=%async_computation | async-start | bytes 262144 | tf_op jit(solution)/shard_map/all_to_all | solution.py:277
  34.9 0.0 copy-done
  34.9 2.0 %block.1 = bf16[64,2048]{1,0:T(8,128)(2,1)} custom-call(s32[3]{0:T(128)S(1)} %pad_add_fusion.1.place_ref, s32[64]{0:T(128)S(1)} %copy-done.1, bf16[64,2048]{1,0:T(8,128)(2,1)S(1)} %copy-done, bf16[144,256]{1,0:T(8,128)(2,1)S(1)} %get-tuple-element.31.unit_ref, bf16[1136,256]{1,0:T(8,128)(2,1)S(1)} %maximum_maximum_fusion.near_ref, ...), custom_call_target="tpu_custom_call" | custom-call | tf_op jit(solution)/shard_map/block/pallas_call | solution.py:279
  36.8 5.9 %all-to-all-done.parts_ref = bf16[16,32,128]{2,1,0:T(8,128)(2,1)S(1)} async-done(((bf16[16,32,128]{2,1,0:T(8,128)(2,1)}), bf16[16,32,128]{2,1,0:T(8,128)(2,1)S(1)}, u32[]{:S(2)}, u32[]{:S(2)}) %all-to-all-start) | async-done | bytes 131104 | tf_op jit(solution)/shard_map/all_to_all | solution.py:277
  42.7 0.9 %merge.1 = bf16[1,8192]{1,0:T(2,128)(2,1)} custom-call(bf16[16,32,128]{2,1,0:T(8,128)(2,1)S(1)} %all-to-all-done.parts_ref), custom_call_target="tpu_custom_call" | custom-call | tf_op jit(solution)/shard_map/merge/pallas_call | solution.py:288
  (15 shorter events, 0.2 us)
Async XLA Ops:
  0.6 8.9 %copy-start.2 = (bf16[4,2048]{1,0:T(4,128)(2,1)S(1)}, bf16[4,2048]{1,0:T(4,128)(2,1)}, u32[]{:S(2)}) copy-start(bf16[4,2048]{1,0:T(4,128)(2,1)} %param.10) | copy-start | bytes 49156
  1.5 3.5 %collective-permute-start = (bf16[144,256]{1,0:T(8,128)(2,1)S(1)}, bf16[144,256]{1,0:T(8,128)(2,1)S(1)}, u32[]{:S(2)}, u32[]{:S(2)}) collective-permute-start(bf16[144,256]{1,0:T(8,128)(2,1)S(1)} %get-tuple-element.31.unit_ref), channel_id=1, source_target_pairs={{0,4},{4,0},{1,5},{5,1},{2,6},{6,2},{3,7},{7,3},{8,12},{12,8},{9,1... | collective-permute-start | bytes 221192 | tf_op jit(solution)/shard_map/ppermute | solution.py:228
  1.6 8.7 %collective-permute-start.2 = (bf16[144,256]{1,0:T(8,128)(2,1)S(1)}, bf16[144,256]{1,0:T(8,128)(2,1)S(1)}, u32[]{:S(2)}, u32[]{:S(2)}) collective-permute-start(bf16[144,256]{1,0:T(8,128)(2,1)S(1)} %get-tuple-element.31.unit_ref), channel_id=1, source_target_pairs={{0,16},{8,24},{16,32},{24,40},{32,48},{40,56},{48,0},{56,8},{4,52}... | collective-permute-start | bytes 221192 | tf_op jit(solution)/shard_map/ppermute | solution.py:211
  4.9 6.0 %collective-permute-start.1 = (bf16[2,144,256]{2,1,0:T(8,128)(2,1)S(1)}, bf16[2,144,256]{2,1,0:T(8,128)(2,1)S(1)}, u32[]{:S(2)}, u32[]{:S(2)}) collective-permute-start(bf16[2,144,256]{2,1,0:T(8,128)(2,1)S(1)} %pad_maximum_fusion.1), channel_id=1, source_target_pairs={{0,8},{8,16},{16,24},{24,32},{32,40},{40,48},{48,56},{56,0},{4,60}... | collective-permute-start | bytes 442376 | tf_op jit(solution)/shard_map/ppermute | solution.py:211
  8.2 8.4 %collective-permute-start.5 = (bf16[128,256]{1,0:T(8,128)(2,1)S(1)}, bf16[128,256]{1,0:T(8,128)(2,1)S(1)}, u32[]{:S(2)}, u32[]{:S(2)}) collective-permute-start(bf16[128,256]{1,0:T(8,128)(2,1)S(1)} %slice_select_fusion.2), channel_id=1, source_target_pairs={{0,24},{4,44},{1,25},{5,45},{2,26},{6,46},{3,27},{7,47}} | collective-permute-start | bytes 196616 | tf_op jit(solution)/shard_map/ppermute | solution.py:235
  8.8 7.7 %collective-permute-start.6 = (bf16[128,256]{1,0:T(8,128)(2,1)S(1)}, bf16[128,256]{1,0:T(8,128)(2,1)S(1)}, u32[]{:S(2)}, u32[]{:S(2)}) collective-permute-start(bf16[128,256]{1,0:T(8,128)(2,1)S(1)} %slice_select_fusion.2), channel_id=1, source_target_pairs={{4,36},{0,52},{5,37},{1,53},{6,38},{2,54},{7,39},{3,55}} | collective-permute-start | bytes 196616 | tf_op jit(solution)/shard_map/ppermute | solution.py:236
  11.0 15.0 %collective-permute-start.3 = (bf16[2,144,256]{2,1,0:T(8,128)(2,1)S(1)}, bf16[2,144,256]{2,1,0:T(8,128)(2,1)S(1)}, u32[]{:S(2)}, u32[]{:S(2)}) collective-permute-start(bf16[2,144,256]{2,1,0:T(8,128)(2,1)S(1)} %pad_maximum_fusion.2), channel_id=1, source_target_pairs={{0,8},{8,16},{16,24},{24,32},{32,40},{40,48},{48,56},{56,0},{4,60}... | collective-permute-start | bytes 442376 | tf_op jit(solution)/shard_map/ppermute | solution.py:211
  13.4 12.6 %collective-permute-start.4 = (bf16[2,144,256]{2,1,0:T(8,128)(2,1)S(1)}, bf16[2,144,256]{2,1,0:T(8,128)(2,1)S(1)}, u32[]{:S(2)}, u32[]{:S(2)}) collective-permute-start(bf16[2,144,256]{2,1,0:T(8,128)(2,1)S(1)} %pad_maximum_fusion.2), channel_id=1, source_target_pairs={{0,16},{8,24},{16,32},{24,40},{32,48},{40,56},{48,0},{56,8},{4,52}... | collective-permute-start | bytes 442376 | tf_op jit(solution)/shard_map/ppermute | solution.py:211
  16.6 6.1 %collective-permute-start.7 = (bf16[320,128]{1,0:T(8,128)(2,1)S(1)}, bf16[320,128]{1,0:T(8,128)(2,1)S(1)}, u32[]{:S(2)}, u32[]{:S(2)}) collective-permute-start(bf16[320,128]{1,0:T(8,128)(2,1)S(1)} %pad_maximum_fusion.3), channel_id=1, source_target_pairs={{0,128},{64,192},{128,0},{192,64},{1,129},{65,193},{129,1},{193,65... | collective-permute-start | bytes 245768 | tf_op jit(solution)/shard_map/ppermute | solution.py:205
  19.7 4.4 %collective-permute-start.8 = (bf16[320,128]{1,0:T(8,128)(2,1)S(1)}, bf16[320,128]{1,0:T(8,128)(2,1)S(1)}, u32[]{:S(2)}, u32[]{:S(2)}) collective-permute-start(bf16[320,128]{1,0:T(8,128)(2,1)S(1)} %pad_maximum_fusion.3), channel_id=1, source_target_pairs={{0,64},{64,0},{128,192},{192,128},{1,65},{65,1},{129,193},{193,129... | collective-permute-start | bytes 245768 | tf_op jit(solution)/shard_map/ppermute | solution.py:205
  20.3 5.7 %collective-permute-start.9 = (bf16[320,128]{1,0:T(8,128)(2,1)S(1)}, bf16[320,128]{1,0:T(8,128)(2,1)S(1)}, u32[]{:S(2)}, u32[]{:S(2)}) collective-permute-start(bf16[320,128]{1,0:T(8,128)(2,1)S(1)} %pad_maximum_fusion.3), channel_id=1, source_target_pairs={{0,192},{64,128},{128,64},{192,0},{1,193},{65,129},{129,65},{193,1... | collective-permute-start | bytes 245768 | tf_op jit(solution)/shard_map/ppermute | solution.py:205
  26.1 0.7 %copy-start.1 = (s32[64]{0:T(128)S(1)}, s32[64]{0:T(128)}, u32[]{:S(2)}) copy-start(s32[64]{0:T(128)} %fill_ref.5) | copy-start | bytes 772
  26.2 2.1 %collective-permute-start.10 = (bf16[1136,256]{1,0:T(8,128)(2,1)S(1)}, bf16[1136,256]{1,0:T(8,128)(2,1)S(1)}, u32[]{:S(2)}, u32[]{:S(2)}) collective-permute-start(bf16[1136,256]{1,0:T(8,128)(2,1)S(1)} %maximum_maximum_fusion.near_ref), channel_id=1, source_target_pairs={{0,4},{4,0},{1,5},{5,1},{2,6},{6,2},{3,7},{7,3},{8,12},{12,8},{9,1... | collective-permute-start | bytes 1744904 | tf_op jit(solution)/shard_map/ppermute | solution.py:256
  28.3 6.6 %copy-start = (bf16[64,2048]{1,0:T(8,128)(2,1)S(1)}, bf16[64,2048]{1,0:T(8,128)(2,1)}, u32[]{:S(2)}) copy-start(bf16[64,2048]{1,0:T(8,128)(2,1)} %query_ref.1) | copy-start | bytes 786436
  30.0 12.7 %all-to-all-start = ((bf16[16,32,128]{2,1,0:T(8,128)(2,1)}), bf16[16,32,128]{2,1,0:T(8,128)(2,1)S(1)}, u32[]{:S(2)}, u32[]{:S(2)}) async-start(bf16[16,32,128]{2,1,0:T(8,128)(2,1)} %question_far.1), calls=%async_computation | async-start | bytes 262144 | tf_op jit(solution)/shard_map/all_to_all | solution.py:277

commit v5 on v4

--- a/solution.py
+++ b/solution.py
@@ -245,8 +245,8 @@
     step3 = moved(onward, 1)
     step4 = moved(onward, 2)
     came = [flipped(sent, f) for f in X_FLIPS[1:]]
-    step3, step4, *came = lax.optimization_barrier((step3, step4, *came))
     near = jnp.concatenate([step1, step2[None], step3, step4]).reshape(GATHERED, KVS * HEAD)
+    near, *came = lax.optimization_barrier((near, *came))
     others = jnp.stack([c[4 * BLOCK :] for c in came]).reshape(-1, HEADS, HEAD)
     anchor = sent
     for flip, c in zip(X_FLIPS[1:], came):

time: 43.8 us -> 43.7 us (level)
    ppermute x3, waiting for transfers between devices: 5.1 us -> 2.46 us  [flipped(): return lax.ppermute(array, 'x', [(i, i ^ flip) for i in range(NX)])]
    ppermute x4, waiting for transfers between devices: 1.42 us -> 3.98 us  [moved(): return lax.ppermute(array, ('z', 'core'), up + down)]
  transfers between devices with their start and end apart: 12 -> 12, of which waited for: 7 -> 7; matrix products, arithmetic and copies ran while one was open for 0% -> 1% of each run, Pallas kernels for 7% -> 7%
where the time goes in v5:
time: 43.7 us; the launch traced here: 43.5 us
  starting transfers between devices  22.7 us (52%)
  waiting for transfers between devices  12.7 us (29%)
  Pallas kernels  5.73 us (13%)
  other arithmetic  1.15 us (3%)
  between operations  0.81 us (2%)
    ppermute x4, starting transfers between devices, moved(): return lax.ppermute(array, ('z', 'core'), up + down)  12.1 us
    all_to_all x1, waiting for transfers between devices, per_device(): parts = lax.all_to_all(parts, ('x', 'tp'), 0, 0, tiled=True)  5.87 us
    all_to_all x1, starting transfers between devices, per_device(): parts = lax.all_to_all(parts, ('x', 'tp'), 0, 0, tiled=True)  4.81 us
    ppermute x3, starting transfers between devices, flipped(): return lax.ppermute(array, 'x', [(i, i ^ flip) for i in range(NX)])  4.25 us
    ppermute x4, waiting for transfers between devices, moved(): return lax.ppermute(array, ('z', 'core'), up + down)  3.98 us
    ppermute x3, waiting for transfers between devices, flipped(): return lax.ppermute(array, 'x', [(i, i ^ flip) for i in range(NX)])  2.46 us
    pallas_call x1, Pallas kernels, per_device(): pl.pallas_call(block_kernel, out_shape=jax.ShapeDtypeStruct(block_query.s...  1.96 us
    pallas_call x1, Pallas kernels, per_device(): question(far_kernel, out_shape=jax.ShapeDtypeStruct((NX * NT, 2 * HEADS,...  1.78 us
  transfers between devices with their start and end apart: 12, of which 7 were waited for; matrix products, arithmetic and copies ran while one was open for 1% of the time, Pallas kernels for 7%

profile of v5, /device:TPU:32, one launch (start us, length us, event | category | flops | bytes accessed | tf_op | source)
XLA Modules:
  0.0 43.5 jit_solution(17629718348479046732)
XLA Ops:
  0.6 0.0 copy-start.2
  0.6 0.8 %fusion.2 = (bf16[1,144,256]{2,1,0:T(8,128)(2,1)S(1)}, bf16[144,256]{1,0:T(8,128)(2,1)S(1)}) fusion(bf16[4,256]{1,0:T(4,128)(2,1)} %param.12, bf16[4,256]{1,0:T(4,128)(2,1)} %param.11, bf16[64,256]{1,0:T(8,128)(2,1)} %param.9, bf16[64,256]{1,0:T(8,128)(2,1)} %param.8), kind=kLoop, calls=%fused_computation.19 | loop fusion | flops 294912 | bytes 217088 | tf_op jit(solution)/shard_map/stack | solution.py:229
  1.5 0.1 collective-permute-start
  1.6 3.3 %collective-permute-start.2 = (bf16[144,256]{1,0:T(8,128)(2,1)S(1)}, bf16[144,256]{1,0:T(8,128)(2,1)S(1)}, u32[]{:S(2)}, u32[]{:S(2)}) collective-permute-start(bf16[144,256]{1,0:T(8,128)(2,1)S(1)} %get-tuple-element.29.unit_ref), channel_id=1, source_target_pairs={{0,16},{8,24},{16,32},{24,40},{32,48},{40,56},{48,0},{56,8},{4,52}... | collective-permute-start | bytes 221192 | tf_op jit(solution)/shard_map/ppermute | solution.py:211
  4.9 0.0 collective-permute-done.swapped_ref
  4.9 3.2 %collective-permute-start.1 = (bf16[2,144,256]{2,1,0:T(8,128)(2,1)S(1)}, bf16[2,144,256]{2,1,0:T(8,128)(2,1)S(1)}, u32[]{:S(2)}, u32[]{:S(2)}) collective-permute-start(bf16[2,144,256]{2,1,0:T(8,128)(2,1)S(1)} %pad_maximum_fusion.1), channel_id=1, source_target_pairs={{0,8},{8,16},{16,24},{24,32},{32,40},{40,48},{48,56},{56,0},{4,60}... | collective-permute-start | bytes 442376 | tf_op jit(solution)/shard_map/ppermute | solution.py:211
  8.2 0.7 %collective-permute-start.5 = (bf16[128,256]{1,0:T(8,128)(2,1)S(1)}, bf16[128,256]{1,0:T(8,128)(2,1)S(1)}, u32[]{:S(2)}, u32[]{:S(2)}) collective-permute-start(bf16[128,256]{1,0:T(8,128)(2,1)S(1)} %slice_select_fusion.2), channel_id=1, source_target_pairs={{0,24},{4,44},{1,25},{5,45},{2,26},{6,46},{3,27},{7,47}} | collective-permute-start | bytes 196616 | tf_op jit(solution)/shard_map/ppermute | solution.py:235
  8.8 0.7 %collective-permute-start.6 = (bf16[128,256]{1,0:T(8,128)(2,1)S(1)}, bf16[128,256]{1,0:T(8,128)(2,1)S(1)}, u32[]{:S(2)}, u32[]{:S(2)}) collective-permute-start(bf16[128,256]{1,0:T(8,128)(2,1)S(1)} %slice_select_fusion.2), channel_id=1, source_target_pairs={{4,36},{0,52},{5,37},{1,53},{6,38},{2,54},{7,39},{3,55}} | collective-permute-start | bytes 196616 | tf_op jit(solution)/shard_map/ppermute | solution.py:236
  9.5 0.0 copy-done.2
  9.5 0.7 %collective-permute-done.2 = bf16[144,256]{1,0:T(8,128)(2,1)S(1)} collective-permute-done((bf16[144,256]{1,0:T(8,128)(2,1)S(1)}, bf16[144,256]{1,0:T(8,128)(2,1)S(1)}, u32[]{:S(2)}, u32[]{:S(2)}) %collective-permute-start.2) | collective-permute-done | bytes 73760 | tf_op jit(solution)/shard_map/ppermute | solution.py:211
  10.3 0.7 %collective-permute-done.1 = bf16[2,144,256]{2,1,0:T(8,128)(2,1)S(1)} collective-permute-done((bf16[2,144,256]{2,1,0:T(8,128)(2,1)S(1)}, bf16[2,144,256]{2,1,0:T(8,128)(2,1)S(1)}, u32[]{:S(2)}, u32[]{:S(2)}) %collective-permute-start.1) | collective-permute-done | bytes 147488 | tf_op jit(solution)/shard_map/ppermute | solution.py:211
  11.0 2.4 %collective-permute-start.3 = (bf16[2,144,256]{2,1,0:T(8,128)(2,1)S(1)}, bf16[2,144,256]{2,1,0:T(8,128)(2,1)S(1)}, u32[]{:S(2)}, u32[]{:S(2)}) collective-permute-start(bf16[2,144,256]{2,1,0:T(8,128)(2,1)S(1)} %pad_maximum_fusion.2), channel_id=1, source_target_pairs={{0,8},{8,16},{16,24},{24,32},{32,40},{40,48},{48,56},{56,0},{4,60}... | collective-permute-start | bytes 442376 | tf_op jit(solution)/shard_map/ppermute | solution.py:211
  13.4 3.1 %collective-permute-start.4 = (bf16[2,144,256]{2,1,0:T(8,128)(2,1)S(1)}, bf16[2,144,256]{2,1,0:T(8,128)(2,1)S(1)}, u32[]{:S(2)}, u32[]{:S(2)}) collective-permute-start(bf16[2,144,256]{2,1,0:T(8,128)(2,1)S(1)} %pad_maximum_fusion.2), channel_id=1, source_target_pairs={{0,16},{8,24},{16,32},{24,40},{32,48},{40,56},{48,0},{56,8},{4,52}... | collective-permute-start | bytes 442376 | tf_op jit(solution)/shard_map/ppermute | solution.py:211
  16.6 0.0 collective-permute-done.5
  16.6 0.0 collective-permute-done.6
  16.6 3.1 %collective-permute-start.7 = (bf16[320,128]{1,0:T(8,128)(2,1)S(1)}, bf16[320,128]{1,0:T(8,128)(2,1)S(1)}, u32[]{:S(2)}, u32[]{:S(2)}) collective-permute-start(bf16[320,128]{1,0:T(8,128)(2,1)S(1)} %pad_maximum_fusion.3), channel_id=1, source_target_pairs={{0,128},{64,192},{128,0},{192,64},{1,129},{65,193},{129,1},{193,65... | collective-permute-start | bytes 245768 | tf_op jit(solution)/shard_map/ppermute | solution.py:205
  19.7 0.6 %collective-permute-start.8 = (bf16[320,128]{1,0:T(8,128)(2,1)S(1)}, bf16[320,128]{1,0:T(8,128)(2,1)S(1)}, u32[]{:S(2)}, u32[]{:S(2)}) collective-permute-start(bf16[320,128]{1,0:T(8,128)(2,1)S(1)} %pad_maximum_fusion.3), channel_id=1, source_target_pairs={{0,64},{64,0},{128,192},{192,128},{1,65},{65,1},{129,193},{193,129... | collective-permute-start | bytes 245768 | tf_op jit(solution)/shard_map/ppermute | solution.py:205
  20.3 0.6 %collective-permute-start.9 = (bf16[320,128]{1,0:T(8,128)(2,1)S(1)}, bf16[320,128]{1,0:T(8,128)(2,1)S(1)}, u32[]{:S(2)}, u32[]{:S(2)}) collective-permute-start(bf16[320,128]{1,0:T(8,128)(2,1)S(1)} %pad_maximum_fusion.3), channel_id=1, source_target_pairs={{0,192},{64,128},{128,64},{192,0},{1,193},{65,129},{129,65},{193,1... | collective-permute-start | bytes 245768 | tf_op jit(solution)/shard_map/ppermute | solution.py:205
  20.9 0.0 collective-permute-done.3
  20.9 2.6 %collective-permute-done.4 = bf16[2,144,256]{2,1,0:T(8,128)(2,1)S(1)} collective-permute-done((bf16[2,144,256]{2,1,0:T(8,128)(2,1)S(1)}, bf16[2,144,256]{2,1,0:T(8,128)(2,1)S(1)}, u32[]{:S(2)}, u32[]{:S(2)}) %collective-permute-start.4) | collective-permute-done | bytes 147488 | tf_op jit(solution)/shard_map/ppermute | solution.py:211
  23.4 0.1 pad_maximum_fusion
  23.5 0.0 collective-permute-done.7
  23.5 0.7 %collective-permute-done.8 = bf16[320,128]{1,0:T(8,128)(2,1)S(1)} collective-permute-done((bf16[320,128]{1,0:T(8,128)(2,1)S(1)}, bf16[320,128]{1,0:T(8,128)(2,1)S(1)}, u32[]{:S(2)}, u32[]{:S(2)}) %collective-permute-start.8) | collective-permute-done | bytes 81952 | tf_op jit(solution)/shard_map/ppermute | solution.py:205
  24.2 1.8 %collective-permute-done.9 = bf16[320,128]{1,0:T(8,128)(2,1)S(1)} collective-permute-done((bf16[320,128]{1,0:T(8,128)(2,1)S(1)}, bf16[320,128]{1,0:T(8,128)(2,1)S(1)}, u32[]{:S(2)}, u32[]{:S(2)}) %collective-permute-start.9) | collective-permute-done | bytes 81952 | tf_op jit(solution)/shard_map/ppermute | solution.py:205
  26.0 0.0 copy-start.1
  26.1 0.1 collective-permute-start.10
  26.2 0.1 pad_add_fusion.1.place_ref
  26.3 0.4 copy-done.1
  26.7 1.1 %question_near.1 = (f32[2,128,128]{2,1,0:T(8,128)S(1)}, f32[2,128,128]{2,1,0:T(8,128)S(1)}, f32[2,128,128]{2,1,0:T(8,128)S(1)}) custom-call(s32[3]{0:T(128)S(1)} %pad_add_fusion.1.place_ref, s32[64]{0:T(128)S(1)} %copy-done.1, bf16[4,16,128]{2,1,0:T(8,128)(2,1)S(1)} %bitcast.24, bf16[12,16,128]{2,1,0:T(8,128)(2,1)S(1)} %bitcast.22, ...), custom_call_target="tpu_custom_call" | custom-call | flops 100000000 | bytes 1000000 | tf_op jit(solution)/shard_map/question_near/pallas_call | solution.py:260
  27.8 0.3 collective-permute-done.10.far_ref
  28.2 0.0 copy-start
  28.2 1.8 %question_far.1 = bf16[16,32,128]{2,1,0:T(8,128)(2,1)} custom-call(s32[3]{0:T(128)S(1)} %pad_add_fusion.1.place_ref, s32[64]{0:T(128)S(1)} %copy-done.1, bf16[4,16,128]{2,1,0:T(8,128)(2,1)S(1)} %bitcast.25, bf16[12,16,128]{2,1,0:T(8,128)(2,1)S(1)} %bitcast.23, bf16[1136,256]{1,0:T(8,128)(2,1)S(1)} %collective-permute-done.10.far_ref, ...), custom_call_target="tpu_custom_call" | custom-call | flops 100000000 | bytes 1000000 | tf_op jit(solution)/shard_map/question_far/pallas_call | solution.py:268
  30.0 4.8 %all-to-all-start = ((bf16[16,32,128]{2,1,0:T(8,128)(2,1)}), bf16[16,32,128]{2,1,0:T(8,128)(2,1)S(1)}, u32[]{:S(2)}, u32[]{:S(2)}) async-start(bf16[16,32,128]{2,1,0:T(8,128)(2,1)} %question_far.1), calls=%async_computation | async-start | bytes 262144 | tf_op jit(solution)/shard_map/all_to_all | solution.py:277
  34.8 0.0 copy-done
  34.8 2.0 %block.1 = bf16[64,2048]{1,0:T(8,128)(2,1)} custom-call(s32[3]{0:T(128)S(1)} %pad_add_fusion.1.place_ref, s32[64]{0:T(128)S(1)} %copy-done.1, bf16[64,2048]{1,0:T(8,128)(2,1)S(1)} %copy-done, bf16[144,256]{1,0:T(8,128)(2,1)S(1)} %get-tuple-element.29.unit_ref, bf16[1136,256]{1,0:T(8,128)(2,1)S(1)} %maximum_maximum_fusion.near_ref, ...), custom_call_target="tpu_custom_call" | custom-call | tf_op jit(solution)/shard_map/block/pallas_call | solution.py:279
  36.7 5.9 %all-to-all-done.parts_ref = bf16[16,32,128]{2,1,0:T(8,128)(2,1)S(1)} async-done(((bf16[16,32,128]{2,1,0:T(8,128)(2,1)}), bf16[16,32,128]{2,1,0:T(8,128)(2,1)S(1)}, u32[]{:S(2)}, u32[]{:S(2)}) %all-to-all-start) | async-done | bytes 131104 | tf_op jit(solution)/shard_map/all_to_all | solution.py:277
  42.6 0.9 %merge.1 = bf16[1,8192]{1,0:T(2,128)(2,1)} custom-call(bf16[16,32,128]{2,1,0:T(8,128)(2,1)S(1)} %all-to-all-done.parts_ref), custom_call_target="tpu_custom_call" | custom-call | tf_op jit(solution)/shard_map/merge/pallas_call | solution.py:288
  (15 shorter events, 0.2 us)
Async XLA Ops:
  0.6 8.9 %copy-start.2 = (bf16[4,2048]{1,0:T(4,128)(2,1)S(1)}, bf16[4,2048]{1,0:T(4,128)(2,1)}, u32[]{:S(2)}) copy-start(bf16[4,2048]{1,0:T(4,128)(2,1)} %param.10) | copy-start | bytes 49156
  1.5 3.5 %collective-permute-start = (bf16[144,256]{1,0:T(8,128)(2,1)S(1)}, bf16[144,256]{1,0:T(8,128)(2,1)S(1)}, u32[]{:S(2)}, u32[]{:S(2)}) collective-permute-start(bf16[144,256]{1,0:T(8,128)(2,1)S(1)} %get-tuple-element.29.unit_ref), channel_id=1, source_target_pairs={{0,4},{4,0},{1,5},{5,1},{2,6},{6,2},{3,7},{7,3},{8,12},{12,8},{9,1... | collective-permute-start | bytes 221192 | tf_op jit(solution)/shard_map/ppermute | solution.py:228
  1.6 8.7 %collective-permute-start.2 = (bf16[144,256]{1,0:T(8,128)(2,1)S(1)}, bf16[144,256]{1,0:T(8,128)(2,1)S(1)}, u32[]{:S(2)}, u32[]{:S(2)}) collective-permute-start(bf16[144,256]{1,0:T(8,128)(2,1)S(1)} %get-tuple-element.29.unit_ref), channel_id=1, source_target_pairs={{0,16},{8,24},{16,32},{24,40},{32,48},{40,56},{48,0},{56,8},{4,52}... | collective-permute-start | bytes 221192 | tf_op jit(solution)/shard_map/ppermute | solution.py:211
  4.9 6.0 %collective-permute-start.1 = (bf16[2,144,256]{2,1,0:T(8,128)(2,1)S(1)}, bf16[2,144,256]{2,1,0:T(8,128)(2,1)S(1)}, u32[]{:S(2)}, u32[]{:S(2)}) collective-permute-start(bf16[2,144,256]{2,1,0:T(8,128)(2,1)S(1)} %pad_maximum_fusion.1), channel_id=1, source_target_pairs={{0,8},{8,16},{16,24},{24,32},{32,40},{40,48},{48,56},{56,0},{4,60}... | collective-permute-start | bytes 442376 | tf_op jit(solution)/shard_map/ppermute | solution.py:211
  8.2 8.4 %collective-permute-start.5 = (bf16[128,256]{1,0:T(8,128)(2,1)S(1)}, bf16[128,256]{1,0:T(8,128)(2,1)S(1)}, u32[]{:S(2)}, u32[]{:S(2)}) collective-permute-start(bf16[128,256]{1,0:T(8,128)(2,1)S(1)} %slice_select_fusion.2), channel_id=1, source_target_pairs={{0,24},{4,44},{1,25},{5,45},{2,26},{6,46},{3,27},{7,47}} | collective-permute-start | bytes 196616 | tf_op jit(solution)/shard_map/ppermute | solution.py:235
  8.8 7.7 %collective-permute-start.6 = (bf16[128,256]{1,0:T(8,128)(2,1)S(1)}, bf16[128,256]{1,0:T(8,128)(2,1)S(1)}, u32[]{:S(2)}, u32[]{:S(2)}) collective-permute-start(bf16[128,256]{1,0:T(8,128)(2,1)S(1)} %slice_select_fusion.2), channel_id=1, source_target_pairs={{4,36},{0,52},{5,37},{1,53},{6,38},{2,54},{7,39},{3,55}} | collective-permute-start | bytes 196616 | tf_op jit(solution)/shard_map/ppermute | solution.py:236
  11.0 9.9 %collective-permute-start.3 = (bf16[2,144,256]{2,1,0:T(8,128)(2,1)S(1)}, bf16[2,144,256]{2,1,0:T(8,128)(2,1)S(1)}, u32[]{:S(2)}, u32[]{:S(2)}) collective-permute-start(bf16[2,144,256]{2,1,0:T(8,128)(2,1)S(1)} %pad_maximum_fusion.2), channel_id=1, source_target_pairs={{0,8},{8,16},{16,24},{24,32},{32,40},{40,48},{48,56},{56,0},{4,60}... | collective-permute-start | bytes 442376 | tf_op jit(solution)/shard_map/ppermute | solution.py:211
  13.4 10.0 %collective-permute-start.4 = (bf16[2,144,256]{2,1,0:T(8,128)(2,1)S(1)}, bf16[2,144,256]{2,1,0:T(8,128)(2,1)S(1)}, u32[]{:S(2)}, u32[]{:S(2)}) collective-permute-start(bf16[2,144,256]{2,1,0:T(8,128)(2,1)S(1)} %pad_maximum_fusion.2), channel_id=1, source_target_pairs={{0,16},{8,24},{16,32},{24,40},{32,48},{40,56},{48,0},{56,8},{4,52}... | collective-permute-start | bytes 442376 | tf_op jit(solution)/shard_map/ppermute | solution.py:211
  16.6 6.9 %collective-permute-start.7 = (bf16[320,128]{1,0:T(8,128)(2,1)S(1)}, bf16[320,128]{1,0:T(8,128)(2,1)S(1)}, u32[]{:S(2)}, u32[]{:S(2)}) collective-permute-start(bf16[320,128]{1,0:T(8,128)(2,1)S(1)} %pad_maximum_fusion.3), channel_id=1, source_target_pairs={{0,128},{64,192},{128,0},{192,64},{1,129},{65,193},{129,1},{193,65... | collective-permute-start | bytes 245768 | tf_op jit(solution)/shard_map/ppermute | solution.py:205
  19.7 4.4 %collective-permute-start.8 = (bf16[320,128]{1,0:T(8,128)(2,1)S(1)}, bf16[320,128]{1,0:T(8,128)(2,1)S(1)}, u32[]{:S(2)}, u32[]{:S(2)}) collective-permute-start(bf16[320,128]{1,0:T(8,128)(2,1)S(1)} %pad_maximum_fusion.3), channel_id=1, source_target_pairs={{0,64},{64,0},{128,192},{192,128},{1,65},{65,1},{129,193},{193,129... | collective-permute-start | bytes 245768 | tf_op jit(solution)/shard_map/ppermute | solution.py:205
  20.3 5.7 %collective-permute-start.9 = (bf16[320,128]{1,0:T(8,128)(2,1)S(1)}, bf16[320,128]{1,0:T(8,128)(2,1)S(1)}, u32[]{:S(2)}, u32[]{:S(2)}) collective-permute-start(bf16[320,128]{1,0:T(8,128)(2,1)S(1)} %pad_maximum_fusion.3), channel_id=1, source_target_pairs={{0,192},{64,128},{128,64},{192,0},{1,193},{65,129},{129,65},{193,1... | collective-permute-start | bytes 245768 | tf_op jit(solution)/shard_map/ppermute | solution.py:205
  26.0 0.7 %copy-start.1 = (s32[64]{0:T(128)S(1)}, s32[64]{0:T(128)}, u32[]{:S(2)}) copy-start(s32[64]{0:T(128)} %fill_ref.5) | copy-start | bytes 772
  26.1 2.1 %collective-permute-start.10 = (bf16[1136,256]{1,0:T(8,128)(2,1)S(1)}, bf16[1136,256]{1,0:T(8,128)(2,1)S(1)}, u32[]{:S(2)}, u32[]{:S(2)}) collective-permute-start(bf16[1136,256]{1,0:T(8,128)(2,1)S(1)} %maximum_maximum_fusion.near_ref), channel_id=1, source_target_pairs={{0,4},{4,0},{1,5},{5,1},{2,6},{6,2},{3,7},{7,3},{8,12},{12,8},{9,1... | collective-permute-start | bytes 1744904 | tf_op jit(solution)/shard_map/ppermute | solution.py:256
  28.2 6.6 %copy-start = (bf16[64,2048]{1,0:T(8,128)(2,1)S(1)}, bf16[64,2048]{1,0:T(8,128)(2,1)}, u32[]{:S(2)}) copy-start(bf16[64,2048]{1,0:T(8,128)(2,1)} %query_ref.1) | copy-start | bytes 786436
  30.0 12.7 %all-to-all-start = ((bf16[16,32,128]{2,1,0:T(8,128)(2,1)}), bf16[16,32,128]{2,1,0:T(8,128)(2,1)S(1)}, u32[]{:S(2)}, u32[]{:S(2)}) async-start(bf16[16,32,128]{2,1,0:T(8,128)(2,1)} %question_far.1), calls=%async_computation | async-start | bytes 262144 | tf_op jit(solution)/shard_map/all_to_all | solution.py:277

commit v6 on v4

--- a/solution.py
+++ b/solution.py
@@ -232,14 +232,14 @@
     step1 = moved(pair, 1)
     step2 = moved(unit, 2)
     first = jnp.where(core == 0, unit, swapped)[: 2 * BLOCK]
-    third = lax.ppermute(first, ("x", "z", "core"), [(0, 3 * NC), (1, 5 * NC + 1)])
-    fourth = lax.ppermute(first, ("x", "z", "core"), [(1, 4 * NC + 1), (0, 6 * NC + 1)])
+    third = lax.ppermute(first, ("x", "z", "core"), [(1, 4 * NC + 1), (0, 6 * NC + 1)])
+    fourth = lax.ppermute(first, ("x", "z", "core"), [(0, 3 * NC), (1, 5 * NC + 1)])
 
     step1, step2 = lax.optimization_barrier((step1, step2))
     carried = jnp.where((z == 1) | (z == NZ - 1), jnp.where(core == 0, step1[0], step1[1]), unit)
     carried = jnp.where(z == 2, step2, carried)
     carried = carried[: 2 * BLOCK]
-    carried = jnp.where((z == 3) | (z == 5), third, jnp.where((z == 4) | (z == 6), fourth, carried))
+    carried = jnp.where((z == 4) | (z == 6), third, jnp.where((z == 3) | (z == 5), fourth, carried))
     sent = jnp.concatenate([carried[:, :HEAD], carried[:, HEAD:], asked.reshape(-1, HEAD)], 0)
     onward = jnp.stack([step1[1], step2])
     step3 = moved(onward, 1)

time: 43.8 us -> 43.8 us (level)
  no operation moved by 1% of the time
where the time goes in v6:
time: 43.8 us; the launch traced here: 43.6 us
  starting transfers between devices  22.7 us (52%)
  waiting for transfers between devices  12.7 us (29%)
  Pallas kernels  5.73 us (13%)
  other arithmetic  1.16 us (3%)
  between operations  0.81 us (2%)
    ppermute x4, starting transfers between devices, moved(): return lax.ppermute(array, ('z', 'core'), up + down)  12.1 us
    all_to_all x1, waiting for transfers between devices, per_device(): parts = lax.all_to_all(parts, ('x', 'tp'), 0, 0, tiled=True)  5.87 us
    ppermute x3, waiting for transfers between devices, flipped(): return lax.ppermute(array, 'x', [(i, i ^ flip) for i in range(NX)])  5.1 us
    all_to_all x1, starting transfers between devices, per_device(): parts = lax.all_to_all(parts, ('x', 'tp'), 0, 0, tiled=True)  4.81 us
    ppermute x3, starting transfers between devices, flipped(): return lax.ppermute(array, 'x', [(i, i ^ flip) for i in range(NX)])  4.25 us
    pallas_call x1, Pallas kernels, per_device(): pl.pallas_call(block_kernel, out_shape=jax.ShapeDtypeStruct(block_query.s...  1.96 us
    pallas_call x1, Pallas kernels, per_device(): question(far_kernel, out_shape=jax.ShapeDtypeStruct((NX * NT, 2 * HEADS,...  1.78 us
    ppermute x4, waiting for transfers between devices, moved(): return lax.ppermute(array, ('z', 'core'), up + down)  1.42 us
  transfers between devices with their start and end apart: 12, of which 7 were waited for; matrix products, arithmetic and copies ran while one was open for 0% of the time, Pallas kernels for 7%

profile of v6, /device:TPU:32, one launch (start us, length us, event | category | flops | bytes accessed | tf_op | source)
XLA Modules:
  0.0 43.6 jit_solution(8206840300990870664)
XLA Ops:
  0.6 0.0 copy-start.2
  0.6 0.8 %fusion.2 = (bf16[1,144,256]{2,1,0:T(8,128)(2,1)S(1)}, bf16[144,256]{1,0:T(8,128)(2,1)S(1)}) fusion(bf16[4,256]{1,0:T(4,128)(2,1)} %param.12, bf16[4,256]{1,0:T(4,128)(2,1)} %param.11, bf16[64,256]{1,0:T(8,128)(2,1)} %param.9, bf16[64,256]{1,0:T(8,128)(2,1)} %param.8), kind=kLoop, calls=%fused_computation.19 | loop fusion | flops 294912 | bytes 217088 | tf_op jit(solution)/shard_map/stack | solution.py:229
  1.5 0.1 collective-permute-start
  1.6 3.3 %collective-permute-start.2 = (bf16[144,256]{1,0:T(8,128)(2,1)S(1)}, bf16[144,256]{1,0:T(8,128)(2,1)S(1)}, u32[]{:S(2)}, u32[]{:S(2)}) collective-permute-start(bf16[144,256]{1,0:T(8,128)(2,1)S(1)} %get-tuple-element.31.unit_ref), channel_id=1, source_target_pairs={{0,16},{8,24},{16,32},{24,40},{32,48},{40,56},{48,0},{56,8},{4,52}... | collective-permute-start | bytes 221192 | tf_op jit(solution)/shard_map/ppermute | solution.py:211
  4.9 0.0 collective-permute-done.swapped_ref
  4.9 3.2 %collective-permute-start.1 = (bf16[2,144,256]{2,1,0:T(8,128)(2,1)S(1)}, bf16[2,144,256]{2,1,0:T(8,128)(2,1)S(1)}, u32[]{:S(2)}, u32[]{:S(2)}) collective-permute-start(bf16[2,144,256]{2,1,0:T(8,128)(2,1)S(1)} %pad_maximum_fusion.1), channel_id=1, source_target_pairs={{0,8},{8,16},{16,24},{24,32},{32,40},{40,48},{48,56},{56,0},{4,60}... | collective-permute-start | bytes 442376 | tf_op jit(solution)/shard_map/ppermute | solution.py:211
  8.2 0.7 %collective-permute-start.5 = (bf16[128,256]{1,0:T(8,128)(2,1)S(1)}, bf16[128,256]{1,0:T(8,128)(2,1)S(1)}, u32[]{:S(2)}, u32[]{:S(2)}) collective-permute-start(bf16[128,256]{1,0:T(8,128)(2,1)S(1)} %slice_select_fusion.2), channel_id=1, source_target_pairs={{4,36},{0,52},{5,37},{1,53},{6,38},{2,54},{7,39},{3,55}} | collective-permute-start | bytes 196616 | tf_op jit(solution)/shard_map/ppermute | solution.py:235
  8.8 0.7 %collective-permute-start.6 = (bf16[128,256]{1,0:T(8,128)(2,1)S(1)}, bf16[128,256]{1,0:T(8,128)(2,1)S(1)}, u32[]{:S(2)}, u32[]{:S(2)}) collective-permute-start(bf16[128,256]{1,0:T(8,128)(2,1)S(1)} %slice_select_fusion.2), channel_id=1, source_target_pairs={{0,24},{4,44},{1,25},{5,45},{2,26},{6,46},{3,27},{7,47}} | collective-permute-start | bytes 196616 | tf_op jit(solution)/shard_map/ppermute | solution.py:236
  9.5 0.0 copy-done.2
  9.5 0.7 %collective-permute-done.2 = bf16[144,256]{1,0:T(8,128)(2,1)S(1)} collective-permute-done((bf16[144,256]{1,0:T(8,128)(2,1)S(1)}, bf16[144,256]{1,0:T(8,128)(2,1)S(1)}, u32[]{:S(2)}, u32[]{:S(2)}) %collective-permute-start.2) | collective-permute-done | bytes 73760 | tf_op jit(solution)/shard_map/ppermute | solution.py:211
  10.3 0.7 %collective-permute-done.1 = bf16[2,144,256]{2,1,0:T(8,128)(2,1)S(1)} collective-permute-done((bf16[2,144,256]{2,1,0:T(8,128)(2,1)S(1)}, bf16[2,144,256]{2,1,0:T(8,128)(2,1)S(1)}, u32[]{:S(2)}, u32[]{:S(2)}) %collective-permute-start.1) | collective-permute-done | bytes 147488 | tf_op jit(solution)/shard_map/ppermute | solution.py:211
  11.0 2.4 %collective-permute-start.3 = (bf16[2,144,256]{2,1,0:T(8,128)(2,1)S(1)}, bf16[2,144,256]{2,1,0:T(8,128)(2,1)S(1)}, u32[]{:S(2)}, u32[]{:S(2)}) collective-permute-start(bf16[2,144,256]{2,1,0:T(8,128)(2,1)S(1)} %pad_maximum_fusion.2), channel_id=1, source_target_pairs={{0,8},{8,16},{16,24},{24,32},{32,40},{40,48},{48,56},{56,0},{4,60}... | collective-permute-start | bytes 442376 | tf_op jit(solution)/shard_map/ppermute | solution.py:211
  13.4 3.1 %collective-permute-start.4 = (bf16[2,144,256]{2,1,0:T(8,128)(2,1)S(1)}, bf16[2,144,256]{2,1,0:T(8,128)(2,1)S(1)}, u32[]{:S(2)}, u32[]{:S(2)}) collective-permute-start(bf16[2,144,256]{2,1,0:T(8,128)(2,1)S(1)} %pad_maximum_fusion.2), channel_id=1, source_target_pairs={{0,16},{8,24},{16,32},{24,40},{32,48},{40,56},{48,0},{56,8},{4,52}... | collective-permute-start | bytes 442376 | tf_op jit(solution)/shard_map/ppermute | solution.py:211
  16.6 0.0 collective-permute-done.5
  16.6 0.0 collective-permute-done.6
  16.6 3.1 %collective-permute-start.7 = (bf16[320,128]{1,0:T(8,128)(2,1)S(1)}, bf16[320,128]{1,0:T(8,128)(2,1)S(1)}, u32[]{:S(2)}, u32[]{:S(2)}) collective-permute-start(bf16[320,128]{1,0:T(8,128)(2,1)S(1)} %pad_maximum_fusion.3), channel_id=1, source_target_pairs={{0,128},{64,192},{128,0},{192,64},{1,129},{65,193},{129,1},{193,65... | collective-permute-start | bytes 245768 | tf_op jit(solution)/shard_map/ppermute | solution.py:205
  19.7 0.6 %collective-permute-start.8 = (bf16[320,128]{1,0:T(8,128)(2,1)S(1)}, bf16[320,128]{1,0:T(8,128)(2,1)S(1)}, u32[]{:S(2)}, u32[]{:S(2)}) collective-permute-start(bf16[320,128]{1,0:T(8,128)(2,1)S(1)} %pad_maximum_fusion.3), channel_id=1, source_target_pairs={{0,64},{64,0},{128,192},{192,128},{1,65},{65,1},{129,193},{193,129... | collective-permute-start | bytes 245768 | tf_op jit(solution)/shard_map/ppermute | solution.py:205
  20.3 0.6 %collective-permute-start.9 = (bf16[320,128]{1,0:T(8,128)(2,1)S(1)}, bf16[320,128]{1,0:T(8,128)(2,1)S(1)}, u32[]{:S(2)}, u32[]{:S(2)}) collective-permute-start(bf16[320,128]{1,0:T(8,128)(2,1)S(1)} %pad_maximum_fusion.3), channel_id=1, source_target_pairs={{0,192},{64,128},{128,64},{192,0},{1,193},{65,129},{129,65},{193,1... | collective-permute-start | bytes 245768 | tf_op jit(solution)/shard_map/ppermute | solution.py:205
  20.9 1.9 %collective-permute-done.7 = bf16[320,128]{1,0:T(8,128)(2,1)S(1)} collective-permute-done((bf16[320,128]{1,0:T(8,128)(2,1)S(1)}, bf16[320,128]{1,0:T(8,128)(2,1)S(1)}, u32[]{:S(2)}, u32[]{:S(2)}) %collective-permute-start.7) | collective-permute-done | bytes 81952 | tf_op jit(solution)/shard_map/ppermute | solution.py:205
  22.8 1.4 %collective-permute-done.8 = bf16[320,128]{1,0:T(8,128)(2,1)S(1)} collective-permute-done((bf16[320,128]{1,0:T(8,128)(2,1)S(1)}, bf16[320,128]{1,0:T(8,128)(2,1)S(1)}, u32[]{:S(2)}, u32[]{:S(2)}) %collective-permute-start.8) | collective-permute-done | bytes 81952 | tf_op jit(solution)/shard_map/ppermute | solution.py:205
  24.2 1.8 %collective-permute-done.9 = bf16[320,128]{1,0:T(8,128)(2,1)S(1)} collective-permute-done((bf16[320,128]{1,0:T(8,128)(2,1)S(1)}, bf16[320,128]{1,0:T(8,128)(2,1)S(1)}, u32[]{:S(2)}, u32[]{:S(2)}) %collective-permute-start.9) | collective-permute-done | bytes 81952 | tf_op jit(solution)/shard_map/ppermute | solution.py:205
  26.0 0.0 collective-permute-done.3
  26.0 0.0 collective-permute-done.4
  26.0 0.1 pad_maximum_fusion
  26.1 0.0 copy-start.1
  26.2 0.1 collective-permute-start.10
  26.3 0.1 pad_add_fusion.1.place_ref
  26.4 0.4 copy-done.1
  26.8 1.1 %question_near.1 = (f32[2,128,128]{2,1,0:T(8,128)S(1)}, f32[2,128,128]{2,1,0:T(8,128)S(1)}, f32[2,128,128]{2,1,0:T(8,128)S(1)}) custom-call(s32[3]{0:T(128)S(1)} %pad_add_fusion.1.place_ref, s32[64]{0:T(128)S(1)} %copy-done.1, bf16[4,16,128]{2,1,0:T(8,128)(2,1)S(1)} %bitcast.24, bf16[12,16,128]{2,1,0:T(8,128)(2,1)S(1)} %bitcast.22, ...), custom_call_target="tpu_custom_call" | custom-call | flops 100000000 | bytes 1000000 | tf_op jit(solution)/shard_map/question_near/pallas_call | solution.py:260
  27.9 0.3 collective-permute-done.10.far_ref
  28.3 0.0 copy-start
  28.3 1.8 %question_far.1 = bf16[16,32,128]{2,1,0:T(8,128)(2,1)} custom-call(s32[3]{0:T(128)S(1)} %pad_add_fusion.1.place_ref, s32[64]{0:T(128)S(1)} %copy-done.1, bf16[4,16,128]{2,1,0:T(8,128)(2,1)S(1)} %bitcast.25, bf16[12,16,128]{2,1,0:T(8,128)(2,1)S(1)} %bitcast.23, bf16[1136,256]{1,0:T(8,128)(2,1)S(1)} %collective-permute-done.10.far_ref, ...), custom_call_target="tpu_custom_call" | custom-call | flops 100000000 | bytes 1000000 | tf_op jit(solution)/shard_map/question_far/pallas_call | solution.py:268
  30.0 4.8 %all-to-all-start = ((bf16[16,32,128]{2,1,0:T(8,128)(2,1)}), bf16[16,32,128]{2,1,0:T(8,128)(2,1)S(1)}, u32[]{:S(2)}, u32[]{:S(2)}) async-start(bf16[16,32,128]{2,1,0:T(8,128)(2,1)} %question_far.1), calls=%async_computation | async-start | bytes 262144 | tf_op jit(solution)/shard_map/all_to_all | solution.py:277
  34.9 0.0 copy-done
  34.9 2.0 %block.1 = bf16[64,2048]{1,0:T(8,128)(2,1)} custom-call(s32[3]{0:T(128)S(1)} %pad_add_fusion.1.place_ref, s32[64]{0:T(128)S(1)} %copy-done.1, bf16[64,2048]{1,0:T(8,128)(2,1)S(1)} %copy-done, bf16[144,256]{1,0:T(8,128)(2,1)S(1)} %get-tuple-element.31.unit_ref, bf16[1136,256]{1,0:T(8,128)(2,1)S(1)} %maximum_maximum_fusion.near_ref, ...), custom_call_target="tpu_custom_call" | custom-call | tf_op jit(solution)/shard_map/block/pallas_call | solution.py:279
  36.8 5.9 %all-to-all-done.parts_ref = bf16[16,32,128]{2,1,0:T(8,128)(2,1)S(1)} async-done(((bf16[16,32,128]{2,1,0:T(8,128)(2,1)}), bf16[16,32,128]{2,1,0:T(8,128)(2,1)S(1)}, u32[]{:S(2)}, u32[]{:S(2)}) %all-to-all-start) | async-done | bytes 131104 | tf_op jit(solution)/shard_map/all_to_all | solution.py:277
  42.7 0.9 %merge.1 = bf16[1,8192]{1,0:T(2,128)(2,1)} custom-call(bf16[16,32,128]{2,1,0:T(8,128)(2,1)S(1)} %all-to-all-done.parts_ref), custom_call_target="tpu_custom_call" | custom-call | tf_op jit(solution)/shard_map/merge/pallas_call | solution.py:288
  (15 shorter events, 0.2 us)
Async XLA Ops:
  0.6 8.9 %copy-start.2 = (bf16[4,2048]{1,0:T(4,128)(2,1)S(1)}, bf16[4,2048]{1,0:T(4,128)(2,1)}, u32[]{:S(2)}) copy-start(bf16[4,2048]{1,0:T(4,128)(2,1)} %param.10) | copy-start | bytes 49156
  1.5 3.5 %collective-permute-start = (bf16[144,256]{1,0:T(8,128)(2,1)S(1)}, bf16[144,256]{1,0:T(8,128)(2,1)S(1)}, u32[]{:S(2)}, u32[]{:S(2)}) collective-permute-start(bf16[144,256]{1,0:T(8,128)(2,1)S(1)} %get-tuple-element.31.unit_ref), channel_id=1, source_target_pairs={{0,4},{4,0},{1,5},{5,1},{2,6},{6,2},{3,7},{7,3},{8,12},{12,8},{9,1... | collective-permute-start | bytes 221192 | tf_op jit(solution)/shard_map/ppermute | solution.py:228
  1.6 8.7 %collective-permute-start.2 = (bf16[144,256]{1,0:T(8,128)(2,1)S(1)}, bf16[144,256]{1,0:T(8,128)(2,1)S(1)}, u32[]{:S(2)}, u32[]{:S(2)}) collective-permute-start(bf16[144,256]{1,0:T(8,128)(2,1)S(1)} %get-tuple-element.31.unit_ref), channel_id=1, source_target_pairs={{0,16},{8,24},{16,32},{24,40},{32,48},{40,56},{48,0},{56,8},{4,52}... | collective-permute-start | bytes 221192 | tf_op jit(solution)/shard_map/ppermute | solution.py:211
  4.9 6.0 %collective-permute-start.1 = (bf16[2,144,256]{2,1,0:T(8,128)(2,1)S(1)}, bf16[2,144,256]{2,1,0:T(8,128)(2,1)S(1)}, u32[]{:S(2)}, u32[]{:S(2)}) collective-permute-start(bf16[2,144,256]{2,1,0:T(8,128)(2,1)S(1)} %pad_maximum_fusion.1), channel_id=1, source_target_pairs={{0,8},{8,16},{16,24},{24,32},{32,40},{40,48},{48,56},{56,0},{4,60}... | collective-permute-start | bytes 442376 | tf_op jit(solution)/shard_map/ppermute | solution.py:211
  8.2 8.4 %collective-permute-start.5 = (bf16[128,256]{1,0:T(8,128)(2,1)S(1)}, bf16[128,256]{1,0:T(8,128)(2,1)S(1)}, u32[]{:S(2)}, u32[]{:S(2)}) collective-permute-start(bf16[128,256]{1,0:T(8,128)(2,1)S(1)} %slice_select_fusion.2), channel_id=1, source_target_pairs={{4,36},{0,52},{5,37},{1,53},{6,38},{2,54},{7,39},{3,55}} | collective-permute-start | bytes 196616 | tf_op jit(solution)/shard_map/ppermute | solution.py:235
  8.8 7.7 %collective-permute-start.6 = (bf16[128,256]{1,0:T(8,128)(2,1)S(1)}, bf16[128,256]{1,0:T(8,128)(2,1)S(1)}, u32[]{:S(2)}, u32[]{:S(2)}) collective-permute-start(bf16[128,256]{1,0:T(8,128)(2,1)S(1)} %slice_select_fusion.2), channel_id=1, source_target_pairs={{0,24},{4,44},{1,25},{5,45},{2,26},{6,46},{3,27},{7,47}} | collective-permute-start | bytes 196616 | tf_op jit(solution)/shard_map/ppermute | solution.py:236
  11.0 15.0 %collective-permute-start.3 = (bf16[2,144,256]{2,1,0:T(8,128)(2,1)S(1)}, bf16[2,144,256]{2,1,0:T(8,128)(2,1)S(1)}, u32[]{:S(2)}, u32[]{:S(2)}) collective-permute-start(bf16[2,144,256]{2,1,0:T(8,128)(2,1)S(1)} %pad_maximum_fusion.2), channel_id=1, source_target_pairs={{0,8},{8,16},{16,24},{24,32},{32,40},{40,48},{48,56},{56,0},{4,60}... | collective-permute-start | bytes 442376 | tf_op jit(solution)/shard_map/ppermute | solution.py:211
  13.4 12.6 %collective-permute-start.4 = (bf16[2,144,256]{2,1,0:T(8,128)(2,1)S(1)}, bf16[2,144,256]{2,1,0:T(8,128)(2,1)S(1)}, u32[]{:S(2)}, u32[]{:S(2)}) collective-permute-start(bf16[2,144,256]{2,1,0:T(8,128)(2,1)S(1)} %pad_maximum_fusion.2), channel_id=1, source_target_pairs={{0,16},{8,24},{16,32},{24,40},{32,48},{40,56},{48,0},{56,8},{4,52}... | collective-permute-start | bytes 442376 | tf_op jit(solution)/shard_map/ppermute | solution.py:211
  16.6 6.1 %collective-permute-start.7 = (bf16[320,128]{1,0:T(8,128)(2,1)S(1)}, bf16[320,128]{1,0:T(8,128)(2,1)S(1)}, u32[]{:S(2)}, u32[]{:S(2)}) collective-permute-start(bf16[320,128]{1,0:T(8,128)(2,1)S(1)} %pad_maximum_fusion.3), channel_id=1, source_target_pairs={{0,128},{64,192},{128,0},{192,64},{1,129},{65,193},{129,1},{193,65... | collective-permute-start | bytes 245768 | tf_op jit(solution)/shard_map/ppermute | solution.py:205
  19.7 4.4 %collective-permute-start.8 = (bf16[320,128]{1,0:T(8,128)(2,1)S(1)}, bf16[320,128]{1,0:T(8,128)(2,1)S(1)}, u32[]{:S(2)}, u32[]{:S(2)}) collective-permute-start(bf16[320,128]{1,0:T(8,128)(2,1)S(1)} %pad_maximum_fusion.3), channel_id=1, source_target_pairs={{0,64},{64,0},{128,192},{192,128},{1,65},{65,1},{129,193},{193,129... | collective-permute-start | bytes 245768 | tf_op jit(solution)/shard_map/ppermute | solution.py:205
  20.3 5.7 %collective-permute-start.9 = (bf16[320,128]{1,0:T(8,128)(2,1)S(1)}, bf16[320,128]{1,0:T(8,128)(2,1)S(1)}, u32[]{:S(2)}, u32[]{:S(2)}) collective-permute-start(bf16[320,128]{1,0:T(8,128)(2,1)S(1)} %pad_maximum_fusion.3), channel_id=1, source_target_pairs={{0,192},{64,128},{128,64},{192,0},{1,193},{65,129},{129,65},{193,1... | collective-permute-start | bytes 245768 | tf_op jit(solution)/shard_map/ppermute | solution.py:205
  26.1 0.7 %copy-start.1 = (s32[64]{0:T(128)S(1)}, s32[64]{0:T(128)}, u32[]{:S(2)}) copy-start(s32[64]{0:T(128)} %fill_ref.5) | copy-start | bytes 772
  26.2 2.1 %collective-permute-start.10 = (bf16[1136,256]{1,0:T(8,128)(2,1)S(1)}, bf16[1136,256]{1,0:T(8,128)(2,1)S(1)}, u32[]{:S(2)}, u32[]{:S(2)}) collective-permute-start(bf16[1136,256]{1,0:T(8,128)(2,1)S(1)} %maximum_maximum_fusion.near_ref), channel_id=1, source_target_pairs={{0,4},{4,0},{1,5},{5,1},{2,6},{6,2},{3,7},{7,3},{8,12},{12,8},{9,1... | collective-permute-start | bytes 1744904 | tf_op jit(solution)/shard_map/ppermute | solution.py:256
  28.3 6.6 %copy-start = (bf16[64,2048]{1,0:T(8,128)(2,1)S(1)}, bf16[64,2048]{1,0:T(8,128)(2,1)}, u32[]{:S(2)}) copy-start(bf16[64,2048]{1,0:T(8,128)(2,1)} %query_ref.1) | copy-start | bytes 786436
  30.0 12.7 %all-to-all-start = ((bf16[16,32,128]{2,1,0:T(8,128)(2,1)}), bf16[16,32,128]{2,1,0:T(8,128)(2,1)S(1)}, u32[]{:S(2)}, u32[]{:S(2)}) async-start(bf16[16,32,128]{2,1,0:T(8,128)(2,1)} %question_far.1), calls=%async_computation | async-start | bytes 262144 | tf_op jit(solution)/shard_map/all_to_all | solution.py:277
